TPU v7x, 256 devices: a whole 4x4x8 slice. The times are simulated.
256 devices in a mesh: dp: 16 (over x_hi, z), tensor: 16 (over y, x_lo, core).
Axes of the slice: x: 4 (x_hi: 2, x_lo: 2; x = x_hi * 2 + x_lo), y: 4, z: 8, core: 2. Of those that a mesh axis runs over, the one named last changes fastest.
Arguments:
- hidden: bfloat16 [32768, 14336], P(('dp', 'tensor')), parts along dimension 0, may hold values from -6 to 6
- down_weight: bfloat16 [14336, 4096], P('tensor'), may hold values from -0.046875 to 0.046875
- residual: bfloat16 [32768, 4096], P(('dp', 'tensor')), parts along dimension 0, may hold values from -6 to 6
- row_order: int32 [32768], P('dp'), parts along dimension 0, may hold values from 0 to 2047, each once
- value_head: bfloat16 [4096], replicated, may hold values from -0.09375 to 0.09375
Outputs:
- layer_out: bfloat16 [32768, 4096], P(('dp', 'tensor')), parts along dimension 0
- scores: float32 [32768], P(('dp', 'tensor')), parts along dimension 0
There are 16 independent parts, one for each index of `dp`. A program takes and returns all parts, laid end to end along the dimension named above; an argument that names none is the same for every part. Nothing has to cross between parts.
Inputs may be any that keep to these rules, and one draw needn't show every extreme that they name: `row_order`: each of the 2048 rollout rows appears exactly once.
All inputs are finite; a program needn't handle non-finite values.
Results may differ from a plain program's by a relative error of at most 0.02.
Values may be sent and summed in bfloat16 or wider, within the bound.
No kernel may reach another device: no remote copies, remote signals or barrier semaphores. Data moves between devices by JAX's collectives and lax.ppermute only.
A program may use at most 128 MiB of HBM per device.

v0:
```python
import jax
import jax.numpy as jnp
from jax import lax
from jax.sharding import PartitionSpec as P


def local(hidden, down_weight, residual, row_order, value_head):
    columns = lax.all_to_all(hidden, "tensor", split_axis=1, concat_axis=0, tiled=True)
    picked = jnp.take(columns, row_order, axis=0)
    full_term = jnp.dot(picked, down_weight, preferred_element_type=jnp.float32)
    down = lax.psum_scatter(
        full_term.astype(jnp.bfloat16), "tensor", scatter_dimension=0, tiled=True
    ).astype(jnp.float32)
    layer_out = (residual.astype(jnp.float32) + down).astype(jnp.bfloat16)
    widened = layer_out.astype(jnp.float32)
    mean_square = jnp.mean(widened * widened, axis=-1, keepdims=True)
    normed = widened * lax.rsqrt(mean_square + 1e-05)
    scores = jnp.sum(normed * value_head.astype(jnp.float32)[None, :], axis=-1)
    return (layer_out, scores)


def solution(mesh):
    return jax.shard_map(
        local,
        mesh=mesh,
        in_specs=(
            P(("dp", "tensor"), None),
            P("tensor", None),
            P(("dp", "tensor"), None),
            P("dp"),
            P(),
        ),
        out_specs=(P(("dp", "tensor"), None), P(("dp", "tensor"))),
        check_vma=False,
    )
```

profile of v0, /device:TPU:24, one launch (start us, length us, event | category | flops | bytes accessed | tf_op | source)
XLA Modules:
  0.0 292.8 jit_solution(12664735985878418856)
XLA Ops:
  7.2 4.4 %copy.10 = bf16[16,16,8,896]{3,2,0,1:T(8,128)(2,1)} copy(bf16[16,16,8,896]{3,2,1,0:T(8,128)(2,1)} %bitcast.9) | data formatting | bytes 7340032 | tf_op jit(solution)/shard_map/all_to_all | solution.py:8
  11.6 0.0 copy-start.2
  11.6 6.4 %all-to-all-start = ((bf16[128,16,896]{2,0,1:T(8,128)(2,1)}), bf16[128,16,896]{2,0,1:T(8,128)(2,1)}, u32[]{:S(2)}, u32[]{:S(2)}) async-start(bf16[128,16,896]{2,0,1:T(8,128)(2,1)} %bitcast.8), calls=%async_computation | async-start | bytes 7340032 | tf_op jit(solution)/shard_map/all_to_all | solution.py:8
  18.0 0.0 reduce-scatter.2.cloned.1.call-start
  18.0 0.0 copy-done.2
  18.1 43.2 %all-to-all-done = bf16[128,16,896]{2,0,1:T(8,128)(2,1)} async-done(((bf16[128,16,896]{2,0,1:T(8,128)(2,1)}), bf16[128,16,896]{2,0,1:T(8,128)(2,1)}, u32[]{:S(2)}, u32[]{:S(2)}) %all-to-all-start) | async-done | bytes 3670048 | tf_op jit(solution)/shard_map/all_to_all | solution.py:8
  61.2 12.9 %gather_fusion = bf16[2048,896]{1,0:T(8,128)(2,1)} fusion(bf16[2048,896]{1,0:T(8,128)(2,1)} %bitcast.1, s32[2048]{0:T(1024)S(1)} %fusion.6), kind=kCustom, calls=%fused_computation | custom fusion | bytes 7348224 | tf_op jit(solution)/shard_map/jit(_take)/gather | solution.py:9
  74.2 24.4 %convolution_convert_fusion = bf16[2048,4096]{1,0:T(8,128)(2,1)} fusion(bf16[896,4096]{1,0:T(8,128)(2,1)} %param.6, bf16[2048,896]{1,0:T(8,128)(2,1)} %gather_fusion, pred[2048]{0:T(1024)(128)(4,1)S(1)} %compare_and_fusion), kind=kOutput, calls=%fused_computation.1 | convolution fusion | flops 15042609152 | bytes 27789312 | tf_op jit(solution)/shard_map/dot_general | solution.py:10
  98.6 0.0 copy-start.3
  98.6 0.0 copy-start.1
  98.6 0.0 reduce-scatter.2.cloned.1.call-update
  98.6 0.7 copy-done.3
  99.3 184.0 %reduce-scatter.2.cloned.1.call-done = bf16[128,4096]{1,0:T(8,128)(2,1)} async-done(((bf16[2048,4096]{1,0:T(8,128)(2,1)}), bf16[128,4096]{1,0:T(8,128)(2,1)}) %reduce-scatter.2.cloned.1.call-update) | async-done | bytes 1048592 | tf_op jit(solution)/shard_map/reduce_scatter | solution.py:11
  283.3 0.0 copy-done.1
  283.3 1.7 fusion.2
  285.0 0.0 copy-start
  285.0 0.9 fusion.4
  286.0 0.0 copy-done
  (4 shorter events, 0.0 us)
Async XLA Ops:
  11.6 6.5 %copy-start.2 = (s32[2048]{0:T(1024)S(1)}, s32[2048]{0:T(1024)}, u32[]{:S(2)}) copy-start(s32[2048]{0:T(1024)} %param.8) | copy-start | bytes 24580
  11.6 49.6 %all-to-all-start = ((bf16[128,16,896]{2,0,1:T(8,128)(2,1)}), bf16[128,16,896]{2,0,1:T(8,128)(2,1)}, u32[]{:S(2)}, u32[]{:S(2)}) async-start(bf16[128,16,896]{2,0,1:T(8,128)(2,1)} %bitcast.8), calls=%async_computation | async-start | bytes 7340032 | tf_op jit(solution)/shard_map/all_to_all | solution.py:8
  18.0 265.3 %reduce-scatter.2.cloned.1.call-start = ((), (), s32[]{:S(2)}) async-start(), calls=%async_computation.2 | async-start | bytes 17825792 | tf_op jit(solution)/shard_map/reduce_scatter | solution.py:11
  98.6 0.7 copy-start.3
  98.6 184.7 %copy-start.1 = (bf16[128,4096]{1,0:T(8,128)(2,1)S(1)}, bf16[128,4096]{1,0:T(8,128)(2,1)}, u32[]{:S(2)}) copy-start(bf16[128,4096]{1,0:T(8,128)(2,1)} %param.7) | copy-start | bytes 3145732
  285.0 1.0 copy-start
Sparse Core Ops, SparseCore 0:
  98.7 184.5 reduce-scatter.1
where the time goes:
time: 295 us; the launch traced here: 293 us
  waiting for transfers between devices  227 us (77%)
  matrix products  24.4 us (8%)
  local copies, waits for them, and re-layouts  18 us (6%)
  between operations  14.1 us (5%)
  starting transfers between devices  6.44 us (2%)
    reduce_scatter x1, waiting for transfers between devices, local(): lax.psum_scatter(full_term.astype(jnp.bfloat16), 'tensor', scatter_dimens...  184 us
    all_to_all x1, waiting for transfers between devices, local(): lax.all_to_all(hidden, 'tensor', split_axis=1, concat_axis=0, tiled=True)  43.2 us
    dot_general x1, matrix products, local(): full_term = jnp.dot(picked, down_weight, preferred_element_type=jnp.float32)  24.4 us
    gather x1, local copies, waits for them, and re-layouts, local(): picked = jnp.take(columns, row_order, axis=0)  12.9 us
    all_to_all x1, starting transfers between devices, local(): lax.all_to_all(hidden, 'tensor', split_axis=1, concat_axis=0, tiled=True)  6.4 us
  transfers between devices with their start and end apart: 2, of which 2 were waited for; matrix products, arithmetic and copies ran while one was open for 0% of the time, Pallas kernels for 0%

commit v1 on v0

v1 whole, which is shorter than its diff:
```python
import functools

import jax
import jax.numpy as jnp
from jax import lax
from jax.experimental import pallas as pl
from jax.experimental.pallas import tpu as pltpu
from jax.sharding import PartitionSpec as P

NY, NX, NC = 4, 2, 2
TILE = 256
A_TILES, B1_TILES, B2_TILES = 7, 5, 4
WA, WB1, WB2 = A_TILES * TILE, B1_TILES * TILE, B2_TILES * TILE
WA1 = 3 * TILE
MIB = 1 << 20


def hop(value, dy, dx, dc):
    pairs = []
    for y in range(NY):
        for x in range(NX):
            for c in range(NC):
                source = (y * NX + x) * NC + c
                target = ((y + dy) % NY * NX + (x + dx) % NX) * NC + (c + dc) % NC
                pairs.append((source, target))
    return lax.ppermute(value, "tensor", pairs)


def gather_kernel(order_ref, rows_ref, out_ref):
    order = order_ref[...]
    at = lax.broadcasted_iota(jnp.int32, (order.shape[0], rows_ref.shape[0]), 1)
    pick = jnp.where(at == order, 1.0, 0.0).astype(jnp.bfloat16)
    out_ref[...] = jnp.dot(
        pick, rows_ref[...], preferred_element_type=jnp.float32
    ).astype(jnp.bfloat16)


def gather(order, rows):
    n, (m, k) = order.shape[0], rows.shape
    return pl.pallas_call(
        gather_kernel,
        grid=(n // 256,),
        in_specs=[
            pl.BlockSpec((256, 1), lambda i: (i, 0)),
            pl.BlockSpec((m, k), lambda i: (0, 0)),
        ],
        out_specs=pl.BlockSpec((256, k), lambda i: (i, 0)),
        out_shape=jax.ShapeDtypeStruct((n, k), jnp.bfloat16),
        compiler_params=pltpu.CompilerParams(vmem_limit_bytes=32 * MIB),
        cost_estimate=pl.CostEstimate(
            flops=2 * n * m * k, bytes_accessed=2 * (m * k + n * k), transcendentals=0
        ),
    )(order, rows)


def term_kernel(split_b, own_ref, sib_ref, w_own_ref, w_sib_ref, *outs):
    j = pl.program_id(0)
    total = jnp.dot(own_ref[...], w_own_ref[...], preferred_element_type=jnp.float32)
    total += jnp.dot(sib_ref[...], w_sib_ref[...], preferred_element_type=jnp.float32)
    total = total.astype(jnp.bfloat16)

    @pl.when(j < A_TILES)
    def _():
        outs[0][...] = total[:128]
        outs[1][...] = total[128:]

    if split_b:

        @pl.when(jnp.logical_and(j >= A_TILES, j < A_TILES + B1_TILES))
        def _():
            outs[2][...] = total[:128]
            outs[3][...] = total[128:]

        @pl.when(j >= A_TILES + B1_TILES)
        def _():
            outs[4][...] = total[:128]
            outs[5][...] = total[128:]

    else:

        @pl.when(j >= A_TILES)
        def _():
            outs[2][...] = total[:128]
            outs[3][...] = total[128:]


def term(own, sib, w_own, w_sib, split_b):
    k, d = w_own.shape
    tiles = d // TILE
    if split_b:
        ranges = [(0, A_TILES), (A_TILES, B1_TILES), (A_TILES + B1_TILES, B2_TILES)]
    else:
        ranges = [(0, A_TILES), (A_TILES, B1_TILES + B2_TILES)]

    def out_spec(first, count):
        return pl.BlockSpec((128, TILE), lambda j: (0, jnp.clip(j - first, 0, count - 1)))

    return pl.pallas_call(
        functools.partial(term_kernel, split_b),
        grid=(tiles,),
        in_specs=[
            pl.BlockSpec((256, k), lambda j: (0, 0)),
            pl.BlockSpec((256, k), lambda j: (0, 0)),
            pl.BlockSpec((k, TILE), lambda j: (0, j)),
            pl.BlockSpec((k, TILE), lambda j: (0, j)),
        ],
        out_specs=[out_spec(*r) for r in ranges for _ in range(2)],
        out_shape=[
            jax.ShapeDtypeStruct((128, r[1] * TILE), jnp.bfloat16) for r in ranges for _ in range(2)
        ],
        compiler_params=pltpu.CompilerParams(vmem_limit_bytes=32 * MIB),
        cost_estimate=pl.CostEstimate(
            flops=2 * 256 * 2 * k * d,
            bytes_accessed=2 * (2 * k * d + 256 * d + 512 * k),
            transcendentals=0,
        ),
    )(own, sib, w_own, w_sib)


def whole_call(kernel, out_shape, *args):
    n_bytes = sum(a.size * a.dtype.itemsize for a in args)
    return pl.pallas_call(
        kernel,
        out_shape=out_shape,
        compiler_params=pltpu.CompilerParams(vmem_limit_bytes=32 * MIB),
        cost_estimate=pl.CostEstimate(flops=n_bytes, bytes_accessed=2 * n_bytes, transcendentals=0),
    )(*args)


def f32(ref):
    return ref[...].astype(jnp.float32)


def bf(shape):
    return jax.ShapeDtypeStruct(shape, jnp.bfloat16)


def add_left_kernel(w, base_ref, come_ref, out_ref):
    out_ref[:, :w] = (base_ref[:, :w].astype(jnp.float32) + f32(come_ref)).astype(jnp.bfloat16)
    out_ref[:, w:] = base_ref[:, w:]


def add_right_kernel(w, base_ref, come_ref, out_ref):
    out_ref[:, :w] = base_ref[:, :w]
    out_ref[:, w:] = (base_ref[:, w:].astype(jnp.float32) + f32(come_ref)).astype(jnp.bfloat16)


def add_part(base, come, left):
    if left:
        kernel = functools.partial(add_left_kernel, come.shape[1])
    else:
        kernel = functools.partial(add_right_kernel, base.shape[1] - come.shape[1])
    return whole_call(kernel, bf(base.shape), base, come)


def split_sum_kernel(w, base_ref, come_ref, left_ref, right_ref):
    left_ref[...] = (
        base_ref[:, :w].astype(jnp.float32) + come_ref[:, :w].astype(jnp.float32)
    ).astype(jnp.bfloat16)
    right_ref[...] = (
        base_ref[:, w:].astype(jnp.float32) + come_ref[:, w:].astype(jnp.float32)
    ).astype(jnp.bfloat16)


def split_sum(base, come, w):
    n, m = base.shape
    return whole_call(
        functools.partial(split_sum_kernel, w), [bf((n, w)), bf((n, m - w))], base, come
    )


def sum3_part_kernel(w, left, base_ref, x_ref, come_ref, out_ref):
    total = f32(base_ref) + f32(x_ref)
    if left:
        out_ref[:, :w] = (total[:, :w] + f32(come_ref)).astype(jnp.bfloat16)
        out_ref[:, w:] = total[:, w:].astype(jnp.bfloat16)
    else:
        out_ref[:, :w] = total[:, :w].astype(jnp.bfloat16)
        out_ref[:, w:] = (total[:, w:] + f32(come_ref)).astype(jnp.bfloat16)


def sum3_part(base, x_come, come, left):
    w = come.shape[1] if left else base.shape[1] - come.shape[1]
    return whole_call(
        functools.partial(sum3_part_kernel, w, left), bf(base.shape), base, x_come, come
    )


def sum3_kernel(a_ref, b_ref, c_ref, out_ref):
    out_ref[...] = (f32(a_ref) + f32(b_ref) + f32(c_ref)).astype(jnp.bfloat16)


def last_kernel(
    wa, a0, a1, a2, a3, b0, b1, b2, b3, residual_ref, head_ref, out_ref, score_ref
):
    down_a = f32(a0) + f32(a1) + f32(a2) + f32(a3)
    down_b = f32(b0) + f32(b1) + f32(b2) + f32(b3)
    out_a = (residual_ref[:, :wa].astype(jnp.float32) + down_a).astype(jnp.bfloat16)
    out_b = (residual_ref[:, wa:].astype(jnp.float32) + down_b).astype(jnp.bfloat16)
    out_ref[:, :wa] = out_a
    out_ref[:, wa:] = out_b
    wide_a, wide_b = out_a.astype(jnp.float32), out_b.astype(jnp.float32)
    squares = jnp.sum(wide_a * wide_a, axis=1, keepdims=True)
    squares += jnp.sum(wide_b * wide_b, axis=1, keepdims=True)
    scale = lax.rsqrt(squares / out_ref.shape[1] + 1e-5)
    head = head_ref[...].astype(jnp.float32)
    dots = jnp.sum((wide_a * scale) * head[:, :wa], axis=1, keepdims=True)
    dots += jnp.sum((wide_b * scale) * head[:, wa:], axis=1, keepdims=True)
    score_ref[...] = dots


def local(hidden, down_weight, residual, row_order, value_head):
    t = lax.axis_index("tensor")
    y, x, core = t // 4, t // 2 % 2, t % 2
    rows, d = residual.shape
    columns = lax.all_to_all(hidden, "tensor", split_axis=1, concat_axis=0, tiled=True)
    w_own = down_weight
    w_sib = hop(down_weight, 0, 0, 1)

    order = row_order.reshape(NY, NX, NC, rows)
    order = jnp.roll(order, (-y, -x, -core), axis=(0, 1, 2))
    order = order[jnp.array([2, 1, 3, 0])][:, ::-1]
    own_order = order[:, :, 0].reshape(-1, 1)
    sib_order = order[:, :, 1].reshape(-1, 1)

    def stage(n0, n1):
        sib = gather(sib_order[n0:n1], columns)
        sib_come = hop(sib, 0, 0, 1)
        own = gather(own_order[n0:n1], columns)
        return own, sib_come

    own2, sib2 = stage(0, 256)
    own_r, sib_r = stage(256, 1024)

    ax2, ao2, b1x, b1o, b2x, b2o = term(own2, sib2, w_own, w_sib, True)
    y1x = hop(b1x, 1, 0, 0)
    y3x = hop(b2x, 3, 0, 0)
    x2 = hop(ax2, 0, 1, 0)
    y1o = hop(b1o, 1, 0, 0)
    y3o = hop(b2o, 3, 0, 0)
    ax1, ao1, bx1, bo1 = term(own_r[:256], sib_r[:256], w_own, w_sib, False)
    x1 = hop(ax1, 0, 1, 0)
    ax3, ao3, bx3, bo3 = term(own_r[256:512], sib_r[256:512], w_own, w_sib, False)
    x3 = hop(ax3, 0, 1, 0)
    ax0, ao0, bx0, bo0 = term(own_r[512:], sib_r[512:], w_own, w_sib, False)
    x0 = hop(ax0, 0, 1, 0)

    v1x = hop(add_part(bx1, y1x, True), 1, 0, 0)
    v3x = hop(add_part(bx3, y3x, False), 3, 0, 0)
    s_left, s_right = split_sum(ao2, x2, WA1)
    u1 = hop(s_left, 1, 0, 0)
    u3 = hop(s_right, 3, 0, 0)
    v1o = hop(add_part(bo1, y1o, True), 1, 0, 0)
    v3o = hop(add_part(bo3, y3o, False), 3, 0, 0)
    g = hop(whole_call(sum3_kernel, bf(bx0.shape), bx0, v1x, v3x), 0, 1, 0)
    z1 = hop(sum3_part(ao1, x1, u1, True), 1, 0, 0)
    z3 = hop(sum3_part(ao3, x3, u3, False), 3, 0, 0)
    layer_out, scores = whole_call(
        functools.partial(last_kernel, WA),
        [bf((rows, d)), jax.ShapeDtypeStruct((rows, 1), jnp.float32)],
        ao0, x0, z1, z3, bo0, g, v1o, v3o, residual, value_head.reshape(1, d),
    )
    return (layer_out, scores.reshape(rows))


def solution(mesh):
    return jax.shard_map(
        local,
        mesh=mesh,
        in_specs=(
            P(("dp", "tensor"), None),
            P("tensor", None),
            P(("dp", "tensor"), None),
            P("dp"),
            P(),
        ),
        out_specs=(P(("dp", "tensor"), None), P(("dp", "tensor"))),
        check_vma=False,
    )
```

time: 295 us -> 176 us (0.60)
  waiting for transfers between devices: 227 us -> 64 us
  Pallas kernels: 0 us -> 75.6 us
  matrix products: 24.4 us -> 0 us
  starting transfers between devices: 6.44 us -> 27.5 us
  between operations: 14.1 us -> 1.03 us
  local copies, waits for them, and re-layouts: 18 us -> 5.99 us
    reduce_scatter x1 -> x0, waiting for transfers between devices: 184 us -> none  [local(): lax.psum_scatter(full_term.astype(jnp.bfloat16), 'tensor', scatter_dimens...]
    pallas_call x0 -> x17, Pallas kernels: none -> 75.6 us  [the longest x4 53.8 us: term(): pl.pallas_call(functools.partial(term_kernel, split_b), grid=(tiles,), in...]
    dot_general x1 -> x0, matrix products: 24.4 us -> none  [local(): full_term = jnp.dot(picked, down_weight, preferred_element_type=jnp.float32)]
    ppermute x0 -> x20, waiting for transfers between devices: none -> 21.6 us  [hop(): return lax.ppermute(value, 'tensor', pairs)]
    ppermute x0 -> x20, starting transfers between devices: none -> 21.1 us  [hop(): return lax.ppermute(value, 'tensor', pairs)]
    gather x1, local copies, waits for them, and re-layouts: 12.9 us -> 0.57 us  [local(): order = order[jnp.array([2, 1, 3, 0])][:, ::-1]]
  transfers between devices with their start and end apart: 2 -> 21, of which waited for: 2 -> 7; matrix products, arithmetic and copies ran while one was open for 0% -> 3% of each run, Pallas kernels for 0% -> 34%
where the time goes in v1:
time: 176 us; the launch traced here: 175 us
  Pallas kernels  75.6 us (43%)
  waiting for transfers between devices  64 us (36%)
  starting transfers between devices  27.5 us (16%)
  local copies, waits for them, and re-layouts  5.99 us (3%)
    pallas_call x4, Pallas kernels, term(): pl.pallas_call(functools.partial(term_kernel, split_b), grid=(tiles,), in...  53.8 us
    all_to_all x1, waiting for transfers between devices, local(): lax.all_to_all(hidden, 'tensor', split_axis=1, concat_axis=0, tiled=True)  42.3 us
    ppermute x20, waiting for transfers between devices, hop(): return lax.ppermute(value, 'tensor', pairs)  21.6 us
    ppermute x20, starting transfers between devices, hop(): return lax.ppermute(value, 'tensor', pairs)  21.1 us
    pallas_call x4, Pallas kernels, gather(): pl.pallas_call(gather_kernel, grid=(n // 256,), in_specs=[pl.BlockSpec((2...  18.9 us
    all_to_all x1, starting transfers between devices, local(): lax.all_to_all(hidden, 'tensor', split_axis=1, concat_axis=0, tiled=True)  6.41 us
    all_to_all x1, local copies, waits for them, and re-layouts, local(): lax.all_to_all(hidden, 'tensor', split_axis=1, concat_axis=0, tiled=True)  4.48 us
  transfers between devices with their start and end apart: 21, of which 7 were waited for; matrix products, arithmetic and copies ran while one was open for 3% of the time, Pallas kernels for 34%

profile of v1, /device:TPU:24, one launch (start us, length us, event | category | flops | bytes accessed | tf_op | source)
XLA Modules:
  0.0 174.8 jit_solution(17576415816306967079)
XLA Ops:
  0.7 4.5 %copy.16 = bf16[16,16,8,896]{3,2,0,1:T(8,128)(2,1)} copy(bf16[16,16,8,896]{3,2,1,0:T(8,128)(2,1)} %bitcast.17) | data formatting | bytes 7340032 | tf_op jit(solution)/shard_map/all_to_all | solution.py:216
  5.2 6.4 %all-to-all-start = ((bf16[128,16,896]{2,0,1:T(8,128)(2,1)}), bf16[128,16,896]{2,0,1:T(8,128)(2,1)}, u32[]{:S(2)}, u32[]{:S(2)}) async-start(bf16[128,16,896]{2,0,1:T(8,128)(2,1)} %bitcast.16), calls=%async_computation | async-start | bytes 7340032 | tf_op jit(solution)/shard_map/all_to_all | solution.py:216
  12.5 42.3 %all-to-all-done = bf16[128,16,896]{2,0,1:T(8,128)(2,1)} async-done(((bf16[128,16,896]{2,0,1:T(8,128)(2,1)}), bf16[128,16,896]{2,0,1:T(8,128)(2,1)}, u32[]{:S(2)}, u32[]{:S(2)}) %all-to-all-start) | async-done | bytes 3670048 | tf_op jit(solution)/shard_map/all_to_all | solution.py:216
  54.9 6.0 %shard_map.78 = bf16[768,896]{1,0:T(8,128)(2,1)S(1)} custom-call(s32[768,1]{1,0:T(8,128)S(1)} %copy.11.order_ref, bf16[2048,896]{1,0:T(8,128)(2,1)} %bitcast.3.rows_ref), custom_call_target="tpu_custom_call" | custom-call | flops 2818572288 | bytes 5046272 | tf_op jit(solution)/shard_map/pallas_call | solution.py:40
  61.5 3.3 %shard_map.82 = bf16[256,896]{1,0:T(8,128)(2,1)S(1)} custom-call(s32[256,1]{1,0:T(8,128)S(1)} %copy.13.order_ref, bf16[2048,896]{1,0:T(8,128)(2,1)} %bitcast.3.rows_ref), custom_call_target="tpu_custom_call" | custom-call | flops 939524096 | bytes 4128768 | tf_op jit(solution)/shard_map/pallas_call | solution.py:40
  65.4 3.5 %shard_map.81.own_ref = bf16[256,896]{1,0:T(8,128)(2,1)S(1)} custom-call(s32[256,1]{1,0:T(8,128)S(1)} %copy.12.order_ref, bf16[2048,896]{1,0:T(8,128)(2,1)} %bitcast.3.rows_ref), custom_call_target="tpu_custom_call" | custom-call | flops 939524096 | bytes 4128768 | tf_op jit(solution)/shard_map/pallas_call | solution.py:40
  68.9 6.2 %shard_map.77 = bf16[768,896]{1,0:T(8,128)(2,1)S(1)} custom-call(s32[768,1]{1,0:T(8,128)S(1)} %copy.10.order_ref, bf16[2048,896]{1,0:T(8,128)(2,1)} %bitcast.3.rows_ref), custom_call_target="tpu_custom_call" | custom-call | flops 2818572288 | bytes 5046272 | tf_op jit(solution)/shard_map/pallas_call | solution.py:40
  75.3 13.6 %shard_map.83 = (bf16[128,1792]{1,0:T(8,128)(2,1)S(1)}, bf16[128,1792]{1,0:T(8,128)(2,1)S(1)}, bf16[128,1280]{1,0:T(8,128)(2,1)S(1)}, bf16[128,1280]{1,0:T(8,128...) custom-call(bf16[256,896]{1,0:T(8,128)(2,1)S(1)} %shard_map.81.own_ref, ...), custom_call_target="tpu_custom_call" | custom-call | flops 3758096384 | bytes 17694720 | tf_op jit(solution)/shard_map/pallas_call | solution.py:98
  90.4 1.9 %collective-permute-start.11 = (bf16[128,1280]{1,0:T(8,128)(2,1)S(1)}, bf16[128,1280]{1,0:T(8,128)(2,1)S(1)}, u32[]{:S(2)}, u32[]{:S(2)}) collective-permute-start(bf16[128,1280]{1,0:T(8,128)(2,1)S(1)} %get-tuple-element.37), channel_id=1, source_target_pairs={{0,4},{1,5},{2,6},{3,7},{4,8},{5,9},{6,10},{7,11},{8,12},{9,13},{1... | collective-permute-start | bytes 983048 | tf_op jit(solution)/shard_map/ppermute | solution.py:26
  92.3 1.9 %collective-permute-start.16 = (bf16[128,1280]{1,0:T(8,128)(2,1)S(1)}, bf16[128,1280]{1,0:T(8,128)(2,1)S(1)}, u32[]{:S(2)}, u32[]{:S(2)}) collective-permute-start(bf16[128,1280]{1,0:T(8,128)(2,1)S(1)} %get-tuple-element.41), channel_id=1, source_target_pairs={{0,4},{1,5},{2,6},{3,7},{4,8},{5,9},{6,10},{7,11},{8,12},{9,13},{1... | collective-permute-start | bytes 983048 | tf_op jit(solution)/shard_map/ppermute | solution.py:26
  94.2 13.4 %shard_map.86 = (bf16[128,1792]{1,0:T(8,128)(2,1)S(1)}, bf16[128,1792]{1,0:T(8,128)(2,1)S(1)}, bf16[128,2304]{1,0:T(8,128)(2,1)S(1)}, bf16[128,2304]{1,0:T(8,128)(2,1)S(1)}) custom-call(bf16[256,896]{1,0:T(8,128)(2,1)S(1)} %get-tuple-element.49.own_ref, bf16[256,896]{1,0:T(8,128)(2,1)S(1)} %get-tuple-element.46.sib_ref, bf16[896,4096]{1,0:T(8,128)(2,1)S(1)} %bitcast.15, ...), custom_call_target="tpu_custom_call" | custom-call | flops 3758096384 | bytes 17694720 | tf_op jit(solution)/shard_map/pallas_call | solution.py:98
  107.6 13.4 %shard_map.80 = (bf16[128,1792]{1,0:T(8,128)(2,1)S(1)}, bf16[128,1792]{1,0:T(8,128)(2,1)S(1)}, bf16[128,2304]{1,0:T(8,128)(2,1)S(1)}, bf16[128,2304]{1,0:T(8,128)(2,1)S(1)}) custom-call(bf16[256,896]{1,0:T(8,128)(2,1)S(1)} %get-tuple-element.50.own_ref, bf16[256,896]{1,0:T(8,128)(2,1)S(1)} %get-tuple-element.47.sib_ref, bf16[896,4096]{1,0:T(8,128)(2,1)S(1)} %bitcast.15, ...), custom_call_target="tpu_custom_call" | custom-call | flops 3758096384 | bytes 17694720 | tf_op jit(solution)/shard_map/pallas_call | solution.py:98
  121.1 2.1 %collective-permute-start.8 = (bf16[128,1792]{1,0:T(8,128)(2,1)S(1)}, bf16[128,1792]{1,0:T(8,128)(2,1)S(1)}, u32[]{:S(2)}, u32[]{:S(2)}) collective-permute-start(bf16[128,1792]{1,0:T(8,128)(2,1)S(1)} %get-tuple-element.32), channel_id=1, source_target_pairs={{0,2},{1,3},{2,0},{3,1},{4,6},{5,7},{6,4},{7,5},{8,10},{9,11},{10,... | collective-permute-start | bytes 1376264 | tf_op jit(solution)/shard_map/ppermute | solution.py:26
  124.8 2.0 %collective-permute-start.12 = (bf16[128,2304]{1,0:T(8,128)(2,1)S(1)}, bf16[128,2304]{1,0:T(8,128)(2,1)S(1)}, u32[]{:S(2)}, u32[]{:S(2)}) collective-permute-start(bf16[128,2304]{1,0:T(8,128)(2,1)S(1)} %shard_map.88), channel_id=1, source_target_pairs={{0,4},{1,5},{2,6},{3,7},{4,8},{5,9},{6,10},{7,11},{8,12},{9,13},{1... | collective-permute-start | bytes 1769480 | tf_op jit(solution)/shard_map/ppermute | solution.py:26
  126.8 13.4 %shard_map.79 = (bf16[128,1792]{1,0:T(8,128)(2,1)S(1)}, bf16[128,1792]{1,0:T(8,128)(2,1)S(1)}, bf16[128,2304]{1,0:T(8,128)(2,1)S(1)}, bf16[128,2304]{1,0:T(8,128)(2,1)S(1)}) custom-call(bf16[256,896]{1,0:T(8,128)(2,1)S(1)} %get-tuple-element.51.own_ref, bf16[256,896]{1,0:T(8,128)(2,1)S(1)} %get-tuple-element.48.sib_ref, bf16[896,4096]{1,0:T(8,128)(2,1)S(1)} %bitcast.15, ...), custom_call_target="tpu_custom_call" | custom-call | flops 3758096384 | bytes 17694720 | tf_op jit(solution)/shard_map/pallas_call | solution.py:98
  140.2 2.1 %collective-permute-start.2 = (bf16[128,1792]{1,0:T(8,128)(2,1)S(1)}, bf16[128,1792]{1,0:T(8,128)(2,1)S(1)}, u32[]{:S(2)}, u32[]{:S(2)}) collective-permute-start(bf16[128,1792]{1,0:T(8,128)(2,1)S(1)} %get-tuple-element.25), channel_id=1, source_target_pairs={{0,2},{1,3},{2,0},{3,1},{4,6},{5,7},{6,4},{7,5},{8,10},{9,11},{10,... | collective-permute-start | bytes 1376264 | tf_op jit(solution)/shard_map/ppermute | solution.py:26
  143.9 1.8 %collective-permute-start.9 = (bf16[128,1024]{1,0:T(8,128)(2,1)S(1)}, bf16[128,1024]{1,0:T(8,128)(2,1)S(1)}, u32[]{:S(2)}, u32[]{:S(2)}) collective-permute-start(bf16[128,1024]{1,0:T(8,128)(2,1)S(1)} %get-tuple-element.33), channel_id=1, source_target_pairs={{0,12},{1,13},{2,14},{3,15},{4,0},{5,1},{6,2},{7,3},{8,4},{9,5},{1... | collective-permute-start | bytes 786440 | tf_op jit(solution)/shard_map/ppermute | solution.py:26
  146.1 3.2 %collective-permute-start.17 = (bf16[128,2304]{1,0:T(8,128)(2,1)S(1)}, bf16[128,2304]{1,0:T(8,128)(2,1)S(1)}, u32[]{:S(2)}, u32[]{:S(2)}) collective-permute-start(bf16[128,2304]{1,0:T(8,128)(2,1)S(1)} %shard_map.91), channel_id=1, source_target_pairs={{0,4},{1,5},{2,6},{3,7},{4,8},{5,9},{6,10},{7,11},{8,12},{9,13},{1... | collective-permute-start | bytes 1769480 | tf_op jit(solution)/shard_map/ppermute | solution.py:26
  150.6 3.8 %collective-permute-done.9.come_ref = bf16[128,1024]{1,0:T(8,128)(2,1)S(1)} collective-permute-done((bf16[128,1024]{1,0:T(8,128)(2,1)S(1)}, bf16[128,1024]{1,0:T(8,128)(2,1)S(1)}, u32[]{:S(2)}, u32[]{:S(2)}) %collective-permute-start.9) | collective-permute-done | bytes 262176 | tf_op jit(solution)/shard_map/ppermute | solution.py:26
  154.9 1.7 collective-permute-start.10
  156.6 10.4 %collective-permute-done.19.b3 = bf16[128,2304]{1,0:T(8,128)(2,1)S(1)} collective-permute-done((bf16[128,2304]{1,0:T(8,128)(2,1)S(1)}, bf16[128,2304]{1,0:T(8,128)(2,1)S(1)}, u32[]{:S(2)}, u32[]{:S(2)}) %collective-permute-start.19) | collective-permute-done | bytes 589856 | tf_op jit(solution)/shard_map/ppermute | solution.py:26
  167.0 2.0 %collective-permute-done.7.a2 = bf16[128,1792]{1,0:T(8,128)(2,1)S(1)} collective-permute-done((bf16[128,1792]{1,0:T(8,128)(2,1)S(1)}, bf16[128,1792]{1,0:T(8,128)(2,1)S(1)}, u32[]{:S(2)}, u32[]{:S(2)}) %collective-permute-start.7) | collective-permute-done | bytes 458784 | tf_op jit(solution)/shard_map/ppermute | solution.py:26
  169.0 3.2 %collective-permute-done.10.a3 = bf16[128,1792]{1,0:T(8,128)(2,1)S(1)} collective-permute-done((bf16[128,1792]{1,0:T(8,128)(2,1)S(1)}, bf16[128,1792]{1,0:T(8,128)(2,1)S(1)}, u32[]{:S(2)}, u32[]{:S(2)}) %collective-permute-start.10) | collective-permute-done | bytes 458784 | tf_op jit(solution)/shard_map/ppermute | solution.py:26
  172.2 1.9 %shard_map.93 = (bf16[128,4096]{1,0:T(8,128)(2,1)}, f32[128,1]{1,0:T(8,128)S(1)}) custom-call(bf16[128,1792]{1,0:T(8,128)(2,1)S(1)} %get-tuple-element.24.a0, bf16[128,1792]{1,0:T(8,128)(2,1)S(1)} %collective-permute-done.2.a1, bf16[128,1792]{1,0:T(8,128)(2,1)S(1)} %collective-permute-done.7.a2, bf16[128,1792]{1,0:T(8,128)(2,1)S(1)} %collective-permute-done.10.a3, ...), custom_call_target="tpu_custom_call" | custom-call | flops 5251072 | bytes 10502144 | tf_op jit(solution)/shard_map/pallas_call | solution.py:122
  (67 shorter events, 9.7 us)
Async XLA Ops:
  0.6 74.7 %collective-permute-start.1 = (bf16[896,4096]{1,0:T(8,128)(2,1)}, bf16[896,4096]{1,0:T(8,128)(2,1)}, u32[]{:S(2)}, u32[]{:S(2)}) collective-permute-start(bf16[896,4096]{1,0:T(8,128)(2,1)} %w_own_ref.7), channel_id=1, source_target_pairs={{0,1},{1,0},{2,3},{3,2},{4,5},{5,4},{6,7},{7,6},{8,9},{9,8},{10,11... | collective-permute-start | bytes 22020104 | tf_op jit(solution)/shard_map/ppermute | solution.py:26
  5.2 49.6 %all-to-all-start = ((bf16[128,16,896]{2,0,1:T(8,128)(2,1)}), bf16[128,16,896]{2,0,1:T(8,128)(2,1)}, u32[]{:S(2)}, u32[]{:S(2)}) async-start(bf16[128,16,896]{2,0,1:T(8,128)(2,1)} %bitcast.16), calls=%async_computation | async-start | bytes 7340032 | tf_op jit(solution)/shard_map/all_to_all | solution.py:216
  60.8 14.3 %collective-permute-start = (bf16[768,896]{1,0:T(8,128)(2,1)S(1)}, bf16[768,896]{1,0:T(8,128)(2,1)S(1)}, u32[]{:S(2)}, u32[]{:S(2)}) collective-permute-start(bf16[768,896]{1,0:T(8,128)(2,1)S(1)} %shard_map.78), channel_id=1, source_target_pairs={{0,1},{1,0},{2,3},{3,2},{4,5},{5,4},{6,7},{7,6},{8,9},{9,8},{10,11... | collective-permute-start | bytes 4128776 | tf_op jit(solution)/shard_map/ppermute | solution.py:26
  64.8 10.5 %collective-permute-start.4 = (bf16[256,896]{1,0:T(8,128)(2,1)S(1)}, bf16[256,896]{1,0:T(8,128)(2,1)S(1)}, u32[]{:S(2)}, u32[]{:S(2)}) collective-permute-start(bf16[256,896]{1,0:T(8,128)(2,1)S(1)} %shard_map.82), channel_id=1, source_target_pairs={{0,1},{1,0},{2,3},{3,2},{4,5},{5,4},{6,7},{7,6},{8,9},{9,8},{10,11... | collective-permute-start | bytes 1376264 | tf_op jit(solution)/shard_map/ppermute | solution.py:26
  65.4 9.9 %slice-start = ((s8[7340032]{0:T(1024)(128)(4,1)}), s8[4194304]{0:T(1024)(128)(4,1)S(1)}, s32[]{:S(2)}) async-start(s8[7340032]{0:T(1024)(128)(4,1)} %bitcast.14), calls=%async_computation.1 | async-start | bytes 8388608
  88.9 32.2 %collective-permute-start.13 = (bf16[128,1024]{1,0:T(8,128)(2,1)S(1)}, bf16[128,1024]{1,0:T(8,128)(2,1)S(1)}, u32[]{:S(2)}, u32[]{:S(2)}) collective-permute-start(bf16[128,1024]{1,0:T(8,128)(2,1)S(1)} %get-tuple-element.39), channel_id=1, source_target_pairs={{0,12},{1,13},{2,14},{3,15},{4,0},{5,1},{6,2},{7,3},{8,4},{9,5},{1... | collective-permute-start | bytes 786440 | tf_op jit(solution)/shard_map/ppermute | solution.py:26
  89.0 34.5 %collective-permute-start.18 = (bf16[128,1024]{1,0:T(8,128)(2,1)S(1)}, bf16[128,1024]{1,0:T(8,128)(2,1)S(1)}, u32[]{:S(2)}, u32[]{:S(2)}) collective-permute-start(bf16[128,1024]{1,0:T(8,128)(2,1)S(1)} %get-tuple-element.43), channel_id=1, source_target_pairs={{0,12},{1,13},{2,14},{3,15},{4,0},{5,1},{6,2},{7,3},{8,4},{9,5},{1... | collective-permute-start | bytes 786440 | tf_op jit(solution)/shard_map/ppermute | solution.py:26
  90.4 32.9 %collective-permute-start.11 = (bf16[128,1280]{1,0:T(8,128)(2,1)S(1)}, bf16[128,1280]{1,0:T(8,128)(2,1)S(1)}, u32[]{:S(2)}, u32[]{:S(2)}) collective-permute-start(bf16[128,1280]{1,0:T(8,128)(2,1)S(1)} %get-tuple-element.37), channel_id=1, source_target_pairs={{0,4},{1,5},{2,6},{3,7},{4,8},{5,9},{6,10},{7,11},{8,12},{9,13},{1... | collective-permute-start | bytes 983048 | tf_op jit(solution)/shard_map/ppermute | solution.py:26
  92.3 32.5 %collective-permute-start.16 = (bf16[128,1280]{1,0:T(8,128)(2,1)S(1)}, bf16[128,1280]{1,0:T(8,128)(2,1)S(1)}, u32[]{:S(2)}, u32[]{:S(2)}) collective-permute-start(bf16[128,1280]{1,0:T(8,128)(2,1)S(1)} %get-tuple-element.41), channel_id=1, source_target_pairs={{0,4},{1,5},{2,6},{3,7},{4,8},{5,9},{6,10},{7,11},{8,12},{9,13},{1... | collective-permute-start | bytes 983048 | tf_op jit(solution)/shard_map/ppermute | solution.py:26
  94.2 46.0 %collective-permute-start.5 = (bf16[128,1792]{1,0:T(8,128)(2,1)S(1)}, bf16[128,1792]{1,0:T(8,128)(2,1)S(1)}, u32[]{:S(2)}, u32[]{:S(2)}) collective-permute-start(bf16[128,1792]{1,0:T(8,128)(2,1)S(1)} %get-tuple-element.29), channel_id=1, source_target_pairs={{0,2},{1,3},{2,0},{3,1},{4,6},{5,7},{6,4},{7,5},{8,10},{9,11},{10,... | collective-permute-start | bytes 1376264 | tf_op jit(solution)/shard_map/ppermute | solution.py:26
  121.1 21.4 %collective-permute-start.8 = (bf16[128,1792]{1,0:T(8,128)(2,1)S(1)}, bf16[128,1792]{1,0:T(8,128)(2,1)S(1)}, u32[]{:S(2)}, u32[]{:S(2)}) collective-permute-start(bf16[128,1792]{1,0:T(8,128)(2,1)S(1)} %get-tuple-element.32), channel_id=1, source_target_pairs={{0,2},{1,3},{2,0},{3,1},{4,6},{5,7},{6,4},{7,5},{8,10},{9,11},{10,... | collective-permute-start | bytes 1376264 | tf_op jit(solution)/shard_map/ppermute | solution.py:26
  123.3 20.6 %collective-permute-start.3 = (bf16[128,1792]{1,0:T(8,128)(2,1)S(1)}, bf16[128,1792]{1,0:T(8,128)(2,1)S(1)}, u32[]{:S(2)}, u32[]{:S(2)}) collective-permute-start(bf16[128,1792]{1,0:T(8,128)(2,1)S(1)} %get-tuple-element.27), channel_id=1, source_target_pairs={{0,2},{1,3},{2,0},{3,1},{4,6},{5,7},{6,4},{7,5},{8,10},{9,11},{10,... | collective-permute-start | bytes 1376264 | tf_op jit(solution)/shard_map/ppermute | solution.py:26
  123.5 22.5 %collective-permute-start.14 = (bf16[128,2304]{1,0:T(8,128)(2,1)S(1)}, bf16[128,2304]{1,0:T(8,128)(2,1)S(1)}, u32[]{:S(2)}, u32[]{:S(2)}) collective-permute-start(bf16[128,2304]{1,0:T(8,128)(2,1)S(1)} %shard_map.89), channel_id=1, source_target_pairs={{0,12},{1,13},{2,14},{3,15},{4,0},{5,1},{6,2},{7,3},{8,4},{9,5},{1... | collective-permute-start | bytes 1769480 | tf_op jit(solution)/shard_map/ppermute | solution.py:26
  124.8 21.2 %collective-permute-start.12 = (bf16[128,2304]{1,0:T(8,128)(2,1)S(1)}, bf16[128,2304]{1,0:T(8,128)(2,1)S(1)}, u32[]{:S(2)}, u32[]{:S(2)}) collective-permute-start(bf16[128,2304]{1,0:T(8,128)(2,1)S(1)} %shard_map.88), channel_id=1, source_target_pairs={{0,4},{1,5},{2,6},{3,7},{4,8},{5,9},{6,10},{7,11},{8,12},{9,13},{1... | collective-permute-start | bytes 1769480 | tf_op jit(solution)/shard_map/ppermute | solution.py:26
  140.2 14.7 %collective-permute-start.2 = (bf16[128,1792]{1,0:T(8,128)(2,1)S(1)}, bf16[128,1792]{1,0:T(8,128)(2,1)S(1)}, u32[]{:S(2)}, u32[]{:S(2)}) collective-permute-start(bf16[128,1792]{1,0:T(8,128)(2,1)S(1)} %get-tuple-element.25), channel_id=1, source_target_pairs={{0,2},{1,3},{2,0},{3,1},{4,6},{5,7},{6,4},{7,5},{8,10},{9,11},{10,... | collective-permute-start | bytes 1376264 | tf_op jit(solution)/shard_map/ppermute | solution.py:26
  142.4 7.9 %collective-permute-start.6 = (bf16[128,768]{1,0:T(8,128)(2,1)S(1)}, bf16[128,768]{1,0:T(8,128)(2,1)S(1)}, u32[]{:S(2)}, u32[]{:S(2)}) collective-permute-start(bf16[128,768]{1,0:T(8,128)(2,1)S(1)} %get-tuple-element.30), channel_id=1, source_target_pairs={{0,4},{1,5},{2,6},{3,7},{4,8},{5,9},{6,10},{7,11},{8,12},{9,13},{1... | collective-permute-start | bytes 589832 | tf_op jit(solution)/shard_map/ppermute | solution.py:26
  143.9 10.5 %collective-permute-start.9 = (bf16[128,1024]{1,0:T(8,128)(2,1)S(1)}, bf16[128,1024]{1,0:T(8,128)(2,1)S(1)}, u32[]{:S(2)}, u32[]{:S(2)}) collective-permute-start(bf16[128,1024]{1,0:T(8,128)(2,1)S(1)} %get-tuple-element.33), channel_id=1, source_target_pairs={{0,12},{1,13},{2,14},{3,15},{4,0},{5,1},{6,2},{7,3},{8,4},{9,5},{1... | collective-permute-start | bytes 786440 | tf_op jit(solution)/shard_map/ppermute | solution.py:26
  145.8 10.8 %copy-start.1 = (bf16[4096]{0:T(1024)(128)(2,1)S(1)}, bf16[4096]{0:T(1024)(128)(2,1)}, u32[]{:S(2)}) copy-start(bf16[4096]{0:T(1024)(128)(2,1)} %param.10) | copy-start | bytes 24580
  145.8 26.4 %copy-start = (bf16[128,4096]{1,0:T(8,128)(2,1)S(1)}, bf16[128,4096]{1,0:T(8,128)(2,1)}, u32[]{:S(2)}) copy-start(bf16[128,4096]{1,0:T(8,128)(2,1)} %residual_ref.1) | copy-start | bytes 3145732
  145.9 21.1 %collective-permute-start.19 = (bf16[128,2304]{1,0:T(8,128)(2,1)S(1)}, bf16[128,2304]{1,0:T(8,128)(2,1)S(1)}, u32[]{:S(2)}, u32[]{:S(2)}) collective-permute-start(bf16[128,2304]{1,0:T(8,128)(2,1)S(1)} %shard_map.92), channel_id=1, source_target_pairs={{0,12},{1,13},{2,14},{3,15},{4,0},{5,1},{6,2},{7,3},{8,4},{9,5},{1... | collective-permute-start | bytes 1769480 | tf_op jit(solution)/shard_map/ppermute | solution.py:26
  146.1 21.0 %collective-permute-start.17 = (bf16[128,2304]{1,0:T(8,128)(2,1)S(1)}, bf16[128,2304]{1,0:T(8,128)(2,1)S(1)}, u32[]{:S(2)}, u32[]{:S(2)}) collective-permute-start(bf16[128,2304]{1,0:T(8,128)(2,1)S(1)} %shard_map.91), channel_id=1, source_target_pairs={{0,4},{1,5},{2,6},{3,7},{4,8},{5,9},{6,10},{7,11},{8,12},{9,13},{1... | collective-permute-start | bytes 1769480 | tf_op jit(solution)/shard_map/ppermute | solution.py:26
  150.4 21.8 %collective-permute-start.15 = (bf16[128,2304]{1,0:T(8,128)(2,1)S(1)}, bf16[128,2304]{1,0:T(8,128)(2,1)S(1)}, u32[]{:S(2)}, u32[]{:S(2)}) collective-permute-start(bf16[128,2304]{1,0:T(8,128)(2,1)S(1)} %shard_map.90), channel_id=1, source_target_pairs={{0,2},{1,3},{2,0},{3,1},{4,6},{5,7},{6,4},{7,5},{8,10},{9,11},{10,... | collective-permute-start | bytes 1769480 | tf_op jit(solution)/shard_map/ppermute | solution.py:26
  154.4 14.6 %collective-permute-start.7 = (bf16[128,1792]{1,0:T(8,128)(2,1)S(1)}, bf16[128,1792]{1,0:T(8,128)(2,1)S(1)}, u32[]{:S(2)}, u32[]{:S(2)}) collective-permute-start(bf16[128,1792]{1,0:T(8,128)(2,1)S(1)} %shard_map.85), channel_id=1, source_target_pairs={{0,4},{1,5},{2,6},{3,7},{4,8},{5,9},{6,10},{7,11},{8,12},{9,13},{1... | collective-permute-start | bytes 1376264 | tf_op jit(solution)/shard_map/ppermute | solution.py:26
  154.9 17.3 %collective-permute-start.10 = (bf16[128,1792]{1,0:T(8,128)(2,1)S(1)}, bf16[128,1792]{1,0:T(8,128)(2,1)S(1)}, u32[]{:S(2)}, u32[]{:S(2)}) collective-permute-start(bf16[128,1792]{1,0:T(8,128)(2,1)S(1)} %shard_map.87), channel_id=1, source_target_pairs={{0,12},{1,13},{2,14},{3,15},{4,0},{5,1},{6,2},{7,3},{8,4},{9,5},{1... | collective-permute-start | bytes 1376264 | tf_op jit(solution)/shard_map/ppermute | solution.py:26
  (3 other events, 19.3 us)

commit v2 on v0

v2 whole, which is shorter than its diff:
```python
import functools

import jax
import jax.numpy as jnp
from jax import lax
from jax.experimental import pallas as pl
from jax.experimental.pallas import tpu as pltpu
from jax.sharding import PartitionSpec as P

NY, NX, NC = 4, 2, 2
TILE = 256
A_TILES, B1_TILES, B2_TILES = 7, 5, 4
WA, WB1, WB2 = A_TILES * TILE, B1_TILES * TILE, B2_TILES * TILE
WB = WB1 + WB2
WA1 = 3 * TILE
MIB = 1 << 20


def hop(value, dy, dx, dc):
    pairs = []
    for y in range(NY):
        for x in range(NX):
            for c in range(NC):
                source = (y * NX + x) * NC + c
                target = ((y + dy) % NY * NX + (x + dx) % NX) * NC + (c + dc) % NC
                pairs.append((source, target))
    return lax.ppermute(value, "tensor", pairs)


def whole_call(kernel, out_shape, *args, scratch=(), flops=0, after=(), hbm=False, limit=24, out_specs=None):
    n_bytes = sum(a.size * a.dtype.itemsize for a in args)
    n, m = len(args), len(after)

    def without_after(*refs):
        kernel(*refs[:n], *refs[n + m :])

    space = pltpu.HBM if hbm else pltpu.VMEM
    return pl.pallas_call(
        without_after,
        out_shape=out_shape,
        in_specs=[pl.BlockSpec(memory_space=space)] * n
        + [pl.BlockSpec(memory_space=pl.ANY)] * m,
        **({"out_specs": out_specs} if out_specs else {}),
        scratch_shapes=scratch,
        compiler_params=pltpu.CompilerParams(vmem_limit_bytes=limit * MIB),
        cost_estimate=pl.CostEstimate(
            flops=flops or n_bytes, bytes_accessed=0 if flops else n_bytes, transcendentals=0
        ),
    )(*args, *after)


def f32(ref, rows=slice(None), columns=slice(None)):
    return ref[rows, columns].astype(jnp.float32)


def bf(*shape):
    return jax.ShapeDtypeStruct(shape, jnp.bfloat16)


def blocks_kernel(hidden_ref, out_ref, held, in_sems, out_sems):
    n, rows, width = held.shape
    comes, goes = [], []
    for at in range(n):
        columns = slice(at * width, (at + 1) * width)
        comes.append(
            pltpu.make_async_copy(hidden_ref.at[:, columns], held.at[at], in_sems.at[at])
        )
        goes.append(
            pltpu.make_async_copy(
                held.at[at], out_ref.at[at * rows : (at + 1) * rows], out_sems.at[at]
            )
        )
    for copy in comes:
        copy.start()
    for come, go in zip(comes, goes):
        come.wait()
        go.start()
    for copy in goes:
        copy.wait()


def gather_kernel(first, order_ref, rows_ref, out_ref):
    for at in range(0, out_ref.shape[0], 256):
        order = order_ref[first + at : first + at + 256]
        place = lax.broadcasted_iota(jnp.int32, (256, rows_ref.shape[0]), 1)
        pick = jnp.where(place == order, 1.0, 0.0).astype(jnp.bfloat16)
        out_ref[at : at + 256] = jnp.dot(
            pick, rows_ref[...], preferred_element_type=jnp.float32
        ).astype(jnp.bfloat16)


def first_gather_kernel(first, parts, order_ref, rows_ref, held_ref, out_ref, sems):
    step = rows_ref.shape[0] // parts
    copies = []
    for at in range(parts):
        part = slice(at * step, (at + 1) * step)
        copies.append(
            pltpu.make_async_copy(rows_ref.at[part], held_ref.at[part], sems.at[at])
        )
    for copy in copies:
        copy.start()
    total = jnp.zeros(out_ref.shape, jnp.float32)
    for at in range(parts):
        place = lax.broadcasted_iota(jnp.int32, (256, step), 1) + at * step
        pick = jnp.where(place == order_ref[first : first + 256], 1.0, 0.0).astype(jnp.bfloat16)
        copies[at].wait()
        total += jnp.dot(
            pick, held_ref[at * step : (at + 1) * step], preferred_element_type=jnp.float32
        )
    out_ref[...] = total.astype(jnp.bfloat16)


def first_gather(order, rows, first, after):
    m, k = rows.shape
    parts = 4
    n = len(after)
    kernel = functools.partial(first_gather_kernel, first, parts)
    return pl.pallas_call(
        lambda order_ref, rows_ref, *refs: kernel(order_ref, rows_ref, *refs[n:]),
        out_shape=[bf(m, k), bf(256, k)],
        in_specs=[pl.BlockSpec(memory_space=pltpu.VMEM)]
        + [pl.BlockSpec(memory_space=pl.ANY)] * (n + 1),
        scratch_shapes=[pltpu.SemaphoreType.DMA((parts,))],
        compiler_params=pltpu.CompilerParams(vmem_limit_bytes=24 * MIB),
        cost_estimate=pl.CostEstimate(
            flops=2 * 256 * m * k, bytes_accessed=0, transcendentals=0
        ),
    )(order, rows, *after)


def gather(order, rows, first, count, after):
    m, k = rows.shape
    return whole_call(
        functools.partial(gather_kernel, first), bf(count, k), order, rows,
        flops=2 * count * m * k, after=after,
    )


def second_gather_kernel(first, second, order_ref, rows_ref, w_ref, w_out_ref, *refs):
    first_ref, second_ref, sem = refs
    copy = pltpu.make_async_copy(w_ref, w_out_ref, sem)
    copy.start()
    gather_kernel(first, order_ref, rows_ref, first_ref)
    gather_kernel(second, order_ref, rows_ref, second_ref)
    copy.wait()


def second_gather(order, rows, first, second, w, after):
    m, k = rows.shape
    n = len(after)
    kernel = functools.partial(second_gather_kernel, first, second)
    return pl.pallas_call(
        lambda order_ref, rows_ref, w_ref, *refs: kernel(order_ref, rows_ref, w_ref, *refs[n:]),
        out_shape=[bf(*w.shape), bf(256, k), bf(512, k)],
        in_specs=[pl.BlockSpec(memory_space=pltpu.VMEM)] * 2
        + [pl.BlockSpec(memory_space=pl.ANY)] * (n + 1),
        scratch_shapes=[pltpu.SemaphoreType.DMA],
        compiler_params=pltpu.CompilerParams(vmem_limit_bytes=24 * MIB),
        cost_estimate=pl.CostEstimate(
            flops=2 * 768 * m * k, bytes_accessed=0, transcendentals=0
        ),
    )(order, rows, w, *after)


def term_kernel(ranges, own_ref, sib_ref, w_own_ref, w_sib_ref, *outs):
    for first, count, groups in ranges:
        for j in range(count):
            tile = slice((first + j) * TILE, (first + j + 1) * TILE)
            here = slice(j * TILE, (j + 1) * TILE)
            total = jnp.dot(own_ref[...], w_own_ref[:, tile], preferred_element_type=jnp.float32)
            total += jnp.dot(sib_ref[...], w_sib_ref[:, tile], preferred_element_type=jnp.float32)
            total = total.astype(jnp.bfloat16)
            for out, blocks in zip(outs, groups):
                for at, block in enumerate(blocks):
                    out[at * 128 : (at + 1) * 128, here] = total[block * 128 : (block + 1) * 128]
        outs = outs[len(groups) :]


def term(own, sib, w_own, w_sib, ranges, after):
    k = w_own.shape[0]
    shapes = [bf(128 * len(g), count * TILE) for _, count, groups in ranges for g in groups]
    return whole_call(
        functools.partial(term_kernel, ranges), shapes, own, sib, w_own, w_sib,
        flops=4 * own.shape[0] * k * TILE * sum(r[1] for r in ranges), after=after,
    )


def left_kernel(row, base_ref, come_ref, out_ref):
    rows = slice(row, row + 128)
    out_ref[:, :WB1] = (f32(base_ref, columns=slice(WB1)) + f32(come_ref, rows)).astype(jnp.bfloat16)
    out_ref[:, WB1:WB] = base_ref[:, WB1:]


def right_kernel(row, base_ref, come_ref, out_ref):
    rows = slice(row, row + 128)
    out_ref[:, :WB1] = base_ref[:, :WB1]
    out_ref[:, WB1:WB] = (
        f32(base_ref, columns=slice(WB1, WB)) + f32(come_ref, rows)
    ).astype(jnp.bfloat16)


def left_more_kernel(base_ref, come_ref, a_ref, x_ref, out_ref):
    left_kernel(128, base_ref, come_ref, out_ref)
    c = slice(WA1)
    out_ref[:, WB:] = (f32(a_ref, columns=c) + f32(x_ref, columns=c)).astype(jnp.bfloat16)


def right_more_kernel(base_ref, come_ref, a_ref, x_ref, out_ref):
    right_kernel(128, base_ref, come_ref, out_ref)
    c = slice(WA1, WA)
    out_ref[:, WB:] = (f32(a_ref, columns=c) + f32(x_ref, columns=c)).astype(jnp.bfloat16)


def to_right_kernel(a_ref, x_ref, come_ref, out_ref):
    total = f32(a_ref) + f32(x_ref, slice(0, 128))
    out_ref[:, :WA1] = (total[:, :WA1] + f32(come_ref, columns=slice(WB, None))).astype(jnp.bfloat16)
    out_ref[:, WA1:] = total[:, WA1:].astype(jnp.bfloat16)


def to_left_kernel(a_ref, x_ref, come_ref, out_ref):
    total = f32(a_ref) + f32(x_ref, slice(128, 256))
    out_ref[:, :WA1] = total[:, :WA1].astype(jnp.bfloat16)
    out_ref[:, WA1:] = (total[:, WA1:] + f32(come_ref, columns=slice(WB, None))).astype(jnp.bfloat16)


def sum3_kernel(a_ref, b_ref, c_ref, out_ref):
    out_ref[...] = (f32(a_ref) + f32(b_ref) + f32(c_ref)).astype(jnp.bfloat16)


def last_kernel(a0, a1, a2, a3, b0, b1, b2, b3, residual_ref, head_ref, out_ref, score_ref):
    c = slice(WB)
    down_a = f32(a0) + f32(a1) + f32(a2) + f32(a3)
    down_b = f32(b0) + f32(b1) + f32(b2, columns=c) + f32(b3, columns=c)
    out_a = (f32(residual_ref, columns=slice(WA)) + down_a).astype(jnp.bfloat16)
    out_b = (f32(residual_ref, columns=slice(WA, None)) + down_b).astype(jnp.bfloat16)
    out_ref[:, :WA] = out_a
    out_ref[:, WA:] = out_b
    wide_a, wide_b = out_a.astype(jnp.float32), out_b.astype(jnp.float32)
    squares = jnp.sum(wide_a * wide_a, axis=1, keepdims=True)
    squares += jnp.sum(wide_b * wide_b, axis=1, keepdims=True)
    scale = lax.rsqrt(squares / out_ref.shape[1] + 1e-5)
    head = head_ref[...].astype(jnp.float32)
    dots = jnp.sum((wide_a * scale) * head[:, :WA], axis=1, keepdims=True)
    dots += jnp.sum((wide_b * scale) * head[:, WA:], axis=1, keepdims=True)
    n = dots.shape[0]
    same = lax.broadcasted_iota(jnp.int32, (n, n), 0) == lax.broadcasted_iota(jnp.int32, (n, n), 1)
    score_ref[...] = jnp.sum(jnp.where(same, dots, 0.0), axis=0, keepdims=True)


def local(hidden, down_weight, residual, row_order, value_head):
    t = lax.axis_index("tensor")
    y, x, core = t // 4, t // 2 % 2, t % 2
    rows, d = residual.shape
    k = down_weight.shape[0]

    blocks = whole_call(
        blocks_kernel, bf(NY * NX * NC * rows, k), hidden,
        scratch=[
            pltpu.VMEM((NY * NX * NC, rows, k), jnp.bfloat16),
            pltpu.SemaphoreType.DMA((NY * NX * NC,)),
            pltpu.SemaphoreType.DMA((NY * NX * NC,)),
        ],
        hbm=True, limit=60,
        out_specs=pl.BlockSpec(memory_space=pltpu.HBM),
    )
    held = lax.all_to_all(blocks, "tensor", split_axis=0, concat_axis=0, tiled=True)
    w_own = down_weight
    w_sib = hop(down_weight, 0, 0, 1)

    order = row_order.reshape(NY, NX, NC, rows)
    order = lax.dynamic_slice_in_dim(jnp.concatenate([order, order], axis=0), y, NY, 0)
    order = jnp.where(x == 0, order[:, ::-1], order)
    order = jnp.where(core == 0, order[:, :, ::-1], order)
    order = jnp.stack([order[2], order[1], order[3], order[0]])
    order = order.transpose(2, 0, 1, 3).reshape(-1, 1)
    own = order.shape[0] // 2

    tb1, tb2 = A_TILES, A_TILES + B1_TILES
    b_only = ((tb1, B1_TILES, ((0, 1),)), (tb2, B2_TILES, ((0, 1),)))
    a_only = ((0, A_TILES, ((0,), (1,))),)
    two_a = ((0, A_TILES, ((0, 2), (1,), (3,))),)
    two_b = ((tb1, B1_TILES + B2_TILES, ((0,), (2,), (1,), (3,))),)
    both = ((0, A_TILES, ((0,), (1,))), (tb1, B1_TILES + B2_TILES, ((0,), (1,))))

    held, give2 = first_gather(order, held, 0, (w_sib,))
    sib2 = hop(give2, 0, 0, 1)
    w_sib, own2, give13 = second_gather(order, held, own, 256, w_sib, (give2,))
    sib13 = hop(give13, 0, 0, 1)
    b1, b2 = term(own2, sib2, w_own, w_sib, b_only, ())
    y1 = hop(b1, 1, 0, 0)
    y3 = hop(b2, 3, 0, 0)
    ax2, ao2 = term(own2, sib2, w_own, w_sib, a_only, (b1,))
    x2 = hop(ax2, 0, 1, 0)
    own13 = gather(order, held, own + 256, 512, (ax2,))
    ax13, ao1, ao3 = term(own13, sib13, w_own, w_sib, two_a, (own13,))
    x13 = hop(ax13, 0, 1, 0)
    bx1, bx3, bo1, bo3 = term(own13, sib13, w_own, w_sib, two_b, (ax13,))
    tv1 = whole_call(functools.partial(left_kernel, 0), bf(128, WB), bx1, y1)
    v1 = hop(tv1, 1, 0, 0)
    tv3 = whole_call(functools.partial(right_kernel, 0), bf(128, WB), bx3, y3, after=(tv1,))
    v3 = hop(tv3, 3, 0, 0)
    give0 = gather(order, held, 768, 256, (tv3, x2))
    sib0 = hop(give0, 0, 0, 1)
    own0 = gather(order, held, own + 768, 256, (give0,))
    ax0, ao0, bx0, bo0 = term(own0, sib0, w_own, w_sib, both, (own0,))
    x0 = hop(ax0, 0, 1, 0)
    tu1 = whole_call(left_more_kernel, bf(128, WB + WA1), bo1, y1, ao2, x2, after=(ax0, v1))
    u1 = hop(tu1, 1, 0, 0)
    tu3 = whole_call(right_more_kernel, bf(128, WB + WA - WA1), bo3, y3, ao2, x2, after=(tu1, v3))
    u3 = hop(tu3, 3, 0, 0)
    tg = whole_call(sum3_kernel, bf(128, WB), bx0, v1, v3, after=(tu3,))
    g = hop(tg, 0, 1, 0)
    tz1 = whole_call(to_right_kernel, bf(128, WA), ao1, x13, u1, after=(tg,))
    z1 = hop(tz1, 1, 0, 0)
    tz3 = whole_call(to_left_kernel, bf(128, WA), ao3, x13, u3, after=(tz1,))
    z3 = hop(tz3, 3, 0, 0)
    layer_out, scores = whole_call(
        last_kernel,
        [bf(rows, d), jax.ShapeDtypeStruct((1, rows), jnp.float32)],
        ao0, x0, z1, z3, bo0, g, u1, u3, residual, value_head.reshape(1, d),
    )
    return (layer_out, scores.reshape(rows))


def solution(mesh):
    return jax.shard_map(
        local,
        mesh=mesh,
        in_specs=(
            P(("dp", "tensor"), None),
            P("tensor", None),
            P(("dp", "tensor"), None),
            P("dp"),
            P(),
        ),
        out_specs=(P(("dp", "tensor"), None), P(("dp", "tensor"))),
        check_vma=False,
    )
```

time: 295 us -> 140 us (0.47)
  waiting for transfers between devices: 227 us -> 78.9 us
  Pallas kernels: 0 us -> 36.4 us
  matrix products: 24.4 us -> 0 us
  local copies, waits for them, and re-layouts: 18 us -> 0.45 us
  starting transfers between devices: 6.44 us -> 22.8 us
  between operations: 14.1 us -> 0.93 us
    reduce_scatter x1 -> x0, waiting for transfers between devices: 184 us -> none  [local(): lax.psum_scatter(full_term.astype(jnp.bfloat16), 'tensor', scatter_dimens...]
    pallas_call x0 -> x19, Pallas kernels: none -> 36.4 us  [the longest x17 29.7 us: whole_call(): pl.pallas_call(without_after, out_shape=out_shape, in_specs=[pl.BlockSpec...]
    ppermute x0 -> x16, waiting for transfers between devices: none -> 36.2 us  [hop(): return lax.ppermute(value, 'tensor', pairs)]
    dot_general x1 -> x0, matrix products: 24.4 us -> none  [local(): full_term = jnp.dot(picked, down_weight, preferred_element_type=jnp.float32)]
    ppermute x0 -> x16, starting transfers between devices: none -> 16.5 us  [hop(): return lax.ppermute(value, 'tensor', pairs)]
    gather x1 -> x0, local copies, waits for them, and re-layouts: 12.9 us -> none  [local(): picked = jnp.take(columns, row_order, axis=0)]
    all_to_all x1 -> x0, local copies, waits for them, and re-layouts: 4.43 us -> none  [local(): lax.all_to_all(hidden, 'tensor', split_axis=1, concat_axis=0, tiled=True)]
  transfers between devices with their start and end apart: 2 -> 17, of which waited for: 2 -> 9; matrix products, arithmetic and copies ran while one was open for 0% -> 0% of each run, Pallas kernels for 0% -> 22%
where the time goes in v2:
time: 140 us
  waiting for transfers between devices  78.9 us (56%)
  Pallas kernels  36.4 us (26%)
  starting transfers between devices  22.8 us (16%)
    all_to_all x1, waiting for transfers between devices, local(): lax.all_to_all(blocks, 'tensor', split_axis=0, concat_axis=0, tiled=True)  42.7 us
    ppermute x16, waiting for transfers between devices, hop(): return lax.ppermute(value, 'tensor', pairs)  36.2 us
    pallas_call x17, Pallas kernels, whole_call(): pl.pallas_call(without_after, out_shape=out_shape, in_specs=[pl.BlockSpec...  29.7 us
    ppermute x16, starting transfers between devices, hop(): return lax.ppermute(value, 'tensor', pairs)  16.5 us
    all_to_all x1, starting transfers between devices, local(): lax.all_to_all(blocks, 'tensor', split_axis=0, concat_axis=0, tiled=True)  6.29 us
    pallas_call x1, Pallas kernels, second_gather(): pl.pallas_call(lambda order_ref, rows_ref, w_ref, *refs: kernel(order_ref...  3.49 us
    pallas_call x1, Pallas kernels, first_gather(): pl.pallas_call(lambda order_ref, rows_ref, *refs: kernel(order_ref, rows_...  3.22 us
  transfers between devices with their start and end apart: 17, of which 9 were waited for; matrix products, arithmetic and copies ran while one was open for 0% of the time, Pallas kernels for 22%

profile of v2, /device:TPU:24, one launch (start us, length us, event | category | flops | bytes accessed | tf_op | source)
XLA Modules:
  0.0 139.5 jit_solution(13638809303408481178)
XLA Ops:
  0.7 3.8 %shard_map.68 = bf16[2048,896]{1,0:T(8,128)(2,1)} custom-call(bf16[128,14336]{1,0:T(8,128)(2,1)} %refs_0_.1), custom_call_target="tpu_custom_call" | custom-call | flops 3670016 | bytes 3670016 | tf_op jit(solution)/shard_map/pallas_call | solution.py:38
  4.6 6.3 %all-to-all-start = ((bf16[16,128,896]{2,1,0:T(8,128)(2,1)}), bf16[16,128,896]{2,1,0:T(8,128)(2,1)}, u32[]{:S(2)}, u32[]{:S(2)}) async-start(bf16[16,128,896]{2,1,0:T(8,128)(2,1)} %bitcast.9), calls=%async_computation | async-start | bytes 7340032 | tf_op jit(solution)/shard_map/all_to_all | solution.py:266
  11.4 42.7 %all-to-all-done = bf16[16,128,896]{2,1,0:T(8,128)(2,1)} async-done(((bf16[16,128,896]{2,1,0:T(8,128)(2,1)}), bf16[16,128,896]{2,1,0:T(8,128)(2,1)}, u32[]{:S(2)}, u32[]{:S(2)}) %all-to-all-start) | async-done | bytes 3670048 | tf_op jit(solution)/shard_map/all_to_all | solution.py:266
  54.1 3.2 %shard_map.69 = (bf16[2048,896]{1,0:T(8,128)(2,1)S(1)}, bf16[256,896]{1,0:T(8,128)(2,1)S(1)}) custom-call(s32[2048,1]{1,0:T(8,128)S(1)} %copy.12.order_ref.refs_0_, bf16[2048,896]{1,0:T(8,128)(2,1)} %bitcast.4.rows_ref, bf16[896,4096]{1,0:T(8,128)(2,1)} %collective-permute-done.refs_0_.w_ref), custom_call_target="tpu_custom_call" | custom-call | flops 939524096 | tf_op jit(solution)/shard_map/pallas_call | solution.py:118
  57.4 3.5 %shard_map.70 = (bf16[896,4096]{1,0:T(8,128)(2,1)S(1)}, bf16[256,896]{1,0:T(8,128)(2,1)S(1)}, bf16[512,896]{1,0:T(8,128)(2,1)S(1)}) custom-call(s32[2048,1]{1,0:T(8,128)S(1)} %copy.12.order_ref.refs_0_, bf16[2048,896]{1,0:T(8,128)(2,1)S(1)} %get-tuple-element.24.rows_ref.refs_1_, bf16[896,4096]{1,0:T(8,128)(2,1)} %collective-permute-done.refs_0_.w_ref, ...), custom_call_target="tpu_custom_call" | custom-call | flops 2818572288 | tf_op jit(solution)/shard_map/pallas_call | solution.py:152
  61.5 2.6 %shard_map.71 = (bf16[256,1280]{1,0:T(8,128)(2,1)S(1)}, bf16[256,1024]{1,0:T(8,128)(2,1)S(1)}) custom-call(bf16[256,896]{1,0:T(8,128)(2,1)S(1)} %get-tuple-element.26.refs_0_, bf16[256,896]{1,0:T(8,128)(2,1)S(1)} %collective-permute-done.1.refs_1_, bf16[896,4096]{1,0:T(8,128)(2,1)S(1)} %bitcast.8, bf16[896,4096]{1,0:T(8,128)(2,1)S(1)} %get-tuple-element.27.refs_3_), custom_call_target="tpu_custom_call" | custom-call | flops 2113929216 | tf_op jit(solution)/shard_map/pallas_call | solution.py:38
  64.1 1.8 %collective-permute-start.4 = (bf16[256,1280]{1,0:T(8,128)(2,1)S(1)}, bf16[256,1280]{1,0:T(8,128)(2,1)S(1)}, u32[]{:S(2)}, u32[]{:S(2)}) collective-permute-start(bf16[256,1280]{1,0:T(8,128)(2,1)S(1)} %get-tuple-element.28.refs_4_), channel_id=1, source_target_pairs={{0,4},{1,5},{2,6},{3,7},{4,8},{5,9},{6,10},{7,11},{8,12},{9,13},{1... | collective-permute-start | bytes 1966088 | tf_op jit(solution)/shard_map/ppermute | solution.py:27
  66.3 2.0 %shard_map.72 = (bf16[128,1792]{1,0:T(8,128)(2,1)S(1)}, bf16[128,1792]{1,0:T(8,128)(2,1)S(1)}) custom-call(bf16[256,896]{1,0:T(8,128)(2,1)S(1)} %get-tuple-element.26.refs_0_, bf16[256,896]{1,0:T(8,128)(2,1)S(1)} %collective-permute-done.1.refs_1_, bf16[896,4096]{1,0:T(8,128)(2,1)S(1)} %bitcast.8, bf16[896,4096]{1,0:T(8,128)(2,1)S(1)} %get-tuple-element.27.refs_3_, ...), custom_call_target="tpu_custom_call" | custom-call | flops 1644167168 | tf_op jit(solution)/shard_map/pallas_call | solution.py:38
  68.7 2.4 %shard_map.73.refs_0_.refs_4_ = bf16[512,896]{1,0:T(8,128)(2,1)S(1)} custom-call(s32[2048,1]{1,0:T(8,128)S(1)} %copy.12.order_ref.refs_0_, bf16[2048,896]{1,0:T(8,128)(2,1)S(1)} %get-tuple-element.24.rows_ref.refs_1_, bf16[128,1792]{1,0:T(8,128)(2,1)S(1)} %get-tuple-element.29.refs_2_), custom_call_target="tpu_custom_call" | custom-call | flops 1879048192 | tf_op jit(solution)/shard_map/pallas_call | solution.py:38
  71.1 4.0 %shard_map.74 = (bf16[256,1792]{1,0:T(8,128)(2,1)S(1)}, bf16[128,1792]{1,0:T(8,128)(2,1)S(1)}, bf16[128,1792]{1,0:T(8,128)(2,1)S(1)}) custom-call(bf16[512,896]{1,0:T(8,128)(2,1)S(1)} %shard_map.73.refs_0_.refs_4_, bf16[512,896]{1,0:T(8,128)(2,1)S(1)} %collective-permute-done.2.refs_1_, bf16[896,4096]{1,0:T(8,128)(2,1)S(1)} %bitcast.8, ...), custom_call_target="tpu_custom_call" | custom-call | flops 3288334336 | tf_op jit(solution)/shard_map/pallas_call | solution.py:38
  75.1 5.0 %shard_map.75 = (bf16[128,2304]{1,0:T(8,128)(2,1)S(1)}, bf16[128,2304]{1,0:T(8,128)(2,1)S(1)}, bf16[128,2304]{1,0:T(8,128)(2,1)S(1)}, bf16[128,2304]{1,0:T(8,128)(2,1)S(1)}) custom-call(bf16[512,896]{1,0:T(8,128)(2,1)S(1)} %shard_map.73.refs_0_.refs_4_, bf16[512,896]{1,0:T(8,128)(2,1)S(1)} %collective-permute-done.2.refs_1_, bf16[896,4096]{1,0:T(8,128)(2,1)S(1)} %bitcast.8, ...), custom_call_target="tpu_custom_call" | custom-call | flops 4227858432 | tf_op jit(solution)/shard_map/pallas_call | solution.py:38
  83.0 3.0 %collective-permute-start.9 = (bf16[128,2304]{1,0:T(8,128)(2,1)S(1)}, bf16[128,2304]{1,0:T(8,128)(2,1)S(1)}, u32[]{:S(2)}, u32[]{:S(2)}) collective-permute-start(bf16[128,2304]{1,0:T(8,128)(2,1)S(1)} %shard_map.76.refs_2_), channel_id=1, source_target_pairs={{0,4},{1,5},{2,6},{3,7},{4,8},{5,9},{6,10},{7,11},{8,12},{9,13},{1... | collective-permute-start | bytes 1769480 | tf_op jit(solution)/shard_map/ppermute | solution.py:27
  86.7 1.3 shard_map.79.refs_0_.refs_4_
  88.0 4.5 %shard_map.80 = (bf16[128,1792]{1,0:T(8,128)(2,1)S(1)}, bf16[128,1792]{1,0:T(8,128)(2,1)S(1)}, bf16[128,2304]{1,0:T(8,128)(2,1)S(1)}, bf16[128,2304]{1,0:T(8,128)(2,1)S(1)}) custom-call(bf16[256,896]{1,0:T(8,128)(2,1)S(1)} %shard_map.79.refs_0_.refs_4_, bf16[256,896]{1,0:T(8,128)(2,1)S(1)} %collective-permute-done.6.refs_1_, bf16[896,4096]{1,0:T(8,128)(2,1)S(1)} %bitcast.8, ...), custom_call_target="tpu_custom_call" | custom-call | flops 3758096384 | tf_op jit(solution)/shard_map/pallas_call | solution.py:38
  92.5 6.7 %collective-permute-done.9.refs_5_.refs_1_ = bf16[128,2304]{1,0:T(8,128)(2,1)S(1)} collective-permute-done((bf16[128,2304]{1,0:T(8,128)(2,1)S(1)}, bf16[128,2304]{1,0:T(8,128)(2,1)S(1)}, u32[]{:S(2)}, u32[]{:S(2)}) %collective-permute-start.9) | collective-permute-done | bytes 589856 | tf_op jit(solution)/shard_map/ppermute | solution.py:27
  99.4 3.3 %collective-permute-done.11.refs_5_.refs_2_ = bf16[128,2304]{1,0:T(8,128)(2,1)S(1)} collective-permute-done((bf16[128,2304]{1,0:T(8,128)(2,1)S(1)}, bf16[128,2304]{1,0:T(8,128)(2,1)S(1)}, u32[]{:S(2)}, u32[]{:S(2)}) %collective-permute-start.11) | collective-permute-done | bytes 589856 | tf_op jit(solution)/shard_map/ppermute | solution.py:27
  102.9 3.2 %collective-permute-start.10 = (bf16[128,3072]{1,0:T(8,128)(2,1)S(1)}, bf16[128,3072]{1,0:T(8,128)(2,1)S(1)}, u32[]{:S(2)}, u32[]{:S(2)}) collective-permute-start(bf16[128,3072]{1,0:T(8,128)(2,1)S(1)} %shard_map.81.refs_4_), channel_id=1, source_target_pairs={{0,4},{1,5},{2,6},{3,7},{4,8},{5,9},{6,10},{7,11},{8,12},{9,13},{1... | collective-permute-start | bytes 2359304 | tf_op jit(solution)/shard_map/ppermute | solution.py:27
  107.1 1.4 collective-permute-start.7
  109.1 13.1 %collective-permute-done.10.refs_2_.refs_6_ = bf16[128,3072]{1,0:T(8,128)(2,1)S(1)} collective-permute-done((bf16[128,3072]{1,0:T(8,128)(2,1)S(1)}, bf16[128,3072]{1,0:T(8,128)(2,1)S(1)}, u32[]{:S(2)}, u32[]{:S(2)}) %collective-permute-start.10) | collective-permute-done | bytes 786464 | tf_op jit(solution)/shard_map/ppermute | solution.py:27
  122.3 3.8 %collective-permute-start.12 = (bf16[128,1792]{1,0:T(8,128)(2,1)S(1)}, bf16[128,1792]{1,0:T(8,128)(2,1)S(1)}, u32[]{:S(2)}, u32[]{:S(2)}) collective-permute-start(bf16[128,1792]{1,0:T(8,128)(2,1)S(1)} %shard_map.84.refs_3_), channel_id=1, source_target_pairs={{0,4},{1,5},{2,6},{3,7},{4,8},{5,9},{6,10},{7,11},{8,12},{9,13},{1... | collective-permute-start | bytes 1376264 | tf_op jit(solution)/shard_map/ppermute | solution.py:27
  126.3 4.6 %collective-permute-done.7.refs_1_ = bf16[128,1792]{1,0:T(8,128)(2,1)S(1)} collective-permute-done((bf16[128,1792]{1,0:T(8,128)(2,1)S(1)}, bf16[128,1792]{1,0:T(8,128)(2,1)S(1)}, u32[]{:S(2)}, u32[]{:S(2)}) %collective-permute-start.7) | collective-permute-done | bytes 458784 | tf_op jit(solution)/shard_map/ppermute | solution.py:27
  130.9 3.2 %collective-permute-done.12.refs_2_ = bf16[128,1792]{1,0:T(8,128)(2,1)S(1)} collective-permute-done((bf16[128,1792]{1,0:T(8,128)(2,1)S(1)}, bf16[128,1792]{1,0:T(8,128)(2,1)S(1)}, u32[]{:S(2)}, u32[]{:S(2)}) %collective-permute-start.12) | collective-permute-done | bytes 458784 | tf_op jit(solution)/shard_map/ppermute | solution.py:27
  134.1 3.6 %collective-permute-done.14.refs_3_ = bf16[128,1792]{1,0:T(8,128)(2,1)S(1)} collective-permute-done((bf16[128,1792]{1,0:T(8,128)(2,1)S(1)}, bf16[128,1792]{1,0:T(8,128)(2,1)S(1)}, u32[]{:S(2)}, u32[]{:S(2)}) %collective-permute-start.14) | collective-permute-done | bytes 458784 | tf_op jit(solution)/shard_map/ppermute | solution.py:27
  137.7 1.8 %shard_map.86 = (bf16[128,4096]{1,0:T(8,128)(2,1)}, f32[1,128]{1,0:T(1,128)}) custom-call(bf16[128,1792]{1,0:T(8,128)(2,1)S(1)} %get-tuple-element.35.refs_0_, bf16[128,1792]{1,0:T(8,128)(2,1)S(1)} %collective-permute-done.7.refs_1_, bf16[128,1792]{1,0:T(8,128)(2,1)S(1)} %collective-permute-done.12.refs_2_, ...), custom_call_target="tpu_custom_call" | custom-call | flops 5709824 | bytes 5709824 | tf_op jit(solution)/shard_map/pallas_call | solution.py:38
  (49 shorter events, 7.7 us)
Async XLA Ops:
  0.6 53.5 %collective-permute-start = (bf16[896,4096]{1,0:T(8,128)(2,1)}, bf16[896,4096]{1,0:T(8,128)(2,1)}, u32[]{:S(2)}, u32[]{:S(2)}) collective-permute-start(bf16[896,4096]{1,0:T(8,128)(2,1)} %refs_2_.9), channel_id=1, source_target_pairs={{0,1},{1,0},{2,3},{3,2},{4,5},{5,4},{6,7},{7,6},{8,9},{9,8},{10,11... | collective-permute-start | bytes 22020104 | tf_op jit(solution)/shard_map/ppermute | solution.py:27
  4.6 6.3 %copy-start.2 = (s32[2048]{0:T(1024)S(1)}, s32[2048]{0:T(1024)}, u32[]{:S(2)}) copy-start(s32[2048]{0:T(1024)} %param.8) | copy-start | bytes 24580
  4.6 49.5 %all-to-all-start = ((bf16[16,128,896]{2,1,0:T(8,128)(2,1)}), bf16[16,128,896]{2,1,0:T(8,128)(2,1)}, u32[]{:S(2)}, u32[]{:S(2)}) async-start(bf16[16,128,896]{2,1,0:T(8,128)(2,1)} %bitcast.9), calls=%async_computation | async-start | bytes 7340032 | tf_op jit(solution)/shard_map/all_to_all | solution.py:266
  54.1 7.4 %slice-start = ((s8[7340032]{0:T(1024)(128)(4,1)}), s8[4194304]{0:T(1024)(128)(4,1)S(1)}, s32[]{:S(2)}) async-start(s8[7340032]{0:T(1024)(128)(4,1)} %bitcast.7), calls=%async_computation.1 | async-start | bytes 8388608
  57.3 4.2 %collective-permute-start.1 = (bf16[256,896]{1,0:T(8,128)(2,1)S(1)}, bf16[256,896]{1,0:T(8,128)(2,1)S(1)}, u32[]{:S(2)}, u32[]{:S(2)}) collective-permute-start(bf16[256,896]{1,0:T(8,128)(2,1)S(1)} %get-tuple-element.25.refs_0_), channel_id=1, source_target_pairs={{0,1},{1,0},{2,3},{3,2},{4,5},{5,4},{6,7},{7,6},{8,9},{9,8},{10,11... | collective-permute-start | bytes 1376264 | tf_op jit(solution)/shard_map/ppermute | solution.py:27
  57.4 4.1 %slice-start.1 = ((s8[7340032]{0:T(1024)(128)(4,1)}), s8[3145728]{0:T(1024)(128)(4,1)S(1)}, s32[]{:S(2)}) async-start(s8[7340032]{0:T(1024)(128)(4,1)} %bitcast.7), calls=%async_computation.2 | async-start | bytes 6291456
  60.9 10.2 %collective-permute-start.2 = (bf16[512,896]{1,0:T(8,128)(2,1)S(1)}, bf16[512,896]{1,0:T(8,128)(2,1)S(1)}, u32[]{:S(2)}, u32[]{:S(2)}) collective-permute-start(bf16[512,896]{1,0:T(8,128)(2,1)S(1)} %get-tuple-element.30), channel_id=1, source_target_pairs={{0,1},{1,0},{2,3},{3,2},{4,5},{5,4},{6,7},{7,6},{8,9},{9,8},{10,11... | collective-permute-start | bytes 2752520 | tf_op jit(solution)/shard_map/ppermute | solution.py:27
  64.1 17.1 %collective-permute-start.4 = (bf16[256,1280]{1,0:T(8,128)(2,1)S(1)}, bf16[256,1280]{1,0:T(8,128)(2,1)S(1)}, u32[]{:S(2)}, u32[]{:S(2)}) collective-permute-start(bf16[256,1280]{1,0:T(8,128)(2,1)S(1)} %get-tuple-element.28.refs_4_), channel_id=1, source_target_pairs={{0,4},{1,5},{2,6},{3,7},{4,8},{5,9},{6,10},{7,11},{8,12},{9,13},{1... | collective-permute-start | bytes 1966088 | tf_op jit(solution)/shard_map/ppermute | solution.py:27
  66.0 15.4 %collective-permute-start.3 = (bf16[256,1024]{1,0:T(8,128)(2,1)S(1)}, bf16[256,1024]{1,0:T(8,128)(2,1)S(1)}, u32[]{:S(2)}, u32[]{:S(2)}) collective-permute-start(bf16[256,1024]{1,0:T(8,128)(2,1)S(1)} %get-tuple-element.33), channel_id=1, source_target_pairs={{0,12},{1,13},{2,14},{3,15},{4,0},{5,1},{6,2},{7,3},{8,4},{9,5},{1... | collective-permute-start | bytes 1572872 | tf_op jit(solution)/shard_map/ppermute | solution.py:27
  68.3 13.1 %collective-permute-start.5 = (bf16[128,1792]{1,0:T(8,128)(2,1)S(1)}, bf16[128,1792]{1,0:T(8,128)(2,1)S(1)}, u32[]{:S(2)}, u32[]{:S(2)}) collective-permute-start(bf16[128,1792]{1,0:T(8,128)(2,1)S(1)} %get-tuple-element.29.refs_2_), channel_id=1, source_target_pairs={{0,2},{1,3},{2,0},{3,1},{4,6},{5,7},{6,4},{7,5},{8,10},{9,11},{10,... | collective-permute-start | bytes 1376264 | tf_op jit(solution)/shard_map/ppermute | solution.py:27
  82.7 5.3 %collective-permute-start.6 = (bf16[256,896]{1,0:T(8,128)(2,1)S(1)}, bf16[256,896]{1,0:T(8,128)(2,1)S(1)}, u32[]{:S(2)}, u32[]{:S(2)}) collective-permute-start(bf16[256,896]{1,0:T(8,128)(2,1)S(1)} %shard_map.78.refs_2_), channel_id=1, source_target_pairs={{0,1},{1,0},{2,3},{3,2},{4,5},{5,4},{6,7},{7,6},{8,9},{9,8},{10,11... | collective-permute-start | bytes 1376264 | tf_op jit(solution)/shard_map/ppermute | solution.py:27
  83.0 16.2 %collective-permute-start.9 = (bf16[128,2304]{1,0:T(8,128)(2,1)S(1)}, bf16[128,2304]{1,0:T(8,128)(2,1)S(1)}, u32[]{:S(2)}, u32[]{:S(2)}) collective-permute-start(bf16[128,2304]{1,0:T(8,128)(2,1)S(1)} %shard_map.76.refs_2_), channel_id=1, source_target_pairs={{0,4},{1,5},{2,6},{3,7},{4,8},{5,9},{6,10},{7,11},{8,12},{9,13},{1... | collective-permute-start | bytes 1769480 | tf_op jit(solution)/shard_map/ppermute | solution.py:27
  86.1 16.6 %collective-permute-start.11 = (bf16[128,2304]{1,0:T(8,128)(2,1)S(1)}, bf16[128,2304]{1,0:T(8,128)(2,1)S(1)}, u32[]{:S(2)}, u32[]{:S(2)}) collective-permute-start(bf16[128,2304]{1,0:T(8,128)(2,1)S(1)} %shard_map.77.refs_2_), channel_id=1, source_target_pairs={{0,12},{1,13},{2,14},{3,15},{4,0},{5,1},{6,2},{7,3},{8,4},{9,5},{1... | collective-permute-start | bytes 1769480 | tf_op jit(solution)/shard_map/ppermute | solution.py:27
  86.1 23.0 %collective-permute-start.8 = (bf16[256,1792]{1,0:T(8,128)(2,1)S(1)}, bf16[256,1792]{1,0:T(8,128)(2,1)S(1)}, u32[]{:S(2)}, u32[]{:S(2)}) collective-permute-start(bf16[256,1792]{1,0:T(8,128)(2,1)S(1)} %get-tuple-element.31.refs_4_), channel_id=1, source_target_pairs={{0,2},{1,3},{2,0},{3,1},{4,6},{5,7},{6,4},{7,5},{8,10},{9,11},{10,... | collective-permute-start | bytes 2752520 | tf_op jit(solution)/shard_map/ppermute | solution.py:27
  102.8 23.2 %collective-permute-start.13 = (bf16[128,3328]{1,0:T(8,128)(2,1)S(1)}, bf16[128,3328]{1,0:T(8,128)(2,1)S(1)}, u32[]{:S(2)}, u32[]{:S(2)}) collective-permute-start(bf16[128,3328]{1,0:T(8,128)(2,1)S(1)} %shard_map.82.refs_3_), channel_id=1, source_target_pairs={{0,12},{1,13},{2,14},{3,15},{4,0},{5,1},{6,2},{7,3},{8,4},{9,5},{1... | collective-permute-start | bytes 2555912 | tf_op jit(solution)/shard_map/ppermute | solution.py:27
  102.9 19.2 %collective-permute-start.10 = (bf16[128,3072]{1,0:T(8,128)(2,1)S(1)}, bf16[128,3072]{1,0:T(8,128)(2,1)S(1)}, u32[]{:S(2)}, u32[]{:S(2)}) collective-permute-start(bf16[128,3072]{1,0:T(8,128)(2,1)S(1)} %shard_map.81.refs_4_), channel_id=1, source_target_pairs={{0,4},{1,5},{2,6},{3,7},{4,8},{5,9},{6,10},{7,11},{8,12},{9,13},{1... | collective-permute-start | bytes 2359304 | tf_op jit(solution)/shard_map/ppermute | solution.py:27
  106.3 19.9 %copy-start.1 = (bf16[4096]{0:T(1024)(128)(2,1)S(1)}, bf16[4096]{0:T(1024)(128)(2,1)}, u32[]{:S(2)}) copy-start(bf16[4096]{0:T(1024)(128)(2,1)} %param.9) | copy-start | bytes 24580
  106.3 31.4 %copy-start = (bf16[128,4096]{1,0:T(8,128)(2,1)S(1)}, bf16[128,4096]{1,0:T(8,128)(2,1)}, u32[]{:S(2)}) copy-start(bf16[128,4096]{1,0:T(8,128)(2,1)} %refs_8_.1) | copy-start | bytes 3145732
  106.3 24.6 %collective-permute-start.15 = (bf16[128,2304]{1,0:T(8,128)(2,1)S(1)}, bf16[128,2304]{1,0:T(8,128)(2,1)S(1)}, u32[]{:S(2)}, u32[]{:S(2)}) collective-permute-start(bf16[128,2304]{1,0:T(8,128)(2,1)S(1)} %shard_map.83.refs_3_), channel_id=1, source_target_pairs={{0,2},{1,3},{2,0},{3,1},{4,6},{5,7},{6,4},{7,5},{8,10},{9,11},{10,... | collective-permute-start | bytes 1769480 | tf_op jit(solution)/shard_map/ppermute | solution.py:27
  107.1 23.9 %collective-permute-start.7 = (bf16[128,1792]{1,0:T(8,128)(2,1)S(1)}, bf16[128,1792]{1,0:T(8,128)(2,1)S(1)}, u32[]{:S(2)}, u32[]{:S(2)}) collective-permute-start(bf16[128,1792]{1,0:T(8,128)(2,1)S(1)} %get-tuple-element.36.refs_4_), channel_id=1, source_target_pairs={{0,2},{1,3},{2,0},{3,1},{4,6},{5,7},{6,4},{7,5},{8,10},{9,11},{10,... | collective-permute-start | bytes 1376264 | tf_op jit(solution)/shard_map/ppermute | solution.py:27
  122.3 11.8 %collective-permute-start.12 = (bf16[128,1792]{1,0:T(8,128)(2,1)S(1)}, bf16[128,1792]{1,0:T(8,128)(2,1)S(1)}, u32[]{:S(2)}, u32[]{:S(2)}) collective-permute-start(bf16[128,1792]{1,0:T(8,128)(2,1)S(1)} %shard_map.84.refs_3_), channel_id=1, source_target_pairs={{0,4},{1,5},{2,6},{3,7},{4,8},{5,9},{6,10},{7,11},{8,12},{9,13},{1... | collective-permute-start | bytes 1376264 | tf_op jit(solution)/shard_map/ppermute | solution.py:27
  126.2 11.6 %collective-permute-start.14 = (bf16[128,1792]{1,0:T(8,128)(2,1)S(1)}, bf16[128,1792]{1,0:T(8,128)(2,1)S(1)}, u32[]{:S(2)}, u32[]{:S(2)}) collective-permute-start(bf16[128,1792]{1,0:T(8,128)(2,1)S(1)} %shard_map.85), channel_id=1, source_target_pairs={{0,12},{1,13},{2,14},{3,15},{4,0},{5,1},{6,2},{7,3},{8,4},{9,5},{1... | collective-permute-start | bytes 1376264 | tf_op jit(solution)/shard_map/ppermute | solution.py:27

commit v3 on v2

--- a/solution.py
+++ b/solution.py
@@ -44,7 +44,7 @@
         scratch_shapes=scratch,
         compiler_params=pltpu.CompilerParams(vmem_limit_bytes=limit * MIB),
         cost_estimate=pl.CostEstimate(
-            flops=flops or n_bytes, bytes_accessed=0 if flops else n_bytes, transcendentals=0
+            flops=(flops or n_bytes) // 5, bytes_accessed=0, transcendentals=0
         ),
     )(*args, *after)
 
@@ -123,7 +123,7 @@
         scratch_shapes=[pltpu.SemaphoreType.DMA((parts,))],
         compiler_params=pltpu.CompilerParams(vmem_limit_bytes=24 * MIB),
         cost_estimate=pl.CostEstimate(
-            flops=2 * 256 * m * k, bytes_accessed=0, transcendentals=0
+            flops=2 * 256 * m * k // 5, bytes_accessed=0, transcendentals=0
         ),
     )(order, rows, *after)
 
@@ -136,39 +136,38 @@
     )
 
 
-def second_gather_kernel(first, second, order_ref, rows_ref, w_ref, w_out_ref, *refs):
-    first_ref, second_ref, sem = refs
+def second_gather_kernel(first, order_ref, rows_ref, w_ref, w_out_ref, out_ref, sem):
     copy = pltpu.make_async_copy(w_ref, w_out_ref, sem)
     copy.start()
-    gather_kernel(first, order_ref, rows_ref, first_ref)
-    gather_kernel(second, order_ref, rows_ref, second_ref)
+    gather_kernel(first, order_ref, rows_ref, out_ref)
     copy.wait()
 
 
-def second_gather(order, rows, first, second, w, after):
+def second_gather(order, rows, first, w, after):
     m, k = rows.shape
     n = len(after)
-    kernel = functools.partial(second_gather_kernel, first, second)
+    kernel = functools.partial(second_gather_kernel, first)
     return pl.pallas_call(
         lambda order_ref, rows_ref, w_ref, *refs: kernel(order_ref, rows_ref, w_ref, *refs[n:]),
-        out_shape=[bf(*w.shape), bf(256, k), bf(512, k)],
+        out_shape=[bf(*w.shape), bf(256, k)],
         in_specs=[pl.BlockSpec(memory_space=pltpu.VMEM)] * 2
         + [pl.BlockSpec(memory_space=pl.ANY)] * (n + 1),
         scratch_shapes=[pltpu.SemaphoreType.DMA],
         compiler_params=pltpu.CompilerParams(vmem_limit_bytes=24 * MIB),
         cost_estimate=pl.CostEstimate(
-            flops=2 * 768 * m * k, bytes_accessed=0, transcendentals=0
+            flops=2 * 256 * m * k // 5, bytes_accessed=0, transcendentals=0
         ),
     )(order, rows, w, *after)
 
 
-def term_kernel(ranges, own_ref, sib_ref, w_own_ref, w_sib_ref, *outs):
+def term_kernel(ranges, start, own_ref, sib_ref, w_own_ref, w_sib_ref, *outs):
+    rows = slice(start, start + 256)
     for first, count, groups in ranges:
         for j in range(count):
             tile = slice((first + j) * TILE, (first + j + 1) * TILE)
             here = slice(j * TILE, (j + 1) * TILE)
-            total = jnp.dot(own_ref[...], w_own_ref[:, tile], preferred_element_type=jnp.float32)
-            total += jnp.dot(sib_ref[...], w_sib_ref[:, tile], preferred_element_type=jnp.float32)
+            total = jnp.dot(own_ref[rows], w_own_ref[:, tile], preferred_element_type=jnp.float32)
+            total += jnp.dot(sib_ref[rows], w_sib_ref[:, tile], preferred_element_type=jnp.float32)
             total = total.astype(jnp.bfloat16)
             for out, blocks in zip(outs, groups):
                 for at, block in enumerate(blocks):
@@ -176,63 +175,76 @@
         outs = outs[len(groups) :]
 
 
-def term(own, sib, w_own, w_sib, ranges, after):
+def term(own, sib, start, w_own, w_sib, ranges, after):
     k = w_own.shape[0]
     shapes = [bf(128 * len(g), count * TILE) for _, count, groups in ranges for g in groups]
     return whole_call(
-        functools.partial(term_kernel, ranges), shapes, own, sib, w_own, w_sib,
-        flops=4 * own.shape[0] * k * TILE * sum(r[1] for r in ranges), after=after,
+        functools.partial(term_kernel, ranges, start), shapes, own, sib, w_own, w_sib,
+        flops=4 * 256 * k * TILE * sum(r[1] for r in ranges), after=after,
     )
 
 
 def left_kernel(row, base_ref, come_ref, out_ref):
     rows = slice(row, row + 128)
     out_ref[:, :WB1] = (f32(base_ref, columns=slice(WB1)) + f32(come_ref, rows)).astype(jnp.bfloat16)
-    out_ref[:, WB1:WB] = base_ref[:, WB1:]
+    out_ref[:, WB1:] = base_ref[:, WB1:]
 
 
 def right_kernel(row, base_ref, come_ref, out_ref):
     rows = slice(row, row + 128)
     out_ref[:, :WB1] = base_ref[:, :WB1]
-    out_ref[:, WB1:WB] = (
-        f32(base_ref, columns=slice(WB1, WB)) + f32(come_ref, rows)
-    ).astype(jnp.bfloat16)
-
-
-def left_more_kernel(base_ref, come_ref, a_ref, x_ref, out_ref):
-    left_kernel(128, base_ref, come_ref, out_ref)
-    c = slice(WA1)
-    out_ref[:, WB:] = (f32(a_ref, columns=c) + f32(x_ref, columns=c)).astype(jnp.bfloat16)
-
-
-def right_more_kernel(base_ref, come_ref, a_ref, x_ref, out_ref):
-    right_kernel(128, base_ref, come_ref, out_ref)
-    c = slice(WA1, WA)
-    out_ref[:, WB:] = (f32(a_ref, columns=c) + f32(x_ref, columns=c)).astype(jnp.bfloat16)
-
-
-def to_right_kernel(a_ref, x_ref, come_ref, out_ref):
-    total = f32(a_ref) + f32(x_ref, slice(0, 128))
-    out_ref[:, :WA1] = (total[:, :WA1] + f32(come_ref, columns=slice(WB, None))).astype(jnp.bfloat16)
-    out_ref[:, WA1:] = total[:, WA1:].astype(jnp.bfloat16)
-
-
-def to_left_kernel(a_ref, x_ref, come_ref, out_ref):
-    total = f32(a_ref) + f32(x_ref, slice(128, 256))
-    out_ref[:, :WA1] = total[:, :WA1].astype(jnp.bfloat16)
-    out_ref[:, WA1:] = (total[:, WA1:] + f32(come_ref, columns=slice(WB, None))).astype(jnp.bfloat16)
-
-
-def sum3_kernel(a_ref, b_ref, c_ref, out_ref):
-    out_ref[...] = (f32(a_ref) + f32(b_ref) + f32(c_ref)).astype(jnp.bfloat16)
-
-
-def last_kernel(a0, a1, a2, a3, b0, b1, b2, b3, residual_ref, head_ref, out_ref, score_ref):
+    out_ref[:, WB1:] = (f32(base_ref, columns=slice(WB1, WB)) + f32(come_ref, rows)).astype(
+        jnp.bfloat16
+    )
+
+
+def both_kernel(row, left_ref, y1_ref, right_ref, y3_ref, left_out, right_out):
+    left_kernel(row, left_ref, y1_ref, left_out)
+    right_kernel(row, right_ref, y3_ref, right_out)
+
+
+def widen_kernel(left_ref, right_ref, a_ref, x_ref, left_out, right_out):
+    left_out[:, :WB] = left_ref[...]
+    right_out[:, :WB] = right_ref[...]
+    total = f32(a_ref) + f32(x_ref)
+    left_out[:, WB:] = total[:, :WA1].astype(jnp.bfloat16)
+    right_out[:, WB:] = total[:, WA1:].astype(jnp.bfloat16)
+
+
+def sums_kernel(a_ref, b_ref, x_ref, a_out, b_out):
+    a_out[...] = f32(a_ref) + f32(x_ref, slice(0, 128))
+    b_out[...] = f32(b_ref) + f32(x_ref, slice(128, 256))
+
+
+def to_right_kernel(total_ref, come_ref, out_ref):
+    come = f32(come_ref, columns=slice(WB, None))
+    out_ref[:, :WA1] = (total_ref[:, :WA1] + come).astype(jnp.bfloat16)
+    out_ref[:, WA1:] = total_ref[:, WA1:].astype(jnp.bfloat16)
+
+
+def to_left_kernel(total_ref, come_ref, out_ref):
+    come = f32(come_ref, columns=slice(WB, None))
+    out_ref[:, :WA1] = total_ref[:, :WA1].astype(jnp.bfloat16)
+    out_ref[:, WA1:] = (total_ref[:, WA1:] + come).astype(jnp.bfloat16)
+
+
+def across_kernel(a_ref, b_ref, left_ref, right_ref, out_ref):
     c = slice(WB)
-    down_a = f32(a0) + f32(a1) + f32(a2) + f32(a3)
-    down_b = f32(b0) + f32(b1) + f32(b2, columns=c) + f32(b3, columns=c)
-    out_a = (f32(residual_ref, columns=slice(WA)) + down_a).astype(jnp.bfloat16)
-    out_b = (f32(residual_ref, columns=slice(WA, None)) + down_b).astype(jnp.bfloat16)
+    total = f32(b_ref) + f32(left_ref, columns=c) + f32(right_ref, columns=c)
+    out_ref[:, :WA] = a_ref[...]
+    out_ref[:, WA:] = total.astype(jnp.bfloat16)
+
+
+def mine_kernel(a_ref, b_ref, left_ref, right_ref, residual_ref, out_ref):
+    out_ref[:, :WA] = f32(residual_ref, columns=slice(WA)) + f32(a_ref)
+    b = f32(b_ref) + f32(left_ref) + f32(right_ref)
+    out_ref[:, WA:] = f32(residual_ref, columns=slice(WA, None)) + b
+
+
+def last_kernel(mine_ref, across_ref, left_ref, right_ref, head_ref, out_ref, score_ref):
+    out_a = f32(across_ref, columns=slice(WA)) + f32(left_ref) + f32(right_ref)
+    out_a = (mine_ref[:, :WA] + out_a).astype(jnp.bfloat16)
+    out_b = (mine_ref[:, WA:] + f32(across_ref, columns=slice(WA, None))).astype(jnp.bfloat16)
     out_ref[:, :WA] = out_a
     out_ref[:, WA:] = out_b
     wide_a, wide_b = out_a.astype(jnp.float32), out_b.astype(jnp.float32)
@@ -271,53 +283,64 @@
     order = lax.dynamic_slice_in_dim(jnp.concatenate([order, order], axis=0), y, NY, 0)
     order = jnp.where(x == 0, order[:, ::-1], order)
     order = jnp.where(core == 0, order[:, :, ::-1], order)
-    order = jnp.stack([order[2], order[1], order[3], order[0]])
-    order = order.transpose(2, 0, 1, 3).reshape(-1, 1)
+    places = [(2, 0), (2, 1), (1, 0), (3, 0), (1, 1), (3, 1), (0, 0), (0, 1)]
+    order = jnp.stack([order[p] for p in places], axis=1).reshape(-1, 1)
     own = order.shape[0] // 2
 
     tb1, tb2 = A_TILES, A_TILES + B1_TILES
-    b_only = ((tb1, B1_TILES, ((0, 1),)), (tb2, B2_TILES, ((0, 1),)))
+    b_halves = ((tb1, B1_TILES, ((0, 1),)), (tb2, B2_TILES, ((0, 1),)))
+    a_stacked = ((0, A_TILES, ((0, 1),)),)
     a_only = ((0, A_TILES, ((0,), (1,))),)
-    two_a = ((0, A_TILES, ((0, 2), (1,), (3,))),)
-    two_b = ((tb1, B1_TILES + B2_TILES, ((0,), (2,), (1,), (3,))),)
     both = ((0, A_TILES, ((0,), (1,))), (tb1, B1_TILES + B2_TILES, ((0,), (1,))))
-
+    b_only = both[1:]
+
+    held_sib = hop(held, 0, 0, 1)
     held, give2 = first_gather(order, held, 0, (w_sib,))
     sib2 = hop(give2, 0, 0, 1)
-    w_sib, own2, give13 = second_gather(order, held, own, 256, w_sib, (give2,))
-    sib13 = hop(give13, 0, 0, 1)
-    b1, b2 = term(own2, sib2, w_own, w_sib, b_only, ())
+    w_sib, own2 = second_gather(order, held, own, w_sib, (give2,))
+    b1, b2 = term(own2, sib2, 0, w_own, w_sib, b_halves, ())
     y1 = hop(b1, 1, 0, 0)
     y3 = hop(b2, 3, 0, 0)
-    ax2, ao2 = term(own2, sib2, w_own, w_sib, a_only, (b1,))
+    ax2, ao2 = term(own2, sib2, 0, w_own, w_sib, a_only, (b1,))
     x2 = hop(ax2, 0, 1, 0)
-    own13 = gather(order, held, own + 256, 512, (ax2,))
-    ax13, ao1, ao3 = term(own13, sib13, w_own, w_sib, two_a, (own13,))
+    own13x = gather(order, held, own + 256, 256, (ax2,))
+    held_sib, sib13x = first_gather(order, held_sib, own + 256, (own13x,))
+    ax13 = term(own13x, sib13x, 0, w_own, w_sib, a_stacked, ())[0]
     x13 = hop(ax13, 0, 1, 0)
-    bx1, bx3, bo1, bo3 = term(own13, sib13, w_own, w_sib, two_b, (ax13,))
-    tv1 = whole_call(functools.partial(left_kernel, 0), bf(128, WB), bx1, y1)
+    bx1, bx3 = term(own13x, sib13x, 0, w_own, w_sib, b_only, (ax13,))
+    own_r = gather(order, held, own + 512, 512, (bx1,))
+    t1, t3 = whole_call(
+        functools.partial(both_kernel, 0), [bf(128, WB)] * 2, bx1, y1, bx3, y3, after=(own_r,)
+    )
+    tv1, tv3 = whole_call(
+        widen_kernel, [bf(128, WB + WA1), bf(128, WB + WA - WA1)], t1, t3, ao2, x2
+    )
     v1 = hop(tv1, 1, 0, 0)
-    tv3 = whole_call(functools.partial(right_kernel, 0), bf(128, WB), bx3, y3, after=(tv1,))
     v3 = hop(tv3, 3, 0, 0)
-    give0 = gather(order, held, 768, 256, (tv3, x2))
-    sib0 = hop(give0, 0, 0, 1)
-    own0 = gather(order, held, own + 768, 256, (give0,))
-    ax0, ao0, bx0, bo0 = term(own0, sib0, w_own, w_sib, both, (own0,))
-    x0 = hop(ax0, 0, 1, 0)
-    tu1 = whole_call(left_more_kernel, bf(128, WB + WA1), bo1, y1, ao2, x2, after=(ax0, v1))
+    sib_r = gather(order, held_sib, own + 512, 512, (tv3,))
+    ao1, ao3, bo1, bo3 = term(own_r, sib_r, 0, w_own, w_sib, both, ())
+    ax0, ao0, bx0, bo0 = term(own_r, sib_r, 256, w_own, w_sib, both, (ao1,))
+    tu1, tu3 = whole_call(
+        functools.partial(both_kernel, 128), [bf(128, WB)] * 2, bo1, y1, bo3, y3, after=(ax0,)
+    )
     u1 = hop(tu1, 1, 0, 0)
-    tu3 = whole_call(right_more_kernel, bf(128, WB + WA - WA1), bo3, y3, ao2, x2, after=(tu1, v3))
     u3 = hop(tu3, 3, 0, 0)
-    tg = whole_call(sum3_kernel, bf(128, WB), bx0, v1, v3, after=(tu3,))
-    g = hop(tg, 0, 1, 0)
-    tz1 = whole_call(to_right_kernel, bf(128, WA), ao1, x13, u1, after=(tg,))
+    wide = jax.ShapeDtypeStruct((128, WA), jnp.float32)
+    s1, s3 = whole_call(sums_kernel, [wide] * 2, ao1, ao3, x13, after=(tu1,))
+    across = whole_call(across_kernel, bf(128, d), ax0, bx0, v1, v3, after=(s1,))
+    g = hop(across, 0, 1, 0)
+    tz1 = whole_call(to_right_kernel, bf(128, WA), s1, v1, after=(across,))
     z1 = hop(tz1, 1, 0, 0)
-    tz3 = whole_call(to_left_kernel, bf(128, WA), ao3, x13, u3, after=(tz1,))
+    tz3 = whole_call(to_left_kernel, bf(128, WA), s3, v3, after=(tz1,))
     z3 = hop(tz3, 3, 0, 0)
+    mine = whole_call(
+        mine_kernel, jax.ShapeDtypeStruct((128, d), jnp.float32), ao0, bo0, u1, u3, residual,
+        after=(tz3,), flops=200 * 10**9,
+    )
     layer_out, scores = whole_call(
         last_kernel,
         [bf(rows, d), jax.ShapeDtypeStruct((1, rows), jnp.float32)],
-        ao0, x0, z1, z3, bo0, g, u1, u3, residual, value_head.reshape(1, d),
+        mine, g, z1, z3, value_head.reshape(1, d),
     )
     return (layer_out, scores.reshape(rows))
 

time: 140 us -> 132 us (0.943)
  waiting for transfers between devices: 78.9 us -> 24.5 us
  blocking collectives: 0 us -> 48.6 us
  starting transfers between devices: 22.8 us -> 14.6 us
  Pallas kernels: 36.4 us -> 41 us
    all_to_all x0 -> x1, blocking collectives: none -> 48.6 us  [local(): lax.all_to_all(blocks, 'tensor', split_axis=0, concat_axis=0, tiled=True)]
    all_to_all x1 -> x0, waiting for transfers between devices: 42.7 us -> none  [local(): lax.all_to_all(blocks, 'tensor', split_axis=0, concat_axis=0, tiled=True)]
    ppermute x16 -> x14, waiting for transfers between devices: 36.2 us -> 24.5 us  [hop(): return lax.ppermute(value, 'tensor', pairs)]
    all_to_all x1 -> x0, starting transfers between devices: 6.29 us -> none  [local(): lax.all_to_all(blocks, 'tensor', split_axis=0, concat_axis=0, tiled=True)]
    pallas_call x1 -> x2, Pallas kernels: 3.22 us -> 6.29 us  [first_gather(): pl.pallas_call(lambda order_ref, rows_ref, *refs: kernel(order_ref, rows_...]
    ppermute x16 -> x14, starting transfers between devices: 16.5 us -> 14.6 us  [hop(): return lax.ppermute(value, 'tensor', pairs)]
    pallas_call x17 -> x19, Pallas kernels: 29.7 us -> 30.9 us  [whole_call(): pl.pallas_call(without_after, out_shape=out_shape, in_specs=[pl.BlockSpec...]
  transfers between devices with their start and end apart: 17 -> 14, of which waited for: 9 -> 7; matrix products, arithmetic and copies ran while one was open for 0% -> 0% of each run, Pallas kernels for 22% -> 30%
where the time goes in v3:
time: 132 us; the launch traced here: 131 us
  blocking collectives  48.6 us (37%)
  Pallas kernels  41 us (31%)
  waiting for transfers between devices  24.5 us (19%)
  starting transfers between devices  14.6 us (11%)
    all_to_all x1, blocking collectives, local(): lax.all_to_all(blocks, 'tensor', split_axis=0, concat_axis=0, tiled=True)  48.6 us
    pallas_call x19, Pallas kernels, whole_call(): pl.pallas_call(without_after, out_shape=out_shape, in_specs=[pl.BlockSpec...  30.9 us
    ppermute x14, waiting for transfers between devices, hop(): return lax.ppermute(value, 'tensor', pairs)  24.5 us
    ppermute x14, starting transfers between devices, hop(): return lax.ppermute(value, 'tensor', pairs)  14.6 us
    pallas_call x2, Pallas kernels, first_gather(): pl.pallas_call(lambda order_ref, rows_ref, *refs: kernel(order_ref, rows_...  6.29 us
    pallas_call x1, Pallas kernels, second_gather(): pl.pallas_call(lambda order_ref, rows_ref, w_ref, *refs: kernel(order_ref...  3.83 us
  transfers between devices with their start and end apart: 14, of which 7 were waited for; matrix products, arithmetic and copies ran while one was open for 0% of the time, Pallas kernels for 30%

profile of v3, /device:TPU:24, one launch (start us, length us, event | category | flops | bytes accessed | tf_op | source)
XLA Modules:
  0.0 131.1 jit_solution(1273981708454242992)
XLA Ops:
  0.7 3.8 %shard_map.68 = bf16[2048,896]{1,0:T(8,128)(2,1)} custom-call(bf16[128,14336]{1,0:T(8,128)(2,1)} %refs_0_.1), custom_call_target="tpu_custom_call" | custom-call | flops 734003 | tf_op jit(solution)/shard_map/pallas_call | solution.py:38
  4.6 48.6 %all_to_all.11 = bf16[16,128,896]{2,1,0:T(8,128)(2,1)} all-to-all(bf16[16,128,896]{2,1,0:T(8,128)(2,1)} %bitcast.29), channel_id=1, replica_groups=mesh['dp'=16,'tensor'=16] {'tensor'}, dimensions={0} | all-to-all | bytes 7340032 | tf_op jit(solution)/shard_map/all_to_all | solution.py:278
  53.7 3.2 %shard_map.69 = (bf16[2048,896]{1,0:T(8,128)(2,1)S(1)}, bf16[256,896]{1,0:T(8,128)(2,1)S(1)}) custom-call(s32[2048,1]{1,0:T(8,128)S(1)} %copy.25.order_ref.refs_0_, bf16[2048,896]{1,0:T(8,128)(2,1)} %bitcast.18.rows_ref, bf16[896,4096]{1,0:T(8,128)(2,1)} %collective-permute-done.refs_0_.w_ref), custom_call_target="tpu_custom_call" | custom-call | flops 187904816 | tf_op jit(solution)/shard_map/pallas_call | solution.py:118
  57.6 3.8 %shard_map.70 = (bf16[896,4096]{1,0:T(8,128)(2,1)S(1)}, bf16[256,896]{1,0:T(8,128)(2,1)S(1)}) custom-call(s32[2048,1]{1,0:T(8,128)S(1)} %copy.25.order_ref.refs_0_, bf16[2048,896]{1,0:T(8,128)(2,1)S(1)} %get-tuple-element.32.rows_ref.refs_1_, bf16[896,4096]{1,0:T(8,128)(2,1)} %collective-permute-done.refs_0_.w_ref, ...), custom_call_target="tpu_custom_call" | custom-call | flops 187904816 | tf_op jit(solution)/shard_map/pallas_call | solution.py:150
  62.2 2.6 %shard_map.71 = (bf16[256,1280]{1,0:T(8,128)(2,1)S(1)}, bf16[256,1024]{1,0:T(8,128)(2,1)S(1)}) custom-call(bf16[256,896]{1,0:T(8,128)(2,1)S(1)} %get-tuple-element.34.refs_0_, bf16[256,896]{1,0:T(8,128)(2,1)S(1)} %collective-permute-done.1.refs_1_, bf16[896,4096]{1,0:T(8,128)(2,1)S(1)} %bitcast.28, bf16[896,4096]{1,0:T(8,128)(2,1)S(1)} %get-tuple-element.35.refs_3_), custom_call_target="tpu_custom_call" | custom-call | flops 422785856 | tf_op jit(solution)/shard_map/pallas_call | solution.py:38
  64.8 2.5 %collective-permute-start.3 = (bf16[256,1280]{1,0:T(8,128)(2,1)S(1)}, bf16[256,1280]{1,0:T(8,128)(2,1)S(1)}, u32[]{:S(2)}, u32[]{:S(2)}) collective-permute-start(bf16[256,1280]{1,0:T(8,128)(2,1)S(1)} %get-tuple-element.36.refs_4_), channel_id=1, source_target_pairs={{0,4},{1,5},{2,6},{3,7},{4,8},{5,9},{6,10},{7,11},{8,12},{9,13},{1... | collective-permute-start | bytes 1966088 | tf_op jit(solution)/shard_map/ppermute | solution.py:27
  67.3 2.0 %shard_map.72 = (bf16[128,1792]{1,0:T(8,128)(2,1)S(1)}, bf16[128,1792]{1,0:T(8,128)(2,1)S(1)}) custom-call(bf16[256,896]{1,0:T(8,128)(2,1)S(1)} %get-tuple-element.34.refs_0_, bf16[256,896]{1,0:T(8,128)(2,1)S(1)} %collective-permute-done.1.refs_1_, bf16[896,4096]{1,0:T(8,128)(2,1)S(1)} %bitcast.28, bf16[896,4096]{1,0:T(8,128)(2,1)S(1)} %get-tuple-element.35.refs_3_, ...), custom_call_target="tpu_custom_call" | custom-call | flops 328833440 | tf_op jit(solution)/shard_map/pallas_call | solution.py:38
  71.8 3.1 %shard_map.74 = (bf16[2048,896]{1,0:T(8,128)(2,1)S(1)}, bf16[256,896]{1,0:T(8,128)(2,1)S(1)}) custom-call(s32[2048,1]{1,0:T(8,128)S(1)} %copy.25.order_ref.refs_0_, bf16[2048,896]{1,0:T(8,128)(2,1)} %collective-permute-done.2.rows_ref, bf16[256,896]{1,0:T(8,128)(2,1)S(1)} %shard_map.73.refs_0_), custom_call_target="tpu_custom_call" | custom-call | flops 187904816 | tf_op jit(solution)/shard_map/pallas_call | solution.py:118
  74.9 2.0 %shard_map.75.refs_4_ = bf16[256,1792]{1,0:T(8,128)(2,1)S(1)} custom-call(bf16[256,896]{1,0:T(8,128)(2,1)S(1)} %shard_map.73.refs_0_, bf16[256,896]{1,0:T(8,128)(2,1)S(1)} %get-tuple-element.38.refs_1_, bf16[896,4096]{1,0:T(8,128)(2,1)S(1)} %bitcast.28, bf16[896,4096]{1,0:T(8,128)(2,1)S(1)} %get-tuple-element.35.refs_3_), custom_call_target="tpu_custom_call" | custom-call | flops 328833440 | tf_op jit(solution)/shard_map/pallas_call | solution.py:38
  78.2 2.6 %shard_map.76 = (bf16[128,2304]{1,0:T(8,128)(2,1)S(1)}, bf16[128,2304]{1,0:T(8,128)(2,1)S(1)}) custom-call(bf16[256,896]{1,0:T(8,128)(2,1)S(1)} %shard_map.73.refs_0_, bf16[256,896]{1,0:T(8,128)(2,1)S(1)} %get-tuple-element.38.refs_1_, bf16[896,4096]{1,0:T(8,128)(2,1)S(1)} %bitcast.28, bf16[896,4096]{1,0:T(8,128)(2,1)S(1)} %get-tuple-element.35.refs_3_, ...), custom_call_target="tpu_custom_call" | custom-call | flops 422785856 | tf_op jit(solution)/shard_map/pallas_call | solution.py:38
  80.8 2.4 %shard_map.77.refs_4_.refs_0_ = bf16[512,896]{1,0:T(8,128)(2,1)S(1)} custom-call(s32[2048,1]{1,0:T(8,128)S(1)} %copy.25.order_ref.refs_0_, bf16[2048,896]{1,0:T(8,128)(2,1)S(1)} %copy-done.1, bf16[128,2304]{1,0:T(8,128)(2,1)S(1)} %get-tuple-element.39.refs_2_.refs_0_), custom_call_target="tpu_custom_call" | custom-call | flops 375809632 | tf_op jit(solution)/shard_map/pallas_call | solution.py:38
  83.9 3.4 %collective-permute-start.10 = (bf16[128,3072]{1,0:T(8,128)(2,1)S(1)}, bf16[128,3072]{1,0:T(8,128)(2,1)S(1)}, u32[]{:S(2)}, u32[]{:S(2)}) collective-permute-start(bf16[128,3072]{1,0:T(8,128)(2,1)S(1)} %get-tuple-element.58), channel_id=1, source_target_pairs={{0,4},{1,5},{2,6},{3,7},{4,8},{5,9},{6,10},{7,11},{8,12},{9,13},{1... | collective-permute-start | bytes 2359304 | tf_op jit(solution)/shard_map/ppermute | solution.py:27
  87.2 2.4 %shard_map.80.refs_1_ = bf16[512,896]{1,0:T(8,128)(2,1)S(1)} custom-call(s32[2048,1]{1,0:T(8,128)S(1)} %copy.25.order_ref.refs_0_, bf16[2048,896]{1,0:T(8,128)(2,1)S(1)} %copy-done.3, bf16[128,3328]{1,0:T(8,128)(2,1)S(1)} %get-tuple-element.46.refs_2_), custom_call_target="tpu_custom_call" | custom-call | flops 375809632 | tf_op jit(solution)/shard_map/pallas_call | solution.py:38
  89.6 4.5 %shard_map.81 = (bf16[128,1792]{1,0:T(8,128)(2,1)S(1)}, bf16[128,1792]{1,0:T(8,128)(2,1)S(1)}, bf16[128,2304]{1,0:T(8,128)(2,1)S(1)}, bf16[128,2304]{1,0:T(8,128)(2,1)S(1)}) custom-call(bf16[512,896]{1,0:T(8,128)(2,1)S(1)} %shard_map.77.refs_4_.refs_0_, bf16[512,896]{1,0:T(8,128)(2,1)S(1)} %shard_map.80.refs_1_, bf16[896,4096]{1,0:T(8,128)(2,1)S(1)} %bitcast.28, ...), custom_call_target="tpu_custom_call" | custom-call | flops 751619264 | tf_op jit(solution)/shard_map/pallas_call | solution.py:38
  94.1 4.5 %shard_map.82 = (bf16[128,1792]{1,0:T(8,128)(2,1)S(1)}, bf16[128,1792]{1,0:T(8,128)(2,1)S(1)}, bf16[128,2304]{1,0:T(8,128)(2,1)S(1)}, bf16[128,2304]{1,0:T(8,128)(2,1)S(1)}) custom-call(bf16[512,896]{1,0:T(8,128)(2,1)S(1)} %shard_map.77.refs_4_.refs_0_, bf16[512,896]{1,0:T(8,128)(2,1)S(1)} %shard_map.80.refs_1_, bf16[896,4096]{1,0:T(8,128)(2,1)S(1)} %bitcast.28, ...), custom_call_target="tpu_custom_call" | custom-call | flops 751619264 | tf_op jit(solution)/shard_map/pallas_call | solution.py:38
  98.8 1.8 %collective-permute-start.6 = (bf16[128,2304]{1,0:T(8,128)(2,1)S(1)}, bf16[128,2304]{1,0:T(8,128)(2,1)S(1)}, u32[]{:S(2)}, u32[]{:S(2)}) collective-permute-start(bf16[128,2304]{1,0:T(8,128)(2,1)S(1)} %get-tuple-element.53.refs_3_), channel_id=1, source_target_pairs={{0,4},{1,5},{2,6},{3,7},{4,8},{5,9},{6,10},{7,11},{8,12},{9,13},{1... | collective-permute-start | bytes 1769480 | tf_op jit(solution)/shard_map/ppermute | solution.py:27
  102.2 3.0 %collective-permute-done.10.refs_2_.refs_1_ = bf16[128,3072]{1,0:T(8,128)(2,1)S(1)} collective-permute-done((bf16[128,3072]{1,0:T(8,128)(2,1)S(1)}, bf16[128,3072]{1,0:T(8,128)(2,1)S(1)}, u32[]{:S(2)}, u32[]{:S(2)}) %collective-permute-start.10) | collective-permute-done | bytes 786464 | tf_op jit(solution)/shard_map/ppermute | solution.py:27
  105.2 1.5 %collective-permute-done.9.refs_3_.refs_1_ = bf16[128,3328]{1,0:T(8,128)(2,1)S(1)} collective-permute-done((bf16[128,3328]{1,0:T(8,128)(2,1)S(1)}, bf16[128,3328]{1,0:T(8,128)(2,1)S(1)}, u32[]{:S(2)}, u32[]{:S(2)}) %collective-permute-start.9) | collective-permute-done | bytes 852000 | tf_op jit(solution)/shard_map/ppermute | solution.py:27
  108.1 2.2 %collective-permute-start.12 = (bf16[128,1792]{1,0:T(8,128)(2,1)S(1)}, bf16[128,1792]{1,0:T(8,128)(2,1)S(1)}, u32[]{:S(2)}, u32[]{:S(2)}) collective-permute-start(bf16[128,1792]{1,0:T(8,128)(2,1)S(1)} %shard_map.86.refs_2_), channel_id=1, source_target_pairs={{0,4},{1,5},{2,6},{3,7},{4,8},{5,9},{6,10},{7,11},{8,12},{9,13},{1... | collective-permute-start | bytes 1376264 | tf_op jit(solution)/shard_map/ppermute | solution.py:27
  110.5 7.4 %collective-permute-done.6.refs_2_ = bf16[128,2304]{1,0:T(8,128)(2,1)S(1)} collective-permute-done((bf16[128,2304]{1,0:T(8,128)(2,1)S(1)}, bf16[128,2304]{1,0:T(8,128)(2,1)S(1)}, u32[]{:S(2)}, u32[]{:S(2)}) %collective-permute-start.6) | collective-permute-done | bytes 589856 | tf_op jit(solution)/shard_map/ppermute | solution.py:27
  117.9 1.5 %collective-permute-done.7.refs_3_ = bf16[128,2304]{1,0:T(8,128)(2,1)S(1)} collective-permute-done((bf16[128,2304]{1,0:T(8,128)(2,1)S(1)}, bf16[128,2304]{1,0:T(8,128)(2,1)S(1)}, u32[]{:S(2)}, u32[]{:S(2)}) %collective-permute-start.7) | collective-permute-done | bytes 589856 | tf_op jit(solution)/shard_map/ppermute | solution.py:27
  119.8 8.2 %collective-permute-done.13.refs_3_ = bf16[128,1792]{1,0:T(8,128)(2,1)S(1)} collective-permute-done((bf16[128,1792]{1,0:T(8,128)(2,1)S(1)}, bf16[128,1792]{1,0:T(8,128)(2,1)S(1)}, u32[]{:S(2)}, u32[]{:S(2)}) %collective-permute-start.13) | collective-permute-done | bytes 458784 | tf_op jit(solution)/shard_map/ppermute | solution.py:27
  127.9 1.7 %collective-permute-done.11.refs_1_ = bf16[128,4096]{1,0:T(8,128)(2,1)S(1)} collective-permute-done((bf16[128,4096]{1,0:T(8,128)(2,1)S(1)}, bf16[128,4096]{1,0:T(8,128)(2,1)S(1)}, u32[]{:S(2)}, u32[]{:S(2)}) %collective-permute-start.11) | collective-permute-done | bytes 1048608 | tf_op jit(solution)/shard_map/ppermute | solution.py:27
  129.7 1.4 %shard_map.89 = (bf16[128,4096]{1,0:T(8,128)(2,1)}, f32[1,128]{1,0:T(1,128)}) custom-call(f32[128,4096]{1,0:T(8,128)S(1)} %shard_map.88.refs_0_, bf16[128,4096]{1,0:T(8,128)(2,1)S(1)} %collective-permute-done.11.refs_1_, bf16[128,1792]{1,0:T(8,128)(2,1)S(1)} %collective-permute-done.12.refs_2_, bf16[128,1792]{1,0:T(8,128)(2,1)S(1)} %collective-permute-done.13.refs_3_, ...), custom_call_target="tpu_custom_call" | custom-call | flops 814284 | tf_op jit(solution)/shard_map/pallas_call | solution.py:38
  (54 shorter events, 9.8 us)
Async XLA Ops:
  0.6 53.1 %collective-permute-start = (bf16[896,4096]{1,0:T(8,128)(2,1)}, bf16[896,4096]{1,0:T(8,128)(2,1)}, u32[]{:S(2)}, u32[]{:S(2)}) collective-permute-start(bf16[896,4096]{1,0:T(8,128)(2,1)} %refs_2_.11), channel_id=1, source_target_pairs={{0,1},{1,0},{2,3},{3,2},{4,5},{5,4},{6,7},{7,6},{8,9},{9,8},{10,11... | collective-permute-start | bytes 22020104 | tf_op jit(solution)/shard_map/ppermute | solution.py:27
  4.5 48.7 %copy-start.6 = (s32[2048]{0:T(1024)S(1)}, s32[2048]{0:T(1024)}, u32[]{:S(2)}) copy-start(s32[2048]{0:T(1024)} %param.8) | copy-start | bytes 24580
  53.2 18.6 %collective-permute-start.2 = (bf16[2048,896]{1,0:T(8,128)(2,1)}, bf16[2048,896]{1,0:T(8,128)(2,1)}, u32[]{:S(2)}, u32[]{:S(2)}) collective-permute-start(bf16[2048,896]{1,0:T(8,128)(2,1)} %bitcast.18.rows_ref), channel_id=1, source_target_pairs={{0,1},{1,0},{2,3},{3,2},{4,5},{5,4},{6,7},{7,6},{8,9},{9,8},{10,11... | collective-permute-start | bytes 11010056 | tf_op jit(solution)/shard_map/ppermute | solution.py:27
  53.7 7.7 %slice-start = ((s8[7340032]{0:T(1024)(128)(4,1)}), s8[4194304]{0:T(1024)(128)(4,1)S(1)}, s32[]{:S(2)}) async-start(s8[7340032]{0:T(1024)(128)(4,1)} %bitcast.27), calls=%async_computation.1 | async-start | bytes 8388608
  57.0 4.4 %copy-start = (bf16[2048,896]{1,0:T(8,128)(2,1)}, bf16[2048,896]{1,0:T(8,128)(2,1)S(1)}, u32[]{:S(2)}) copy-start(bf16[2048,896]{1,0:T(8,128)(2,1)S(1)} %get-tuple-element.32.rows_ref.refs_1_) | copy-start | bytes 11010052
  57.0 4.4 %collective-permute-start.1 = (bf16[256,896]{1,0:T(8,128)(2,1)S(1)}, bf16[256,896]{1,0:T(8,128)(2,1)S(1)}, u32[]{:S(2)}, u32[]{:S(2)}) collective-permute-start(bf16[256,896]{1,0:T(8,128)(2,1)S(1)} %get-tuple-element.33.refs_0_), channel_id=1, source_target_pairs={{0,1},{1,0},{2,3},{3,2},{4,5},{5,4},{6,7},{7,6},{8,9},{9,8},{10,11... | collective-permute-start | bytes 1376264 | tf_op jit(solution)/shard_map/ppermute | solution.py:27
  57.6 4.7 %slice-start.1 = ((s8[7340032]{0:T(1024)(128)(4,1)}), s8[3145728]{0:T(1024)(128)(4,1)S(1)}, s32[]{:S(2)}) async-start(s8[7340032]{0:T(1024)(128)(4,1)} %bitcast.27), calls=%async_computation.2 | async-start | bytes 6291456
  64.8 18.4 %collective-permute-start.3 = (bf16[256,1280]{1,0:T(8,128)(2,1)S(1)}, bf16[256,1280]{1,0:T(8,128)(2,1)S(1)}, u32[]{:S(2)}, u32[]{:S(2)}) collective-permute-start(bf16[256,1280]{1,0:T(8,128)(2,1)S(1)} %get-tuple-element.36.refs_4_), channel_id=1, source_target_pairs={{0,4},{1,5},{2,6},{3,7},{4,8},{5,9},{6,10},{7,11},{8,12},{9,13},{1... | collective-permute-start | bytes 1966088 | tf_op jit(solution)/shard_map/ppermute | solution.py:27
  67.3 3.2 %copy-start.1 = (bf16[2048,896]{1,0:T(8,128)(2,1)S(1)}, bf16[2048,896]{1,0:T(8,128)(2,1)}, u32[]{:S(2)}) copy-start(bf16[2048,896]{1,0:T(8,128)(2,1)} %copy-done) | copy-start | bytes 11010052
  67.3 15.9 %collective-permute-start.4 = (bf16[256,1024]{1,0:T(8,128)(2,1)S(1)}, bf16[256,1024]{1,0:T(8,128)(2,1)S(1)}, u32[]{:S(2)}, u32[]{:S(2)}) collective-permute-start(bf16[256,1024]{1,0:T(8,128)(2,1)S(1)} %get-tuple-element.42), channel_id=1, source_target_pairs={{0,12},{1,13},{2,14},{3,15},{4,0},{5,1},{6,2},{7,3},{8,4},{9,5},{1... | collective-permute-start | bytes 1572872 | tf_op jit(solution)/shard_map/ppermute | solution.py:27
  69.4 14.0 %collective-permute-start.5 = (bf16[128,1792]{1,0:T(8,128)(2,1)S(1)}, bf16[128,1792]{1,0:T(8,128)(2,1)S(1)}, u32[]{:S(2)}, u32[]{:S(2)}) collective-permute-start(bf16[128,1792]{1,0:T(8,128)(2,1)S(1)} %get-tuple-element.37.refs_2_), channel_id=1, source_target_pairs={{0,2},{1,3},{2,0},{3,1},{4,6},{5,7},{6,4},{7,5},{8,10},{9,11},{10,... | collective-permute-start | bytes 1376264 | tf_op jit(solution)/shard_map/ppermute | solution.py:27
  74.9 2.1 %copy-start.2 = (bf16[2048,896]{1,0:T(8,128)(2,1)}, bf16[2048,896]{1,0:T(8,128)(2,1)S(1)}, u32[]{:S(2)}) copy-start(bf16[2048,896]{1,0:T(8,128)(2,1)S(1)} %get-tuple-element.40.refs_1_) | copy-start | bytes 11010052
  77.0 25.0 %collective-permute-start.8 = (bf16[256,1792]{1,0:T(8,128)(2,1)S(1)}, bf16[256,1792]{1,0:T(8,128)(2,1)S(1)}, u32[]{:S(2)}, u32[]{:S(2)}) collective-permute-start(bf16[256,1792]{1,0:T(8,128)(2,1)S(1)} %shard_map.75.refs_4_), channel_id=1, source_target_pairs={{0,2},{1,3},{2,0},{3,1},{4,6},{5,7},{6,4},{7,5},{8,10},{9,11},{10,... | collective-permute-start | bytes 2752520 | tf_op jit(solution)/shard_map/ppermute | solution.py:27
  83.2 4.0 %copy-start.3 = (bf16[2048,896]{1,0:T(8,128)(2,1)S(1)}, bf16[2048,896]{1,0:T(8,128)(2,1)}, u32[]{:S(2)}) copy-start(bf16[2048,896]{1,0:T(8,128)(2,1)} %copy-done.2) | copy-start | bytes 11010052
  83.6 23.1 %collective-permute-start.9 = (bf16[128,3328]{1,0:T(8,128)(2,1)S(1)}, bf16[128,3328]{1,0:T(8,128)(2,1)S(1)}, u32[]{:S(2)}, u32[]{:S(2)}) collective-permute-start(bf16[128,3328]{1,0:T(8,128)(2,1)S(1)} %get-tuple-element.46.refs_2_), channel_id=1, source_target_pairs={{0,12},{1,13},{2,14},{3,15},{4,0},{5,1},{6,2},{7,3},{8,4},{9,5},{1... | collective-permute-start | bytes 2555912 | tf_op jit(solution)/shard_map/ppermute | solution.py:27
  83.9 21.4 %collective-permute-start.10 = (bf16[128,3072]{1,0:T(8,128)(2,1)S(1)}, bf16[128,3072]{1,0:T(8,128)(2,1)S(1)}, u32[]{:S(2)}, u32[]{:S(2)}) collective-permute-start(bf16[128,3072]{1,0:T(8,128)(2,1)S(1)} %get-tuple-element.58), channel_id=1, source_target_pairs={{0,4},{1,5},{2,6},{3,7},{4,8},{5,9},{6,10},{7,11},{8,12},{9,13},{1... | collective-permute-start | bytes 2359304 | tf_op jit(solution)/shard_map/ppermute | solution.py:27
  94.1 6.8 %copy-start.5 = (bf16[4096]{0:T(1024)(128)(2,1)S(1)}, bf16[4096]{0:T(1024)(128)(2,1)}, u32[]{:S(2)}) copy-start(bf16[4096]{0:T(1024)(128)(2,1)} %param.9) | copy-start | bytes 24580
  98.8 19.1 %collective-permute-start.6 = (bf16[128,2304]{1,0:T(8,128)(2,1)S(1)}, bf16[128,2304]{1,0:T(8,128)(2,1)S(1)}, u32[]{:S(2)}, u32[]{:S(2)}) collective-permute-start(bf16[128,2304]{1,0:T(8,128)(2,1)S(1)} %get-tuple-element.53.refs_3_), channel_id=1, source_target_pairs={{0,4},{1,5},{2,6},{3,7},{4,8},{5,9},{6,10},{7,11},{8,12},{9,13},{1... | collective-permute-start | bytes 1769480 | tf_op jit(solution)/shard_map/ppermute | solution.py:27
  100.6 18.8 %collective-permute-start.7 = (bf16[128,2304]{1,0:T(8,128)(2,1)S(1)}, bf16[128,2304]{1,0:T(8,128)(2,1)S(1)}, u32[]{:S(2)}, u32[]{:S(2)}) collective-permute-start(bf16[128,2304]{1,0:T(8,128)(2,1)S(1)} %get-tuple-element.54), channel_id=1, source_target_pairs={{0,12},{1,13},{2,14},{3,15},{4,0},{5,1},{6,2},{7,3},{8,4},{9,5},{1... | collective-permute-start | bytes 1769480 | tf_op jit(solution)/shard_map/ppermute | solution.py:27
  107.0 12.4 %copy-start.4 = (bf16[128,4096]{1,0:T(8,128)(2,1)S(1)}, bf16[128,4096]{1,0:T(8,128)(2,1)}, u32[]{:S(2)}) copy-start(bf16[128,4096]{1,0:T(8,128)(2,1)} %refs_4_.1) | copy-start | bytes 3145732
  107.0 22.7 %collective-permute-start.11 = (bf16[128,4096]{1,0:T(8,128)(2,1)S(1)}, bf16[128,4096]{1,0:T(8,128)(2,1)S(1)}, u32[]{:S(2)}, u32[]{:S(2)}) collective-permute-start(bf16[128,4096]{1,0:T(8,128)(2,1)S(1)} %shard_map.85.refs_2_), channel_id=1, source_target_pairs={{0,2},{1,3},{2,0},{3,1},{4,6},{5,7},{6,4},{7,5},{8,10},{9,11},{10,... | collective-permute-start | bytes 3145736 | tf_op jit(solution)/shard_map/ppermute | solution.py:27
  108.1 19.9 %collective-permute-start.12 = (bf16[128,1792]{1,0:T(8,128)(2,1)S(1)}, bf16[128,1792]{1,0:T(8,128)(2,1)S(1)}, u32[]{:S(2)}, u32[]{:S(2)}) collective-permute-start(bf16[128,1792]{1,0:T(8,128)(2,1)S(1)} %shard_map.86.refs_2_), channel_id=1, source_target_pairs={{0,4},{1,5},{2,6},{3,7},{4,8},{5,9},{6,10},{7,11},{8,12},{9,13},{1... | collective-permute-start | bytes 1376264 | tf_op jit(solution)/shard_map/ppermute | solution.py:27
  110.4 17.6 %collective-permute-start.13 = (bf16[128,1792]{1,0:T(8,128)(2,1)S(1)}, bf16[128,1792]{1,0:T(8,128)(2,1)S(1)}, u32[]{:S(2)}, u32[]{:S(2)}) collective-permute-start(bf16[128,1792]{1,0:T(8,128)(2,1)S(1)} %shard_map.87.refs_5_), channel_id=1, source_target_pairs={{0,12},{1,13},{2,14},{3,15},{4,0},{5,1},{6,2},{7,3},{8,4},{9,5},{1... | collective-permute-start | bytes 1376264 | tf_op jit(solution)/shard_map/ppermute | solution.py:27

commit v4 on v3

--- a/solution.py
+++ b/solution.py
@@ -81,12 +81,21 @@
 
 def gather_kernel(first, order_ref, rows_ref, out_ref):
     for at in range(0, out_ref.shape[0], 256):
-        order = order_ref[first + at : first + at + 256]
+        order = column_of(order_ref, first + at)
         place = lax.broadcasted_iota(jnp.int32, (256, rows_ref.shape[0]), 1)
         pick = jnp.where(place == order, 1.0, 0.0).astype(jnp.bfloat16)
         out_ref[at : at + 256] = jnp.dot(
             pick, rows_ref[...], preferred_element_type=jnp.float32
         ).astype(jnp.bfloat16)
+
+
+def column_of(order_ref, first):
+    one, two = (lax.broadcasted_iota(jnp.int32, (128, 128), axis) for axis in (0, 1))
+    halves = []
+    for at in (first // 128, first // 128 + 1):
+        row = order_ref[at : at + 1].astype(jnp.float32)
+        halves.append(jnp.sum(jnp.where(one == two, row, 0.0), axis=1, keepdims=True))
+    return jnp.concatenate(halves, axis=0).astype(jnp.int32)
 
 
 def first_gather_kernel(first, parts, order_ref, rows_ref, held_ref, out_ref, sems):
@@ -99,10 +108,11 @@
         )
     for copy in copies:
         copy.start()
+    order = column_of(order_ref, first)
     total = jnp.zeros(out_ref.shape, jnp.float32)
     for at in range(parts):
         place = lax.broadcasted_iota(jnp.int32, (256, step), 1) + at * step
-        pick = jnp.where(place == order_ref[first : first + 256], 1.0, 0.0).astype(jnp.bfloat16)
+        pick = jnp.where(place == order, 1.0, 0.0).astype(jnp.bfloat16)
         copies[at].wait()
         total += jnp.dot(
             pick, held_ref[at * step : (at + 1) * step], preferred_element_type=jnp.float32
@@ -136,28 +146,52 @@
     )
 
 
-def second_gather_kernel(first, order_ref, rows_ref, w_ref, w_out_ref, out_ref, sem):
-    copy = pltpu.make_async_copy(w_ref, w_out_ref, sem)
-    copy.start()
-    gather_kernel(first, order_ref, rows_ref, out_ref)
-    copy.wait()
-
-
-def second_gather(order, rows, first, w, after):
-    m, k = rows.shape
-    n = len(after)
-    kernel = functools.partial(second_gather_kernel, first)
+def first_term_kernel(cuts, own_ref, sib_ref, w_own_ref, w_ref, held_ref, b1_ref, b2_ref, total, sems):
+    chunks = [slice(*c) for c in zip(cuts, cuts[1:])]
+    copies = [
+        pltpu.make_async_copy(w_ref.at[chunk], held_ref.at[chunk], sems.at[at])
+        for at, chunk in enumerate(chunks)
+    ]
+    for copy in copies:
+        copy.start()
+    tiles = [
+        (slice(at, at + TILE), slice(WA + at, WA + at + TILE)) for at in range(0, WB, TILE)
+    ]
+    for here, there in tiles:
+        total[:, here] = jnp.dot(
+            own_ref[...], w_own_ref[:, there], preferred_element_type=jnp.float32
+        )
+    for chunk, copy in zip(chunks, copies):
+        copy.wait()
+        for here, there in tiles:
+            more = total[:, here] + jnp.dot(
+                sib_ref[:, chunk], held_ref[chunk, there], preferred_element_type=jnp.float32
+            )
+            if chunk is not chunks[-1]:
+                total[:, here] = more
+            elif here.start < WB1:
+                b1_ref[:, here] = more.astype(jnp.bfloat16)
+            else:
+                b2_ref[:, here.start - WB1 : here.stop - WB1] = more.astype(jnp.bfloat16)
+
+
+def first_term(own, sib, w_own, w_sib):
+    k, d = w_sib.shape
+    cuts = (0, 512, 768, k)
     return pl.pallas_call(
-        lambda order_ref, rows_ref, w_ref, *refs: kernel(order_ref, rows_ref, w_ref, *refs[n:]),
-        out_shape=[bf(*w.shape), bf(256, k)],
-        in_specs=[pl.BlockSpec(memory_space=pltpu.VMEM)] * 2
-        + [pl.BlockSpec(memory_space=pl.ANY)] * (n + 1),
-        scratch_shapes=[pltpu.SemaphoreType.DMA],
+        functools.partial(first_term_kernel, cuts),
+        out_shape=[bf(k, d), bf(256, WB1), bf(256, WB2)],
+        in_specs=[pl.BlockSpec(memory_space=pltpu.VMEM)] * 3
+        + [pl.BlockSpec(memory_space=pl.ANY)],
+        scratch_shapes=[
+            pltpu.VMEM((256, WB), jnp.float32),
+            pltpu.SemaphoreType.DMA((len(cuts) - 1,)),
+        ],
         compiler_params=pltpu.CompilerParams(vmem_limit_bytes=24 * MIB),
         cost_estimate=pl.CostEstimate(
-            flops=2 * 256 * m * k // 5, bytes_accessed=0, transcendentals=0
+            flops=4 * 256 * k * WB // 5, bytes_accessed=0, transcendentals=0
         ),
-    )(order, rows, w, *after)
+    )(own, sib, w_own, w_sib)
 
 
 def term_kernel(ranges, start, own_ref, sib_ref, w_own_ref, w_sib_ref, *outs):
@@ -284,11 +318,10 @@
     order = jnp.where(x == 0, order[:, ::-1], order)
     order = jnp.where(core == 0, order[:, :, ::-1], order)
     places = [(2, 0), (2, 1), (1, 0), (3, 0), (1, 1), (3, 1), (0, 0), (0, 1)]
-    order = jnp.stack([order[p] for p in places], axis=1).reshape(-1, 1)
-    own = order.shape[0] // 2
-
-    tb1, tb2 = A_TILES, A_TILES + B1_TILES
-    b_halves = ((tb1, B1_TILES, ((0, 1),)), (tb2, B2_TILES, ((0, 1),)))
+    order = jnp.stack([order[p] for p in places], axis=1).reshape(-1, rows)
+    own = order.size // 2
+
+    tb1 = A_TILES
     a_stacked = ((0, A_TILES, ((0, 1),)),)
     a_only = ((0, A_TILES, ((0,), (1,))),)
     both = ((0, A_TILES, ((0,), (1,))), (tb1, B1_TILES + B2_TILES, ((0,), (1,))))
@@ -297,8 +330,8 @@
     held_sib = hop(held, 0, 0, 1)
     held, give2 = first_gather(order, held, 0, (w_sib,))
     sib2 = hop(give2, 0, 0, 1)
-    w_sib, own2 = second_gather(order, held, own, w_sib, (give2,))
-    b1, b2 = term(own2, sib2, 0, w_own, w_sib, b_halves, ())
+    own2 = gather(order, held, own, 256, (give2,))
+    w_sib, b1, b2 = first_term(own2, sib2, w_own, w_sib)
     y1 = hop(b1, 1, 0, 0)
     y3 = hop(b2, 3, 0, 0)
     ax2, ao2 = term(own2, sib2, 0, w_own, w_sib, a_only, (b1,))
@@ -308,16 +341,16 @@
     ax13 = term(own13x, sib13x, 0, w_own, w_sib, a_stacked, ())[0]
     x13 = hop(ax13, 0, 1, 0)
     bx1, bx3 = term(own13x, sib13x, 0, w_own, w_sib, b_only, (ax13,))
-    own_r = gather(order, held, own + 512, 512, (bx1,))
     t1, t3 = whole_call(
-        functools.partial(both_kernel, 0), [bf(128, WB)] * 2, bx1, y1, bx3, y3, after=(own_r,)
+        functools.partial(both_kernel, 0), [bf(128, WB)] * 2, bx1, y1, bx3, y3
     )
     tv1, tv3 = whole_call(
         widen_kernel, [bf(128, WB + WA1), bf(128, WB + WA - WA1)], t1, t3, ao2, x2
     )
     v1 = hop(tv1, 1, 0, 0)
     v3 = hop(tv3, 3, 0, 0)
-    sib_r = gather(order, held_sib, own + 512, 512, (tv3,))
+    own_r = gather(order, held, own + 512, 512, (tv3,))
+    sib_r = gather(order, held_sib, own + 512, 512, (own_r,))
     ao1, ao3, bo1, bo3 = term(own_r, sib_r, 0, w_own, w_sib, both, ())
     ax0, ao0, bx0, bo0 = term(own_r, sib_r, 256, w_own, w_sib, both, (ao1,))
     tu1, tu3 = whole_call(

time: 132 us -> 130 us (0.985)
  waiting for transfers between devices: 24.5 us -> 21.8 us
  starting transfers between devices: 14.6 us -> 16.1 us
    ppermute x14, waiting for transfers between devices: 24.5 us -> 21.8 us  [hop(): return lax.ppermute(value, 'tensor', pairs)]
    ppermute x14, starting transfers between devices: 14.6 us -> 16.1 us  [hop(): return lax.ppermute(value, 'tensor', pairs)]
  transfers between devices with their start and end apart: 14 -> 14, of which waited for: 7 -> 8; matrix products, arithmetic and copies ran while one was open for 0% -> 0% of each run, Pallas kernels for 30% -> 31%
where the time goes in v4:
time: 130 us; the launch traced here: 128 us
  blocking collectives  48.6 us (37%)
  Pallas kernels  40.9 us (31%)
  waiting for transfers between devices  21.8 us (17%)
  starting transfers between devices  16.1 us (12%)
    all_to_all x1, blocking collectives, local(): lax.all_to_all(blocks, 'tensor', split_axis=0, concat_axis=0, tiled=True)  48.6 us
    pallas_call x19, Pallas kernels, whole_call(): pl.pallas_call(without_after, out_shape=out_shape, in_specs=[pl.BlockSpec...  30.5 us
    ppermute x14, waiting for transfers between devices, hop(): return lax.ppermute(value, 'tensor', pairs)  21.8 us
    ppermute x14, starting transfers between devices, hop(): return lax.ppermute(value, 'tensor', pairs)  16.1 us
    pallas_call x2, Pallas kernels, first_gather(): pl.pallas_call(lambda order_ref, rows_ref, *refs: kernel(order_ref, rows_...  6.29 us
    pallas_call x1, Pallas kernels, first_term(): pl.pallas_call(functools.partial(first_term_kernel, cuts), out_shape=[bf(...  4.1 us
  transfers between devices with their start and end apart: 14, of which 8 were waited for; matrix products, arithmetic and copies ran while one was open for 0% of the time, Pallas kernels for 31%

profile of v4, /device:TPU:24, one launch (start us, length us, event | category | flops | bytes accessed | tf_op | source)
XLA Modules:
  0.0 128.4 jit_solution(15380179223216811330)
XLA Ops:
  0.7 3.8 %shard_map.68 = bf16[2048,896]{1,0:T(8,128)(2,1)} custom-call(bf16[128,14336]{1,0:T(8,128)(2,1)} %refs_0_.1), custom_call_target="tpu_custom_call" | custom-call | flops 734003 | tf_op jit(solution)/shard_map/pallas_call | solution.py:38
  4.6 48.6 %all_to_all.11 = bf16[16,128,896]{2,1,0:T(8,128)(2,1)} all-to-all(bf16[16,128,896]{2,1,0:T(8,128)(2,1)} %bitcast.35), channel_id=1, replica_groups=mesh['dp'=16,'tensor'=16] {'tensor'}, dimensions={0} | all-to-all | bytes 7340032 | tf_op jit(solution)/shard_map/all_to_all | solution.py:312
  53.4 3.2 %shard_map.69 = (bf16[2048,896]{1,0:T(8,128)(2,1)S(1)}, bf16[256,896]{1,0:T(8,128)(2,1)S(1)}) custom-call(s32[16,128]{1,0:T(8,128)S(1)} %bitcast.29, bf16[2048,896]{1,0:T(8,128)(2,1)} %bitcast.18.rows_ref, bf16[896,4096]{1,0:T(8,128)(2,1)} %collective-permute-done.refs_0_.w_ref), custom_call_target="tpu_custom_call" | custom-call | flops 187904816 | tf_op jit(solution)/shard_map/pallas_call | solution.py:128
  57.2 1.5 %shard_map.70.own_ref.refs_0_ = bf16[256,896]{1,0:T(8,128)(2,1)S(1)} custom-call(s32[16,128]{1,0:T(8,128)S(1)} %bitcast.30, bf16[2048,896]{1,0:T(8,128)(2,1)S(1)} %get-tuple-element.31.refs_1_, bf16[256,896]{1,0:T(8,128)(2,1)S(1)} %get-tuple-element.32.refs_2_), custom_call_target="tpu_custom_call" | custom-call | flops 187904816 | tf_op jit(solution)/shard_map/pallas_call | solution.py:38
  58.7 1.6 %collective-permute-done.1.sib_ref.refs_1_ = bf16[256,896]{1,0:T(8,128)(2,1)S(1)} collective-permute-done((bf16[256,896]{1,0:T(8,128)(2,1)S(1)}, bf16[256,896]{1,0:T(8,128)(2,1)S(1)}, u32[]{:S(2)}, u32[]{:S(2)}) %collective-permute-start.1) | collective-permute-done | bytes 458784 | tf_op jit(solution)/shard_map/ppermute | solution.py:27
  60.3 4.1 %shard_map.71 = (bf16[896,4096]{1,0:T(8,128)(2,1)S(1)}, bf16[256,1280]{1,0:T(8,128)(2,1)S(1)}, bf16[256,1024]{1,0:T(8,128)(2,1)S(1)}) custom-call(bf16[256,896]{1,0:T(8,128)(2,1)S(1)} %shard_map.70.own_ref.refs_0_, bf16[256,896]{1,0:T(8,128)(2,1)S(1)} %collective-permute-done.1.sib_ref.refs_1_, bf16[896,4096]{1,0:T(8,128)(2,1)S(1)} %bitcast.28, ...), custom_call_target="tpu_custom_call" | custom-call | flops 422785856 | tf_op jit(solution)/shard_map/pallas_call | solution.py:181
  64.4 2.5 %collective-permute-start.3 = (bf16[256,1280]{1,0:T(8,128)(2,1)S(1)}, bf16[256,1280]{1,0:T(8,128)(2,1)S(1)}, u32[]{:S(2)}, u32[]{:S(2)}) collective-permute-start(bf16[256,1280]{1,0:T(8,128)(2,1)S(1)} %get-tuple-element.34.refs_4_), channel_id=1, source_target_pairs={{0,4},{1,5},{2,6},{3,7},{4,8},{5,9},{6,10},{7,11},{8,12},{9,13},{1... | collective-permute-start | bytes 1966088 | tf_op jit(solution)/shard_map/ppermute | solution.py:27
  66.9 2.0 %shard_map.72 = (bf16[128,1792]{1,0:T(8,128)(2,1)S(1)}, bf16[128,1792]{1,0:T(8,128)(2,1)S(1)}) custom-call(bf16[256,896]{1,0:T(8,128)(2,1)S(1)} %shard_map.70.own_ref.refs_0_, bf16[256,896]{1,0:T(8,128)(2,1)S(1)} %collective-permute-done.1.sib_ref.refs_1_, bf16[896,4096]{1,0:T(8,128)(2,1)S(1)} %bitcast.28, bf16[896,4096]{1,0:T(8,128)(2,1)S(1)} %get-tuple-element.33.refs_3_, ...), custom_call_target="tpu_custom_call" | custom-call | flops 328833440 | tf_op jit(solution)/shard_map/pallas_call | solution.py:38
  70.0 1.5 %shard_map.73.refs_0_ = bf16[256,896]{1,0:T(8,128)(2,1)S(1)} custom-call(s32[16,128]{1,0:T(8,128)S(1)} %bitcast.31, bf16[2048,896]{1,0:T(8,128)(2,1)S(1)} %get-tuple-element.31.refs_1_, bf16[128,1792]{1,0:T(8,128)(2,1)S(1)} %get-tuple-element.35.refs_2_), custom_call_target="tpu_custom_call" | custom-call | flops 187904816 | tf_op jit(solution)/shard_map/pallas_call | solution.py:38
  71.4 3.1 %shard_map.74 = (bf16[2048,896]{1,0:T(8,128)(2,1)S(1)}, bf16[256,896]{1,0:T(8,128)(2,1)S(1)}) custom-call(s32[16,128]{1,0:T(8,128)S(1)} %bitcast.32, bf16[2048,896]{1,0:T(8,128)(2,1)} %collective-permute-done.2.rows_ref, bf16[256,896]{1,0:T(8,128)(2,1)S(1)} %shard_map.73.refs_0_), custom_call_target="tpu_custom_call" | custom-call | flops 187904816 | tf_op jit(solution)/shard_map/pallas_call | solution.py:128
  74.5 2.1 %shard_map.75.refs_4_ = bf16[256,1792]{1,0:T(8,128)(2,1)S(1)} custom-call(bf16[256,896]{1,0:T(8,128)(2,1)S(1)} %shard_map.73.refs_0_, bf16[256,896]{1,0:T(8,128)(2,1)S(1)} %get-tuple-element.36.refs_1_, bf16[896,4096]{1,0:T(8,128)(2,1)S(1)} %bitcast.28, bf16[896,4096]{1,0:T(8,128)(2,1)S(1)} %get-tuple-element.33.refs_3_), custom_call_target="tpu_custom_call" | custom-call | flops 328833440 | tf_op jit(solution)/shard_map/pallas_call | solution.py:38
  76.6 1.4 %collective-permute-start.8 = (bf16[256,1792]{1,0:T(8,128)(2,1)S(1)}, bf16[256,1792]{1,0:T(8,128)(2,1)S(1)}, u32[]{:S(2)}, u32[]{:S(2)}) collective-permute-start(bf16[256,1792]{1,0:T(8,128)(2,1)S(1)} %shard_map.75.refs_4_), channel_id=1, source_target_pairs={{0,2},{1,3},{2,0},{3,1},{4,6},{5,7},{6,4},{7,5},{8,10},{9,11},{10,... | collective-permute-start | bytes 2752520 | tf_op jit(solution)/shard_map/ppermute | solution.py:27
  78.0 2.7 %shard_map.76 = (bf16[128,2304]{1,0:T(8,128)(2,1)S(1)}, bf16[128,2304]{1,0:T(8,128)(2,1)S(1)}) custom-call(bf16[256,896]{1,0:T(8,128)(2,1)S(1)} %shard_map.73.refs_0_, bf16[256,896]{1,0:T(8,128)(2,1)S(1)} %get-tuple-element.36.refs_1_, bf16[896,4096]{1,0:T(8,128)(2,1)S(1)} %bitcast.28, bf16[896,4096]{1,0:T(8,128)(2,1)S(1)} %get-tuple-element.33.refs_3_, ...), custom_call_target="tpu_custom_call" | custom-call | flops 422785856 | tf_op jit(solution)/shard_map/pallas_call | solution.py:38
  83.1 3.4 %collective-permute-start.10 = (bf16[128,3072]{1,0:T(8,128)(2,1)S(1)}, bf16[128,3072]{1,0:T(8,128)(2,1)S(1)}, u32[]{:S(2)}, u32[]{:S(2)}) collective-permute-start(bf16[128,3072]{1,0:T(8,128)(2,1)S(1)} %get-tuple-element.56), channel_id=1, source_target_pairs={{0,4},{1,5},{2,6},{3,7},{4,8},{5,9},{6,10},{7,11},{8,12},{9,13},{1... | collective-permute-start | bytes 2359304 | tf_op jit(solution)/shard_map/ppermute | solution.py:27
  86.5 2.6 %shard_map.79.refs_2_.refs_0_ = bf16[512,896]{1,0:T(8,128)(2,1)S(1)} custom-call(s32[16,128]{1,0:T(8,128)S(1)} %bitcast.33, bf16[2048,896]{1,0:T(8,128)(2,1)S(1)} %get-tuple-element.31.refs_1_, bf16[128,3328]{1,0:T(8,128)(2,1)S(1)} %get-tuple-element.43.refs_2_), custom_call_target="tpu_custom_call" | custom-call | flops 375809632 | tf_op jit(solution)/shard_map/pallas_call | solution.py:38
  89.0 2.6 %shard_map.80.refs_1_ = bf16[512,896]{1,0:T(8,128)(2,1)S(1)} custom-call(s32[16,128]{1,0:T(8,128)S(1)} %bitcast.34, bf16[2048,896]{1,0:T(8,128)(2,1)S(1)} %get-tuple-element.44.refs_1_, bf16[512,896]{1,0:T(8,128)(2,1)S(1)} %shard_map.79.refs_2_.refs_0_), custom_call_target="tpu_custom_call" | custom-call | flops 375809632 | tf_op jit(solution)/shard_map/pallas_call | solution.py:38
  91.6 4.5 %shard_map.81 = (bf16[128,1792]{1,0:T(8,128)(2,1)S(1)}, bf16[128,1792]{1,0:T(8,128)(2,1)S(1)}, bf16[128,2304]{1,0:T(8,128)(2,1)S(1)}, bf16[128,2304]{1,0:T(8,128)(2,1)S(1)}) custom-call(bf16[512,896]{1,0:T(8,128)(2,1)S(1)} %shard_map.79.refs_2_.refs_0_, bf16[512,896]{1,0:T(8,128)(2,1)S(1)} %shard_map.80.refs_1_, bf16[896,4096]{1,0:T(8,128)(2,1)S(1)} %bitcast.28, ...), custom_call_target="tpu_custom_call" | custom-call | flops 751619264 | tf_op jit(solution)/shard_map/pallas_call | solution.py:38
  96.1 4.5 %shard_map.82 = (bf16[128,1792]{1,0:T(8,128)(2,1)S(1)}, bf16[128,1792]{1,0:T(8,128)(2,1)S(1)}, bf16[128,2304]{1,0:T(8,128)(2,1)S(1)}, bf16[128,2304]{1,0:T(8,128)(2,1)S(1)}) custom-call(bf16[512,896]{1,0:T(8,128)(2,1)S(1)} %shard_map.79.refs_2_.refs_0_, bf16[512,896]{1,0:T(8,128)(2,1)S(1)} %shard_map.80.refs_1_, bf16[896,4096]{1,0:T(8,128)(2,1)S(1)} %bitcast.28, ...), custom_call_target="tpu_custom_call" | custom-call | flops 751619264 | tf_op jit(solution)/shard_map/pallas_call | solution.py:38
  100.8 1.8 %collective-permute-start.6 = (bf16[128,2304]{1,0:T(8,128)(2,1)S(1)}, bf16[128,2304]{1,0:T(8,128)(2,1)S(1)}, u32[]{:S(2)}, u32[]{:S(2)}) collective-permute-start(bf16[128,2304]{1,0:T(8,128)(2,1)S(1)} %get-tuple-element.51.refs_3_), channel_id=1, source_target_pairs={{0,4},{1,5},{2,6},{3,7},{4,8},{5,9},{6,10},{7,11},{8,12},{9,13},{1... | collective-permute-start | bytes 1769480 | tf_op jit(solution)/shard_map/ppermute | solution.py:27
  104.9 3.8 %collective-permute-start.12 = (bf16[128,1792]{1,0:T(8,128)(2,1)S(1)}, bf16[128,1792]{1,0:T(8,128)(2,1)S(1)}, u32[]{:S(2)}, u32[]{:S(2)}) collective-permute-start(bf16[128,1792]{1,0:T(8,128)(2,1)S(1)} %shard_map.86.refs_2_), channel_id=1, source_target_pairs={{0,4},{1,5},{2,6},{3,7},{4,8},{5,9},{6,10},{7,11},{8,12},{9,13},{1... | collective-permute-start | bytes 1376264 | tf_op jit(solution)/shard_map/ppermute | solution.py:27
  108.9 8.3 %collective-permute-done.6.refs_2_ = bf16[128,2304]{1,0:T(8,128)(2,1)S(1)} collective-permute-done((bf16[128,2304]{1,0:T(8,128)(2,1)S(1)}, bf16[128,2304]{1,0:T(8,128)(2,1)S(1)}, u32[]{:S(2)}, u32[]{:S(2)}) %collective-permute-start.6) | collective-permute-done | bytes 589856 | tf_op jit(solution)/shard_map/ppermute | solution.py:27
  117.1 2.9 %collective-permute-done.7.refs_3_ = bf16[128,2304]{1,0:T(8,128)(2,1)S(1)} collective-permute-done((bf16[128,2304]{1,0:T(8,128)(2,1)S(1)}, bf16[128,2304]{1,0:T(8,128)(2,1)S(1)}, u32[]{:S(2)}, u32[]{:S(2)}) %collective-permute-start.7) | collective-permute-done | bytes 589856 | tf_op jit(solution)/shard_map/ppermute | solution.py:27
  120.4 6.1 %collective-permute-done.13.refs_3_ = bf16[128,1792]{1,0:T(8,128)(2,1)S(1)} collective-permute-done((bf16[128,1792]{1,0:T(8,128)(2,1)S(1)}, bf16[128,1792]{1,0:T(8,128)(2,1)S(1)}, u32[]{:S(2)}, u32[]{:S(2)}) %collective-permute-start.13) | collective-permute-done | bytes 458784 | tf_op jit(solution)/shard_map/ppermute | solution.py:27
  127.0 1.4 %shard_map.89 = (bf16[128,4096]{1,0:T(8,128)(2,1)}, f32[1,128]{1,0:T(1,128)}) custom-call(f32[128,4096]{1,0:T(8,128)S(1)} %shard_map.88.refs_0_, bf16[128,4096]{1,0:T(8,128)(2,1)S(1)} %collective-permute-done.11.refs_1_, bf16[128,1792]{1,0:T(8,128)(2,1)S(1)} %collective-permute-done.12.refs_2_, bf16[128,1792]{1,0:T(8,128)(2,1)S(1)} %collective-permute-done.13.refs_3_, ...), custom_call_target="tpu_custom_call" | custom-call | flops 814284 | tf_op jit(solution)/shard_map/pallas_call | solution.py:38
  (45 shorter events, 7.7 us)
Async XLA Ops:
  0.6 52.7 %collective-permute-start = (bf16[896,4096]{1,0:T(8,128)(2,1)}, bf16[896,4096]{1,0:T(8,128)(2,1)}, u32[]{:S(2)}, u32[]{:S(2)}) collective-permute-start(bf16[896,4096]{1,0:T(8,128)(2,1)} %refs_2_.9), channel_id=1, source_target_pairs={{0,1},{1,0},{2,3},{3,2},{4,5},{5,4},{6,7},{7,6},{8,9},{9,8},{10,11... | collective-permute-start | bytes 22020104 | tf_op jit(solution)/shard_map/ppermute | solution.py:27
  4.6 48.7 %copy-start.2 = (s32[2048]{0:T(1024)S(1)}, s32[2048]{0:T(1024)}, u32[]{:S(2)}) copy-start(s32[2048]{0:T(1024)} %param.8) | copy-start | bytes 24580
  53.2 18.2 %collective-permute-start.2 = (bf16[2048,896]{1,0:T(8,128)(2,1)}, bf16[2048,896]{1,0:T(8,128)(2,1)}, u32[]{:S(2)}, u32[]{:S(2)}) collective-permute-start(bf16[2048,896]{1,0:T(8,128)(2,1)} %bitcast.18.rows_ref), channel_id=1, source_target_pairs={{0,1},{1,0},{2,3},{3,2},{4,5},{5,4},{6,7},{7,6},{8,9},{9,8},{10,11... | collective-permute-start | bytes 11010056 | tf_op jit(solution)/shard_map/ppermute | solution.py:27
  53.4 6.9 %slice-start = ((s8[7340032]{0:T(1024)(128)(4,1)}), s8[4194304]{0:T(1024)(128)(4,1)S(1)}, s32[]{:S(2)}) async-start(s8[7340032]{0:T(1024)(128)(4,1)} %bitcast.27), calls=%async_computation.1 | async-start | bytes 8388608
  53.4 6.9 %slice-start.1 = ((s8[7340032]{0:T(1024)(128)(4,1)}), s8[3145728]{0:T(1024)(128)(4,1)S(1)}, s32[]{:S(2)}) async-start(s8[7340032]{0:T(1024)(128)(4,1)} %bitcast.27), calls=%async_computation.2 | async-start | bytes 6291456
  56.6 3.7 %collective-permute-start.1 = (bf16[256,896]{1,0:T(8,128)(2,1)S(1)}, bf16[256,896]{1,0:T(8,128)(2,1)S(1)}, u32[]{:S(2)}, u32[]{:S(2)}) collective-permute-start(bf16[256,896]{1,0:T(8,128)(2,1)S(1)} %get-tuple-element.32.refs_2_), channel_id=1, source_target_pairs={{0,1},{1,0},{2,3},{3,2},{4,5},{5,4},{6,7},{7,6},{8,9},{9,8},{10,11... | collective-permute-start | bytes 1376264 | tf_op jit(solution)/shard_map/ppermute | solution.py:27
  64.4 17.4 %collective-permute-start.3 = (bf16[256,1280]{1,0:T(8,128)(2,1)S(1)}, bf16[256,1280]{1,0:T(8,128)(2,1)S(1)}, u32[]{:S(2)}, u32[]{:S(2)}) collective-permute-start(bf16[256,1280]{1,0:T(8,128)(2,1)S(1)} %get-tuple-element.34.refs_4_), channel_id=1, source_target_pairs={{0,4},{1,5},{2,6},{3,7},{4,8},{5,9},{6,10},{7,11},{8,12},{9,13},{1... | collective-permute-start | bytes 1966088 | tf_op jit(solution)/shard_map/ppermute | solution.py:27
  66.9 14.9 %collective-permute-start.4 = (bf16[256,1024]{1,0:T(8,128)(2,1)S(1)}, bf16[256,1024]{1,0:T(8,128)(2,1)S(1)}, u32[]{:S(2)}, u32[]{:S(2)}) collective-permute-start(bf16[256,1024]{1,0:T(8,128)(2,1)S(1)} %get-tuple-element.39), channel_id=1, source_target_pairs={{0,12},{1,13},{2,14},{3,15},{4,0},{5,1},{6,2},{7,3},{8,4},{9,5},{1... | collective-permute-start | bytes 1572872 | tf_op jit(solution)/shard_map/ppermute | solution.py:27
  69.0 13.7 %collective-permute-start.5 = (bf16[128,1792]{1,0:T(8,128)(2,1)S(1)}, bf16[128,1792]{1,0:T(8,128)(2,1)S(1)}, u32[]{:S(2)}, u32[]{:S(2)}) collective-permute-start(bf16[128,1792]{1,0:T(8,128)(2,1)S(1)} %get-tuple-element.35.refs_2_), channel_id=1, source_target_pairs={{0,2},{1,3},{2,0},{3,1},{4,6},{5,7},{6,4},{7,5},{8,10},{9,11},{10,... | collective-permute-start | bytes 1376264 | tf_op jit(solution)/shard_map/ppermute | solution.py:27
  76.6 26.3 %collective-permute-start.8 = (bf16[256,1792]{1,0:T(8,128)(2,1)S(1)}, bf16[256,1792]{1,0:T(8,128)(2,1)S(1)}, u32[]{:S(2)}, u32[]{:S(2)}) collective-permute-start(bf16[256,1792]{1,0:T(8,128)(2,1)S(1)} %shard_map.75.refs_4_), channel_id=1, source_target_pairs={{0,2},{1,3},{2,0},{3,1},{4,6},{5,7},{6,4},{7,5},{8,10},{9,11},{10,... | collective-permute-start | bytes 2752520 | tf_op jit(solution)/shard_map/ppermute | solution.py:27
  82.8 20.9 %collective-permute-start.9 = (bf16[128,3328]{1,0:T(8,128)(2,1)S(1)}, bf16[128,3328]{1,0:T(8,128)(2,1)S(1)}, u32[]{:S(2)}, u32[]{:S(2)}) collective-permute-start(bf16[128,3328]{1,0:T(8,128)(2,1)S(1)} %get-tuple-element.43.refs_2_), channel_id=1, source_target_pairs={{0,12},{1,13},{2,14},{3,15},{4,0},{5,1},{6,2},{7,3},{8,4},{9,5},{1... | collective-permute-start | bytes 2555912 | tf_op jit(solution)/shard_map/ppermute | solution.py:27
  83.1 20.1 %collective-permute-start.10 = (bf16[128,3072]{1,0:T(8,128)(2,1)S(1)}, bf16[128,3072]{1,0:T(8,128)(2,1)S(1)}, u32[]{:S(2)}, u32[]{:S(2)}) collective-permute-start(bf16[128,3072]{1,0:T(8,128)(2,1)S(1)} %get-tuple-element.56), channel_id=1, source_target_pairs={{0,4},{1,5},{2,6},{3,7},{4,8},{5,9},{6,10},{7,11},{8,12},{9,13},{1... | collective-permute-start | bytes 2359304 | tf_op jit(solution)/shard_map/ppermute | solution.py:27
  96.1 6.8 %copy-start.1 = (bf16[4096]{0:T(1024)(128)(2,1)S(1)}, bf16[4096]{0:T(1024)(128)(2,1)}, u32[]{:S(2)}) copy-start(bf16[4096]{0:T(1024)(128)(2,1)} %param.9) | copy-start | bytes 24580
  100.8 16.3 %collective-permute-start.6 = (bf16[128,2304]{1,0:T(8,128)(2,1)S(1)}, bf16[128,2304]{1,0:T(8,128)(2,1)S(1)}, u32[]{:S(2)}, u32[]{:S(2)}) collective-permute-start(bf16[128,2304]{1,0:T(8,128)(2,1)S(1)} %get-tuple-element.51.refs_3_), channel_id=1, source_target_pairs={{0,4},{1,5},{2,6},{3,7},{4,8},{5,9},{6,10},{7,11},{8,12},{9,13},{1... | collective-permute-start | bytes 1769480 | tf_op jit(solution)/shard_map/ppermute | solution.py:27
  102.6 17.5 %collective-permute-start.7 = (bf16[128,2304]{1,0:T(8,128)(2,1)S(1)}, bf16[128,2304]{1,0:T(8,128)(2,1)S(1)}, u32[]{:S(2)}, u32[]{:S(2)}) collective-permute-start(bf16[128,2304]{1,0:T(8,128)(2,1)S(1)} %get-tuple-element.52), channel_id=1, source_target_pairs={{0,12},{1,13},{2,14},{3,15},{4,0},{5,1},{6,2},{7,3},{8,4},{9,5},{1... | collective-permute-start | bytes 1769480 | tf_op jit(solution)/shard_map/ppermute | solution.py:27
  104.0 16.1 %copy-start = (bf16[128,4096]{1,0:T(8,128)(2,1)S(1)}, bf16[128,4096]{1,0:T(8,128)(2,1)}, u32[]{:S(2)}) copy-start(bf16[128,4096]{1,0:T(8,128)(2,1)} %refs_4_.1) | copy-start | bytes 3145732
  104.0 23.0 %collective-permute-start.11 = (bf16[128,4096]{1,0:T(8,128)(2,1)S(1)}, bf16[128,4096]{1,0:T(8,128)(2,1)S(1)}, u32[]{:S(2)}, u32[]{:S(2)}) collective-permute-start(bf16[128,4096]{1,0:T(8,128)(2,1)S(1)} %shard_map.85.refs_2_), channel_id=1, source_target_pairs={{0,2},{1,3},{2,0},{3,1},{4,6},{5,7},{6,4},{7,5},{8,10},{9,11},{10,... | collective-permute-start | bytes 3145736 | tf_op jit(solution)/shard_map/ppermute | solution.py:27
  104.9 21.6 %collective-permute-start.12 = (bf16[128,1792]{1,0:T(8,128)(2,1)S(1)}, bf16[128,1792]{1,0:T(8,128)(2,1)S(1)}, u32[]{:S(2)}, u32[]{:S(2)}) collective-permute-start(bf16[128,1792]{1,0:T(8,128)(2,1)S(1)} %shard_map.86.refs_2_), channel_id=1, source_target_pairs={{0,4},{1,5},{2,6},{3,7},{4,8},{5,9},{6,10},{7,11},{8,12},{9,13},{1... | collective-permute-start | bytes 1376264 | tf_op jit(solution)/shard_map/ppermute | solution.py:27
  108.8 17.7 %collective-permute-start.13 = (bf16[128,1792]{1,0:T(8,128)(2,1)S(1)}, bf16[128,1792]{1,0:T(8,128)(2,1)S(1)}, u32[]{:S(2)}, u32[]{:S(2)}) collective-permute-start(bf16[128,1792]{1,0:T(8,128)(2,1)S(1)} %shard_map.87.refs_5_), channel_id=1, source_target_pairs={{0,12},{1,13},{2,14},{3,15},{4,0},{5,1},{6,2},{7,3},{8,4},{9,5},{1... | collective-permute-start | bytes 1376264 | tf_op jit(solution)/shard_map/ppermute | solution.py:27

commit v5 on v3

--- a/solution.py
+++ b/solution.py
@@ -13,6 +13,7 @@
 WA, WB1, WB2 = A_TILES * TILE, B1_TILES * TILE, B2_TILES * TILE
 WB = WB1 + WB2
 WA1 = 3 * TILE
+TOP = 512
 MIB = 1 << 20
 
 
@@ -81,12 +82,21 @@
 
 def gather_kernel(first, order_ref, rows_ref, out_ref):
     for at in range(0, out_ref.shape[0], 256):
-        order = order_ref[first + at : first + at + 256]
+        order = column_of(order_ref, first + at)
         place = lax.broadcasted_iota(jnp.int32, (256, rows_ref.shape[0]), 1)
         pick = jnp.where(place == order, 1.0, 0.0).astype(jnp.bfloat16)
         out_ref[at : at + 256] = jnp.dot(
             pick, rows_ref[...], preferred_element_type=jnp.float32
         ).astype(jnp.bfloat16)
+
+
+def column_of(order_ref, first):
+    one, two = (lax.broadcasted_iota(jnp.int32, (128, 128), axis) for axis in (0, 1))
+    halves = []
+    for at in (first // 128, first // 128 + 1):
+        row = order_ref[at : at + 1].astype(jnp.float32)
+        halves.append(jnp.sum(jnp.where(one == two, row, 0.0), axis=1, keepdims=True))
+    return jnp.concatenate(halves, axis=0).astype(jnp.int32)
 
 
 def first_gather_kernel(first, parts, order_ref, rows_ref, held_ref, out_ref, sems):
@@ -99,10 +109,11 @@
         )
     for copy in copies:
         copy.start()
+    order = column_of(order_ref, first)
     total = jnp.zeros(out_ref.shape, jnp.float32)
     for at in range(parts):
         place = lax.broadcasted_iota(jnp.int32, (256, step), 1) + at * step
-        pick = jnp.where(place == order_ref[first : first + 256], 1.0, 0.0).astype(jnp.bfloat16)
+        pick = jnp.where(place == order, 1.0, 0.0).astype(jnp.bfloat16)
         copies[at].wait()
         total += jnp.dot(
             pick, held_ref[at * step : (at + 1) * step], preferred_element_type=jnp.float32
@@ -136,8 +147,8 @@
     )
 
 
-def second_gather_kernel(first, order_ref, rows_ref, w_ref, w_out_ref, out_ref, sem):
-    copy = pltpu.make_async_copy(w_ref, w_out_ref, sem)
+def second_gather_kernel(first, order_ref, rows_ref, w_ref, top_ref, out_ref, sem):
+    copy = pltpu.make_async_copy(w_ref.at[:TOP], top_ref, sem)
     copy.start()
     gather_kernel(first, order_ref, rows_ref, out_ref)
     copy.wait()
@@ -149,7 +160,7 @@
     kernel = functools.partial(second_gather_kernel, first)
     return pl.pallas_call(
         lambda order_ref, rows_ref, w_ref, *refs: kernel(order_ref, rows_ref, w_ref, *refs[n:]),
-        out_shape=[bf(*w.shape), bf(256, k)],
+        out_shape=[bf(TOP, w.shape[1]), bf(256, k)],
         in_specs=[pl.BlockSpec(memory_space=pltpu.VMEM)] * 2
         + [pl.BlockSpec(memory_space=pl.ANY)] * (n + 1),
         scratch_shapes=[pltpu.SemaphoreType.DMA],
@@ -160,14 +171,56 @@
     )(order, rows, w, *after)
 
 
-def term_kernel(ranges, start, own_ref, sib_ref, w_own_ref, w_sib_ref, *outs):
+def first_term_kernel(own_ref, sib_ref, own_w, top_w, w_ref, low_w, b1_ref, b2_ref, total, sem):
+    copy = pltpu.make_async_copy(w_ref.at[TOP:], low_w, sem)
+    copy.start()
+    tiles = [
+        (slice(at, at + TILE), slice(WA + at, WA + at + TILE)) for at in range(0, WB, TILE)
+    ]
+    for here, there in tiles:
+        one = jnp.dot(own_ref[...], own_w[:, there], preferred_element_type=jnp.float32)
+        total[:, here] = one + jnp.dot(
+            sib_ref[:, :TOP], top_w[:, there], preferred_element_type=jnp.float32
+        )
+    copy.wait()
+    for here, there in tiles:
+        more = total[:, here] + jnp.dot(
+            sib_ref[:, TOP:], low_w[:, there], preferred_element_type=jnp.float32
+        )
+        if here.start < WB1:
+            b1_ref[:, here] = more.astype(jnp.bfloat16)
+        else:
+            b2_ref[:, here.start - WB1 : here.stop - WB1] = more.astype(jnp.bfloat16)
+
+
+def first_term(own, sib, w_own, w_top, w_sib):
+    k, d = w_sib.shape
+    return pl.pallas_call(
+        first_term_kernel,
+        out_shape=[bf(k - TOP, d), bf(256, WB1), bf(256, WB2)],
+        in_specs=[pl.BlockSpec(memory_space=pltpu.VMEM)] * 4
+        + [pl.BlockSpec(memory_space=pl.ANY)],
+        scratch_shapes=[pltpu.VMEM((256, WB), jnp.float32), pltpu.SemaphoreType.DMA],
+        compiler_params=pltpu.CompilerParams(vmem_limit_bytes=24 * MIB),
+        cost_estimate=pl.CostEstimate(
+            flops=4 * 256 * k * WB // 5, bytes_accessed=0, transcendentals=0
+        ),
+    )(own, sib, w_own, w_top, w_sib)
+
+
+def term_kernel(ranges, start, own_ref, sib_ref, own_w, top_w, low_w, *outs):
     rows = slice(start, start + 256)
     for first, count, groups in ranges:
         for j in range(count):
             tile = slice((first + j) * TILE, (first + j + 1) * TILE)
             here = slice(j * TILE, (j + 1) * TILE)
-            total = jnp.dot(own_ref[rows], w_own_ref[:, tile], preferred_element_type=jnp.float32)
-            total += jnp.dot(sib_ref[rows], w_sib_ref[:, tile], preferred_element_type=jnp.float32)
+            total = jnp.dot(own_ref[rows], own_w[:, tile], preferred_element_type=jnp.float32)
+            total += jnp.dot(
+                sib_ref[rows, :TOP], top_w[:, tile], preferred_element_type=jnp.float32
+            )
+            total += jnp.dot(
+                sib_ref[rows, TOP:], low_w[:, tile], preferred_element_type=jnp.float32
+            )
             total = total.astype(jnp.bfloat16)
             for out, blocks in zip(outs, groups):
                 for at, block in enumerate(blocks):
@@ -175,11 +228,11 @@
         outs = outs[len(groups) :]
 
 
-def term(own, sib, start, w_own, w_sib, ranges, after):
-    k = w_own.shape[0]
+def term(own, sib, start, w, ranges, after):
+    k = w[0].shape[0]
     shapes = [bf(128 * len(g), count * TILE) for _, count, groups in ranges for g in groups]
     return whole_call(
-        functools.partial(term_kernel, ranges, start), shapes, own, sib, w_own, w_sib,
+        functools.partial(term_kernel, ranges, start), shapes, own, sib, *w,
         flops=4 * 256 * k * TILE * sum(r[1] for r in ranges), after=after,
     )
 
@@ -284,11 +337,10 @@
     order = jnp.where(x == 0, order[:, ::-1], order)
     order = jnp.where(core == 0, order[:, :, ::-1], order)
     places = [(2, 0), (2, 1), (1, 0), (3, 0), (1, 1), (3, 1), (0, 0), (0, 1)]
-    order = jnp.stack([order[p] for p in places], axis=1).reshape(-1, 1)
-    own = order.shape[0] // 2
-
-    tb1, tb2 = A_TILES, A_TILES + B1_TILES
-    b_halves = ((tb1, B1_TILES, ((0, 1),)), (tb2, B2_TILES, ((0, 1),)))
+    order = jnp.stack([order[p] for p in places], axis=1).reshape(-1, rows)
+    own = order.size // 2
+
+    tb1 = A_TILES
     a_stacked = ((0, A_TILES, ((0, 1),)),)
     a_only = ((0, A_TILES, ((0,), (1,))),)
     both = ((0, A_TILES, ((0,), (1,))), (tb1, B1_TILES + B2_TILES, ((0,), (1,))))
@@ -297,29 +349,30 @@
     held_sib = hop(held, 0, 0, 1)
     held, give2 = first_gather(order, held, 0, (w_sib,))
     sib2 = hop(give2, 0, 0, 1)
-    w_sib, own2 = second_gather(order, held, own, w_sib, (give2,))
-    b1, b2 = term(own2, sib2, 0, w_own, w_sib, b_halves, ())
+    w_top, own2 = second_gather(order, held, own, w_sib, (give2,))
+    w_low, b1, b2 = first_term(own2, sib2, w_own, w_top, w_sib)
+    w = (w_own, w_top, w_low)
     y1 = hop(b1, 1, 0, 0)
     y3 = hop(b2, 3, 0, 0)
-    ax2, ao2 = term(own2, sib2, 0, w_own, w_sib, a_only, (b1,))
+    ax2, ao2 = term(own2, sib2, 0, w, a_only, (b1,))
     x2 = hop(ax2, 0, 1, 0)
     own13x = gather(order, held, own + 256, 256, (ax2,))
     held_sib, sib13x = first_gather(order, held_sib, own + 256, (own13x,))
-    ax13 = term(own13x, sib13x, 0, w_own, w_sib, a_stacked, ())[0]
+    ax13 = term(own13x, sib13x, 0, w, a_stacked, ())[0]
     x13 = hop(ax13, 0, 1, 0)
-    bx1, bx3 = term(own13x, sib13x, 0, w_own, w_sib, b_only, (ax13,))
-    own_r = gather(order, held, own + 512, 512, (bx1,))
+    bx1, bx3 = term(own13x, sib13x, 0, w, b_only, (ax13,))
     t1, t3 = whole_call(
-        functools.partial(both_kernel, 0), [bf(128, WB)] * 2, bx1, y1, bx3, y3, after=(own_r,)
+        functools.partial(both_kernel, 0), [bf(128, WB)] * 2, bx1, y1, bx3, y3
     )
     tv1, tv3 = whole_call(
         widen_kernel, [bf(128, WB + WA1), bf(128, WB + WA - WA1)], t1, t3, ao2, x2
     )
     v1 = hop(tv1, 1, 0, 0)
     v3 = hop(tv3, 3, 0, 0)
-    sib_r = gather(order, held_sib, own + 512, 512, (tv3,))
-    ao1, ao3, bo1, bo3 = term(own_r, sib_r, 0, w_own, w_sib, both, ())
-    ax0, ao0, bx0, bo0 = term(own_r, sib_r, 256, w_own, w_sib, both, (ao1,))
+    own_r = gather(order, held, own + 512, 512, (tv3,))
+    sib_r = gather(order, held_sib, own + 512, 512, (own_r,))
+    ao1, ao3, bo1, bo3 = term(own_r, sib_r, 0, w, both, ())
+    ax0, ao0, bx0, bo0 = term(own_r, sib_r, 256, w, both, (ao1,))
     tu1, tu3 = whole_call(
         functools.partial(both_kernel, 128), [bf(128, WB)] * 2, bo1, y1, bo3, y3, after=(ax0,)
     )

time: 132 us -> 129 us (0.977)
  waiting for transfers between devices: 24.5 us -> 20.4 us
    ppermute x14, waiting for transfers between devices: 24.5 us -> 20.4 us  [hop(): return lax.ppermute(value, 'tensor', pairs)]
    pallas_call x0 -> x1, Pallas kernels: none -> 2.89 us  [first_term(): pl.pallas_call(first_term_kernel, out_shape=[bf(k - TOP, d), bf(256, WB1)...]
    pallas_call x19 -> x18, Pallas kernels: 30.9 us -> 29.3 us  [whole_call(): pl.pallas_call(without_after, out_shape=out_shape, in_specs=[pl.BlockSpec...]
    pallas_call x1, Pallas kernels: 3.83 us -> 2.37 us  [second_gather(): pl.pallas_call(lambda order_ref, rows_ref, w_ref, *refs: kernel(order_ref...]
  transfers between devices with their start and end apart: 14 -> 14, of which waited for: 7 -> 8; matrix products, arithmetic and copies ran while one was open for 0% -> 0% of each run, Pallas kernels for 30% -> 31%
where the time goes in v5:
time: 129 us; the launch traced here: 127 us
  blocking collectives  48.6 us (38%)
  Pallas kernels  40.9 us (32%)
  waiting for transfers between devices  20.4 us (16%)
  starting transfers between devices  15.9 us (12%)
    all_to_all x1, blocking collectives, local(): lax.all_to_all(blocks, 'tensor', split_axis=0, concat_axis=0, tiled=True)  48.6 us
    pallas_call x18, Pallas kernels, whole_call(): pl.pallas_call(without_after, out_shape=out_shape, in_specs=[pl.BlockSpec...  29.3 us
    ppermute x14, waiting for transfers between devices, hop(): return lax.ppermute(value, 'tensor', pairs)  20.4 us
    ppermute x14, starting transfers between devices, hop(): return lax.ppermute(value, 'tensor', pairs)  15.9 us
    pallas_call x2, Pallas kernels, first_gather(): pl.pallas_call(lambda order_ref, rows_ref, *refs: kernel(order_ref, rows_...  6.3 us
    pallas_call x1, Pallas kernels, first_term(): pl.pallas_call(first_term_kernel, out_shape=[bf(k - TOP, d), bf(256, WB1)...  2.89 us
  transfers between devices with their start and end apart: 14, of which 8 were waited for; matrix products, arithmetic and copies ran while one was open for 0% of the time, Pallas kernels for 31%

profile of v5, /device:TPU:24, one launch (start us, length us, event | category | flops | bytes accessed | tf_op | source)
XLA Modules:
  0.0 126.9 jit_solution(17836695375905086678)
XLA Ops:
  0.7 3.8 %shard_map.68 = bf16[2048,896]{1,0:T(8,128)(2,1)} custom-call(bf16[128,14336]{1,0:T(8,128)(2,1)} %refs_0_.1), custom_call_target="tpu_custom_call" | custom-call | flops 734003 | tf_op jit(solution)/shard_map/pallas_call | solution.py:39
  4.6 48.6 %all_to_all.11 = bf16[16,128,896]{2,1,0:T(8,128)(2,1)} all-to-all(bf16[16,128,896]{2,1,0:T(8,128)(2,1)} %bitcast.35), channel_id=1, replica_groups=mesh['dp'=16,'tensor'=16] {'tensor'}, dimensions={0} | all-to-all | bytes 7340032 | tf_op jit(solution)/shard_map/all_to_all | solution.py:331
  53.4 3.2 %shard_map.69 = (bf16[2048,896]{1,0:T(8,128)(2,1)S(1)}, bf16[256,896]{1,0:T(8,128)(2,1)S(1)}) custom-call(s32[16,128]{1,0:T(8,128)S(1)} %bitcast.29, bf16[2048,896]{1,0:T(8,128)(2,1)} %bitcast.18.rows_ref, bf16[896,4096]{1,0:T(8,128)(2,1)} %collective-permute-done.refs_0_.w_ref), custom_call_target="tpu_custom_call" | custom-call | flops 187904816 | tf_op jit(solution)/shard_map/pallas_call | solution.py:129
  57.2 2.4 %shard_map.70 = (bf16[512,4096]{1,0:T(8,128)(2,1)S(1)}, bf16[256,896]{1,0:T(8,128)(2,1)S(1)}) custom-call(s32[16,128]{1,0:T(8,128)S(1)} %bitcast.30, bf16[2048,896]{1,0:T(8,128)(2,1)S(1)} %get-tuple-element.33.rows_ref.refs_1_, bf16[896,4096]{1,0:T(8,128)(2,1)} %collective-permute-done.refs_0_.w_ref, bf16[256,896]{1,0:T(8,128)(2,1)S(1)} %get-tuple-element.34.refs_0_), custom_call_target="tpu_custom_call" | custom-call | flops 187904816 | tf_op jit(solution)/shard_map/pallas_call | solution.py:161
  60.4 2.9 %shard_map.71 = (bf16[384,4096]{1,0:T(8,128)(2,1)S(1)}, bf16[256,1280]{1,0:T(8,128)(2,1)S(1)}, bf16[256,1024]{1,0:T(8,128)(2,1)S(1)}) custom-call(bf16[256,896]{1,0:T(8,128)(2,1)S(1)} %get-tuple-element.35.own_ref.refs_0_, bf16[256,896]{1,0:T(8,128)(2,1)S(1)} %collective-permute-done.1.sib_ref.refs_1_, bf16[896,4096]{1,0:T(8,128)(2,1)S(1)} %bitcast.28, ...), custom_call_target="tpu_custom_call" | custom-call | flops 422785856 | tf_op jit(solution)/shard_map/pallas_call | solution.py:198
  63.2 2.5 %collective-permute-start.3 = (bf16[256,1280]{1,0:T(8,128)(2,1)S(1)}, bf16[256,1280]{1,0:T(8,128)(2,1)S(1)}, u32[]{:S(2)}, u32[]{:S(2)}) collective-permute-start(bf16[256,1280]{1,0:T(8,128)(2,1)S(1)} %get-tuple-element.38.refs_5_), channel_id=1, source_target_pairs={{0,4},{1,5},{2,6},{3,7},{4,8},{5,9},{6,10},{7,11},{8,12},{9,13},{1... | collective-permute-start | bytes 1966088 | tf_op jit(solution)/shard_map/ppermute | solution.py:28
  65.7 2.1 %shard_map.72 = (bf16[128,1792]{1,0:T(8,128)(2,1)S(1)}, bf16[128,1792]{1,0:T(8,128)(2,1)S(1)}) custom-call(bf16[256,896]{1,0:T(8,128)(2,1)S(1)} %get-tuple-element.35.own_ref.refs_0_, bf16[256,896]{1,0:T(8,128)(2,1)S(1)} %collective-permute-done.1.sib_ref.refs_1_, bf16[896,4096]{1,0:T(8,128)(2,1)S(1)} %bitcast.28, ...), custom_call_target="tpu_custom_call" | custom-call | flops 328833440 | tf_op jit(solution)/shard_map/pallas_call | solution.py:39
  67.9 1.0 collective-permute-start.5
  68.9 1.5 %shard_map.73.refs_0_ = bf16[256,896]{1,0:T(8,128)(2,1)S(1)} custom-call(s32[16,128]{1,0:T(8,128)S(1)} %bitcast.31, bf16[2048,896]{1,0:T(8,128)(2,1)S(1)} %get-tuple-element.33.rows_ref.refs_1_, bf16[128,1792]{1,0:T(8,128)(2,1)S(1)} %get-tuple-element.39.refs_2_), custom_call_target="tpu_custom_call" | custom-call | flops 187904816 | tf_op jit(solution)/shard_map/pallas_call | solution.py:39
  70.4 3.1 %shard_map.74 = (bf16[2048,896]{1,0:T(8,128)(2,1)S(1)}, bf16[256,896]{1,0:T(8,128)(2,1)S(1)}) custom-call(s32[16,128]{1,0:T(8,128)S(1)} %bitcast.32, bf16[2048,896]{1,0:T(8,128)(2,1)} %collective-permute-done.2.rows_ref, bf16[256,896]{1,0:T(8,128)(2,1)S(1)} %shard_map.73.refs_0_), custom_call_target="tpu_custom_call" | custom-call | flops 187904816 | tf_op jit(solution)/shard_map/pallas_call | solution.py:129
  73.5 2.1 %shard_map.75.refs_5_ = bf16[256,1792]{1,0:T(8,128)(2,1)S(1)} custom-call(bf16[256,896]{1,0:T(8,128)(2,1)S(1)} %shard_map.73.refs_0_, bf16[256,896]{1,0:T(8,128)(2,1)S(1)} %get-tuple-element.40.refs_1_, bf16[896,4096]{1,0:T(8,128)(2,1)S(1)} %bitcast.28, bf16[512,4096]{1,0:T(8,128)(2,1)S(1)} %get-tuple-element.36.top_w.refs_3_, ...), custom_call_target="tpu_custom_call" | custom-call | flops 328833440 | tf_op jit(solution)/shard_map/pallas_call | solution.py:39
  75.6 1.3 %collective-permute-start.8 = (bf16[256,1792]{1,0:T(8,128)(2,1)S(1)}, bf16[256,1792]{1,0:T(8,128)(2,1)S(1)}, u32[]{:S(2)}, u32[]{:S(2)}) collective-permute-start(bf16[256,1792]{1,0:T(8,128)(2,1)S(1)} %shard_map.75.refs_5_), channel_id=1, source_target_pairs={{0,2},{1,3},{2,0},{3,1},{4,6},{5,7},{6,4},{7,5},{8,10},{9,11},{10,... | collective-permute-start | bytes 2752520 | tf_op jit(solution)/shard_map/ppermute | solution.py:28
  76.9 2.7 %shard_map.76 = (bf16[128,2304]{1,0:T(8,128)(2,1)S(1)}, bf16[128,2304]{1,0:T(8,128)(2,1)S(1)}) custom-call(bf16[256,896]{1,0:T(8,128)(2,1)S(1)} %shard_map.73.refs_0_, bf16[256,896]{1,0:T(8,128)(2,1)S(1)} %get-tuple-element.40.refs_1_, bf16[896,4096]{1,0:T(8,128)(2,1)S(1)} %bitcast.28, bf16[512,4096]{1,0:T(8,128)(2,1)S(1)} %get-tuple-element.36.top_w.refs_3_, ...), custom_call_target="tpu_custom_call" | custom-call | flops 422785856 | tf_op jit(solution)/shard_map/pallas_call | solution.py:39
  82.0 3.4 %collective-permute-start.10 = (bf16[128,3072]{1,0:T(8,128)(2,1)S(1)}, bf16[128,3072]{1,0:T(8,128)(2,1)S(1)}, u32[]{:S(2)}, u32[]{:S(2)}) collective-permute-start(bf16[128,3072]{1,0:T(8,128)(2,1)S(1)} %get-tuple-element.60), channel_id=1, source_target_pairs={{0,4},{1,5},{2,6},{3,7},{4,8},{5,9},{6,10},{7,11},{8,12},{9,13},{1... | collective-permute-start | bytes 2359304 | tf_op jit(solution)/shard_map/ppermute | solution.py:28
  85.4 2.6 %shard_map.79.refs_2_.refs_0_ = bf16[512,896]{1,0:T(8,128)(2,1)S(1)} custom-call(s32[16,128]{1,0:T(8,128)S(1)} %bitcast.33, bf16[2048,896]{1,0:T(8,128)(2,1)S(1)} %get-tuple-element.33.rows_ref.refs_1_, bf16[128,3328]{1,0:T(8,128)(2,1)S(1)} %get-tuple-element.47.refs_2_), custom_call_target="tpu_custom_call" | custom-call | flops 375809632 | tf_op jit(solution)/shard_map/pallas_call | solution.py:39
  88.0 2.6 %shard_map.80.refs_1_ = bf16[512,896]{1,0:T(8,128)(2,1)S(1)} custom-call(s32[16,128]{1,0:T(8,128)S(1)} %bitcast.34, bf16[2048,896]{1,0:T(8,128)(2,1)S(1)} %get-tuple-element.48.refs_1_, bf16[512,896]{1,0:T(8,128)(2,1)S(1)} %shard_map.79.refs_2_.refs_0_), custom_call_target="tpu_custom_call" | custom-call | flops 375809632 | tf_op jit(solution)/shard_map/pallas_call | solution.py:39
  90.5 4.6 %shard_map.81 = (bf16[128,1792]{1,0:T(8,128)(2,1)S(1)}, bf16[128,1792]{1,0:T(8,128)(2,1)S(1)}, bf16[128,2304]{1,0:T(8,128)(2,1)S(1)}, bf16[128,2304]{1,0:T(8,128)(2,1)S(1)}) custom-call(bf16[512,896]{1,0:T(8,128)(2,1)S(1)} %shard_map.79.refs_2_.refs_0_, bf16[512,896]{1,0:T(8,128)(2,1)S(1)} %shard_map.80.refs_1_, bf16[896,4096]{1,0:T(8,128)(2,1)S(1)} %bitcast.28, ...), custom_call_target="tpu_custom_call" | custom-call | flops 751619264 | tf_op jit(solution)/shard_map/pallas_call | solution.py:39
  95.2 4.6 %shard_map.82 = (bf16[128,1792]{1,0:T(8,128)(2,1)S(1)}, bf16[128,1792]{1,0:T(8,128)(2,1)S(1)}, bf16[128,2304]{1,0:T(8,128)(2,1)S(1)}, bf16[128,2304]{1,0:T(8,128)(2,1)S(1)}) custom-call(bf16[512,896]{1,0:T(8,128)(2,1)S(1)} %shard_map.79.refs_2_.refs_0_, bf16[512,896]{1,0:T(8,128)(2,1)S(1)} %shard_map.80.refs_1_, bf16[896,4096]{1,0:T(8,128)(2,1)S(1)} %bitcast.28, ...), custom_call_target="tpu_custom_call" | custom-call | flops 751619264 | tf_op jit(solution)/shard_map/pallas_call | solution.py:39
  99.9 1.8 %collective-permute-start.6 = (bf16[128,2304]{1,0:T(8,128)(2,1)S(1)}, bf16[128,2304]{1,0:T(8,128)(2,1)S(1)}, u32[]{:S(2)}, u32[]{:S(2)}) collective-permute-start(bf16[128,2304]{1,0:T(8,128)(2,1)S(1)} %get-tuple-element.55.refs_3_), channel_id=1, source_target_pairs={{0,4},{1,5},{2,6},{3,7},{4,8},{5,9},{6,10},{7,11},{8,12},{9,13},{1... | collective-permute-start | bytes 1769480 | tf_op jit(solution)/shard_map/ppermute | solution.py:28
  103.7 3.6 %collective-permute-start.12 = (bf16[128,1792]{1,0:T(8,128)(2,1)S(1)}, bf16[128,1792]{1,0:T(8,128)(2,1)S(1)}, u32[]{:S(2)}, u32[]{:S(2)}) collective-permute-start(bf16[128,1792]{1,0:T(8,128)(2,1)S(1)} %shard_map.86.refs_2_), channel_id=1, source_target_pairs={{0,4},{1,5},{2,6},{3,7},{4,8},{5,9},{6,10},{7,11},{8,12},{9,13},{1... | collective-permute-start | bytes 1376264 | tf_op jit(solution)/shard_map/ppermute | solution.py:28
  107.4 8.8 %collective-permute-done.6.refs_2_ = bf16[128,2304]{1,0:T(8,128)(2,1)S(1)} collective-permute-done((bf16[128,2304]{1,0:T(8,128)(2,1)S(1)}, bf16[128,2304]{1,0:T(8,128)(2,1)S(1)}, u32[]{:S(2)}, u32[]{:S(2)}) %collective-permute-start.6) | collective-permute-done | bytes 589856 | tf_op jit(solution)/shard_map/ppermute | solution.py:28
  116.3 2.9 %collective-permute-done.7.refs_3_ = bf16[128,2304]{1,0:T(8,128)(2,1)S(1)} collective-permute-done((bf16[128,2304]{1,0:T(8,128)(2,1)S(1)}, bf16[128,2304]{1,0:T(8,128)(2,1)S(1)}, u32[]{:S(2)}, u32[]{:S(2)}) %collective-permute-start.7) | collective-permute-done | bytes 589856 | tf_op jit(solution)/shard_map/ppermute | solution.py:28
  119.6 5.9 %collective-permute-done.13.refs_3_ = bf16[128,1792]{1,0:T(8,128)(2,1)S(1)} collective-permute-done((bf16[128,1792]{1,0:T(8,128)(2,1)S(1)}, bf16[128,1792]{1,0:T(8,128)(2,1)S(1)}, u32[]{:S(2)}, u32[]{:S(2)}) %collective-permute-start.13) | collective-permute-done | bytes 458784 | tf_op jit(solution)/shard_map/ppermute | solution.py:28
  125.5 1.4 %shard_map.89 = (bf16[128,4096]{1,0:T(8,128)(2,1)}, f32[1,128]{1,0:T(1,128)}) custom-call(f32[128,4096]{1,0:T(8,128)S(1)} %shard_map.88.refs_0_, bf16[128,4096]{1,0:T(8,128)(2,1)S(1)} %collective-permute-done.11.refs_1_, bf16[128,1792]{1,0:T(8,128)(2,1)S(1)} %collective-permute-done.12.refs_2_, bf16[128,1792]{1,0:T(8,128)(2,1)S(1)} %collective-permute-done.13.refs_3_, ...), custom_call_target="tpu_custom_call" | custom-call | flops 814284 | tf_op jit(solution)/shard_map/pallas_call | solution.py:39
  (45 shorter events, 6.7 us)
Async XLA Ops:
  0.6 52.7 %collective-permute-start = (bf16[896,4096]{1,0:T(8,128)(2,1)}, bf16[896,4096]{1,0:T(8,128)(2,1)}, u32[]{:S(2)}, u32[]{:S(2)}) collective-permute-start(bf16[896,4096]{1,0:T(8,128)(2,1)} %refs_2_.9), channel_id=1, source_target_pairs={{0,1},{1,0},{2,3},{3,2},{4,5},{5,4},{6,7},{7,6},{8,9},{9,8},{10,11... | collective-permute-start | bytes 22020104 | tf_op jit(solution)/shard_map/ppermute | solution.py:28
  4.6 48.7 %copy-start.2 = (s32[2048]{0:T(1024)S(1)}, s32[2048]{0:T(1024)}, u32[]{:S(2)}) copy-start(s32[2048]{0:T(1024)} %param.8) | copy-start | bytes 24580
  53.2 17.1 %collective-permute-start.2 = (bf16[2048,896]{1,0:T(8,128)(2,1)}, bf16[2048,896]{1,0:T(8,128)(2,1)}, u32[]{:S(2)}, u32[]{:S(2)}) collective-permute-start(bf16[2048,896]{1,0:T(8,128)(2,1)} %bitcast.18.rows_ref), channel_id=1, source_target_pairs={{0,1},{1,0},{2,3},{3,2},{4,5},{5,4},{6,7},{7,6},{8,9},{9,8},{10,11... | collective-permute-start | bytes 11010056 | tf_op jit(solution)/shard_map/ppermute | solution.py:28
  53.4 6.9 %slice-start = ((s8[7340032]{0:T(1024)(128)(4,1)}), s8[4194304]{0:T(1024)(128)(4,1)S(1)}, s32[]{:S(2)}) async-start(s8[7340032]{0:T(1024)(128)(4,1)} %bitcast.27), calls=%async_computation.1 | async-start | bytes 8388608
  56.6 3.7 %collective-permute-start.1 = (bf16[256,896]{1,0:T(8,128)(2,1)S(1)}, bf16[256,896]{1,0:T(8,128)(2,1)S(1)}, u32[]{:S(2)}, u32[]{:S(2)}) collective-permute-start(bf16[256,896]{1,0:T(8,128)(2,1)S(1)} %get-tuple-element.34.refs_0_), channel_id=1, source_target_pairs={{0,1},{1,0},{2,3},{3,2},{4,5},{5,4},{6,7},{7,6},{8,9},{9,8},{10,11... | collective-permute-start | bytes 1376264 | tf_op jit(solution)/shard_map/ppermute | solution.py:28
  57.2 3.2 %slice-start.1 = ((s8[7340032]{0:T(1024)(128)(4,1)}), s8[3145728]{0:T(1024)(128)(4,1)S(1)}, s32[]{:S(2)}) async-start(s8[7340032]{0:T(1024)(128)(4,1)} %bitcast.27), calls=%async_computation.2 | async-start | bytes 6291456
  63.2 17.3 %collective-permute-start.3 = (bf16[256,1280]{1,0:T(8,128)(2,1)S(1)}, bf16[256,1280]{1,0:T(8,128)(2,1)S(1)}, u32[]{:S(2)}, u32[]{:S(2)}) collective-permute-start(bf16[256,1280]{1,0:T(8,128)(2,1)S(1)} %get-tuple-element.38.refs_5_), channel_id=1, source_target_pairs={{0,4},{1,5},{2,6},{3,7},{4,8},{5,9},{6,10},{7,11},{8,12},{9,13},{1... | collective-permute-start | bytes 1966088 | tf_op jit(solution)/shard_map/ppermute | solution.py:28
  65.7 14.8 %collective-permute-start.4 = (bf16[256,1024]{1,0:T(8,128)(2,1)S(1)}, bf16[256,1024]{1,0:T(8,128)(2,1)S(1)}, u32[]{:S(2)}, u32[]{:S(2)}) collective-permute-start(bf16[256,1024]{1,0:T(8,128)(2,1)S(1)} %get-tuple-element.43), channel_id=1, source_target_pairs={{0,12},{1,13},{2,14},{3,15},{4,0},{5,1},{6,2},{7,3},{8,4},{9,5},{1... | collective-permute-start | bytes 1572872 | tf_op jit(solution)/shard_map/ppermute | solution.py:28
  67.9 13.7 %collective-permute-start.5 = (bf16[128,1792]{1,0:T(8,128)(2,1)S(1)}, bf16[128,1792]{1,0:T(8,128)(2,1)S(1)}, u32[]{:S(2)}, u32[]{:S(2)}) collective-permute-start(bf16[128,1792]{1,0:T(8,128)(2,1)S(1)} %get-tuple-element.39.refs_2_), channel_id=1, source_target_pairs={{0,2},{1,3},{2,0},{3,1},{4,6},{5,7},{6,4},{7,5},{8,10},{9,11},{10,... | collective-permute-start | bytes 1376264 | tf_op jit(solution)/shard_map/ppermute | solution.py:28
  75.6 26.5 %collective-permute-start.8 = (bf16[256,1792]{1,0:T(8,128)(2,1)S(1)}, bf16[256,1792]{1,0:T(8,128)(2,1)S(1)}, u32[]{:S(2)}, u32[]{:S(2)}) collective-permute-start(bf16[256,1792]{1,0:T(8,128)(2,1)S(1)} %shard_map.75.refs_5_), channel_id=1, source_target_pairs={{0,2},{1,3},{2,0},{3,1},{4,6},{5,7},{6,4},{7,5},{8,10},{9,11},{10,... | collective-permute-start | bytes 2752520 | tf_op jit(solution)/shard_map/ppermute | solution.py:28
  81.7 20.7 %collective-permute-start.9 = (bf16[128,3328]{1,0:T(8,128)(2,1)S(1)}, bf16[128,3328]{1,0:T(8,128)(2,1)S(1)}, u32[]{:S(2)}, u32[]{:S(2)}) collective-permute-start(bf16[128,3328]{1,0:T(8,128)(2,1)S(1)} %get-tuple-element.47.refs_2_), channel_id=1, source_target_pairs={{0,12},{1,13},{2,14},{3,15},{4,0},{5,1},{6,2},{7,3},{8,4},{9,5},{1... | collective-permute-start | bytes 2555912 | tf_op jit(solution)/shard_map/ppermute | solution.py:28
  82.0 20.3 %collective-permute-start.10 = (bf16[128,3072]{1,0:T(8,128)(2,1)S(1)}, bf16[128,3072]{1,0:T(8,128)(2,1)S(1)}, u32[]{:S(2)}, u32[]{:S(2)}) collective-permute-start(bf16[128,3072]{1,0:T(8,128)(2,1)S(1)} %get-tuple-element.60), channel_id=1, source_target_pairs={{0,4},{1,5},{2,6},{3,7},{4,8},{5,9},{6,10},{7,11},{8,12},{9,13},{1... | collective-permute-start | bytes 2359304 | tf_op jit(solution)/shard_map/ppermute | solution.py:28
  95.1 6.9 %copy-start.1 = (bf16[4096]{0:T(1024)(128)(2,1)S(1)}, bf16[4096]{0:T(1024)(128)(2,1)}, u32[]{:S(2)}) copy-start(bf16[4096]{0:T(1024)(128)(2,1)} %param.9) | copy-start | bytes 24580
  99.9 16.3 %collective-permute-start.6 = (bf16[128,2304]{1,0:T(8,128)(2,1)S(1)}, bf16[128,2304]{1,0:T(8,128)(2,1)S(1)}, u32[]{:S(2)}, u32[]{:S(2)}) collective-permute-start(bf16[128,2304]{1,0:T(8,128)(2,1)S(1)} %get-tuple-element.55.refs_3_), channel_id=1, source_target_pairs={{0,4},{1,5},{2,6},{3,7},{4,8},{5,9},{6,10},{7,11},{8,12},{9,13},{1... | collective-permute-start | bytes 1769480 | tf_op jit(solution)/shard_map/ppermute | solution.py:28
  101.7 17.5 %collective-permute-start.7 = (bf16[128,2304]{1,0:T(8,128)(2,1)S(1)}, bf16[128,2304]{1,0:T(8,128)(2,1)S(1)}, u32[]{:S(2)}, u32[]{:S(2)}) collective-permute-start(bf16[128,2304]{1,0:T(8,128)(2,1)S(1)} %get-tuple-element.56), channel_id=1, source_target_pairs={{0,12},{1,13},{2,14},{3,15},{4,0},{5,1},{6,2},{7,3},{8,4},{9,5},{1... | collective-permute-start | bytes 1769480 | tf_op jit(solution)/shard_map/ppermute | solution.py:28
  102.7 16.5 %copy-start = (bf16[128,4096]{1,0:T(8,128)(2,1)S(1)}, bf16[128,4096]{1,0:T(8,128)(2,1)}, u32[]{:S(2)}) copy-start(bf16[128,4096]{1,0:T(8,128)(2,1)} %refs_4_.1) | copy-start | bytes 3145732
  102.7 22.8 %collective-permute-start.11 = (bf16[128,4096]{1,0:T(8,128)(2,1)S(1)}, bf16[128,4096]{1,0:T(8,128)(2,1)S(1)}, u32[]{:S(2)}, u32[]{:S(2)}) collective-permute-start(bf16[128,4096]{1,0:T(8,128)(2,1)S(1)} %shard_map.85.refs_2_), channel_id=1, source_target_pairs={{0,2},{1,3},{2,0},{3,1},{4,6},{5,7},{6,4},{7,5},{8,10},{9,11},{10,... | collective-permute-start | bytes 3145736 | tf_op jit(solution)/shard_map/ppermute | solution.py:28
  103.7 21.7 %collective-permute-start.12 = (bf16[128,1792]{1,0:T(8,128)(2,1)S(1)}, bf16[128,1792]{1,0:T(8,128)(2,1)S(1)}, u32[]{:S(2)}, u32[]{:S(2)}) collective-permute-start(bf16[128,1792]{1,0:T(8,128)(2,1)S(1)} %shard_map.86.refs_2_), channel_id=1, source_target_pairs={{0,4},{1,5},{2,6},{3,7},{4,8},{5,9},{6,10},{7,11},{8,12},{9,13},{1... | collective-permute-start | bytes 1376264 | tf_op jit(solution)/shard_map/ppermute | solution.py:28
  107.4 18.1 %collective-permute-start.13 = (bf16[128,1792]{1,0:T(8,128)(2,1)S(1)}, bf16[128,1792]{1,0:T(8,128)(2,1)S(1)}, u32[]{:S(2)}, u32[]{:S(2)}) collective-permute-start(bf16[128,1792]{1,0:T(8,128)(2,1)S(1)} %shard_map.87.refs_5_), channel_id=1, source_target_pairs={{0,12},{1,13},{2,14},{3,15},{4,0},{5,1},{6,2},{7,3},{8,4},{9,5},{1... | collective-permute-start | bytes 1376264 | tf_op jit(solution)/shard_map/ppermute | solution.py:28

commit v6 on v5

--- a/solution.py
+++ b/solution.py
@@ -12,7 +12,7 @@
 A_TILES, B1_TILES, B2_TILES = 7, 5, 4
 WA, WB1, WB2 = A_TILES * TILE, B1_TILES * TILE, B2_TILES * TILE
 WB = WB1 + WB2
-WA1 = 3 * TILE
+WA1 = 4 * TILE
 TOP = 512
 MIB = 1 << 20
 

time: 129 us -> 130 us (level)
  transfers between devices with their start and end apart: 14 -> 14, of which waited for: 8 -> 7; matrix products, arithmetic and copies ran while one was open for 0% -> 0% of each run, Pallas kernels for 31% -> 31%
where the time goes in v6:
time: 130 us; the launch traced here: 128 us
  blocking collectives  48.6 us (37%)
  Pallas kernels  40.9 us (31%)
  waiting for transfers between devices  21.5 us (17%)
  starting transfers between devices  15.9 us (12%)
    all_to_all x1, blocking collectives, local(): lax.all_to_all(blocks, 'tensor', split_axis=0, concat_axis=0, tiled=True)  48.6 us
    pallas_call x18, Pallas kernels, whole_call(): pl.pallas_call(without_after, out_shape=out_shape, in_specs=[pl.BlockSpec...  29.4 us
    ppermute x14, waiting for transfers between devices, hop(): return lax.ppermute(value, 'tensor', pairs)  21.5 us
    ppermute x14, starting transfers between devices, hop(): return lax.ppermute(value, 'tensor', pairs)  15.9 us
    pallas_call x2, Pallas kernels, first_gather(): pl.pallas_call(lambda order_ref, rows_ref, *refs: kernel(order_ref, rows_...  6.3 us
    pallas_call x1, Pallas kernels, first_term(): pl.pallas_call(first_term_kernel, out_shape=[bf(k - TOP, d), bf(256, WB1)...  2.89 us
  transfers between devices with their start and end apart: 14, of which 7 were waited for; matrix products, arithmetic and copies ran while one was open for 0% of the time, Pallas kernels for 31%

profile of v6, /device:TPU:24, one launch (start us, length us, event | category | flops | bytes accessed | tf_op | source)
XLA Modules:
  0.0 128.1 jit_solution(15010497817178656972)
XLA Ops:
  0.7 3.8 %shard_map.68 = bf16[2048,896]{1,0:T(8,128)(2,1)} custom-call(bf16[128,14336]{1,0:T(8,128)(2,1)} %refs_0_.1), custom_call_target="tpu_custom_call" | custom-call | flops 734003 | tf_op jit(solution)/shard_map/pallas_call | solution.py:39
  4.6 48.6 %all_to_all.11 = bf16[16,128,896]{2,1,0:T(8,128)(2,1)} all-to-all(bf16[16,128,896]{2,1,0:T(8,128)(2,1)} %bitcast.35), channel_id=1, replica_groups=mesh['dp'=16,'tensor'=16] {'tensor'}, dimensions={0} | all-to-all | bytes 7340032 | tf_op jit(solution)/shard_map/all_to_all | solution.py:331
  53.4 3.2 %shard_map.69 = (bf16[2048,896]{1,0:T(8,128)(2,1)S(1)}, bf16[256,896]{1,0:T(8,128)(2,1)S(1)}) custom-call(s32[16,128]{1,0:T(8,128)S(1)} %bitcast.29, bf16[2048,896]{1,0:T(8,128)(2,1)} %bitcast.18.rows_ref, bf16[896,4096]{1,0:T(8,128)(2,1)} %collective-permute-done.refs_0_.w_ref), custom_call_target="tpu_custom_call" | custom-call | flops 187904816 | tf_op jit(solution)/shard_map/pallas_call | solution.py:129
  57.2 2.4 %shard_map.70 = (bf16[512,4096]{1,0:T(8,128)(2,1)S(1)}, bf16[256,896]{1,0:T(8,128)(2,1)S(1)}) custom-call(s32[16,128]{1,0:T(8,128)S(1)} %bitcast.30, bf16[2048,896]{1,0:T(8,128)(2,1)S(1)} %get-tuple-element.33.rows_ref.refs_1_, bf16[896,4096]{1,0:T(8,128)(2,1)} %collective-permute-done.refs_0_.w_ref, bf16[256,896]{1,0:T(8,128)(2,1)S(1)} %get-tuple-element.34.refs_0_), custom_call_target="tpu_custom_call" | custom-call | flops 187904816 | tf_op jit(solution)/shard_map/pallas_call | solution.py:161
  60.4 2.9 %shard_map.71 = (bf16[384,4096]{1,0:T(8,128)(2,1)S(1)}, bf16[256,1280]{1,0:T(8,128)(2,1)S(1)}, bf16[256,1024]{1,0:T(8,128)(2,1)S(1)}) custom-call(bf16[256,896]{1,0:T(8,128)(2,1)S(1)} %get-tuple-element.35.own_ref.refs_0_, bf16[256,896]{1,0:T(8,128)(2,1)S(1)} %collective-permute-done.1.sib_ref.refs_1_, bf16[896,4096]{1,0:T(8,128)(2,1)S(1)} %bitcast.28, ...), custom_call_target="tpu_custom_call" | custom-call | flops 422785856 | tf_op jit(solution)/shard_map/pallas_call | solution.py:198
  63.2 2.5 %collective-permute-start.3 = (bf16[256,1280]{1,0:T(8,128)(2,1)S(1)}, bf16[256,1280]{1,0:T(8,128)(2,1)S(1)}, u32[]{:S(2)}, u32[]{:S(2)}) collective-permute-start(bf16[256,1280]{1,0:T(8,128)(2,1)S(1)} %get-tuple-element.38.refs_5_), channel_id=1, source_target_pairs={{0,4},{1,5},{2,6},{3,7},{4,8},{5,9},{6,10},{7,11},{8,12},{9,13},{1... | collective-permute-start | bytes 1966088 | tf_op jit(solution)/shard_map/ppermute | solution.py:28
  65.7 2.1 %shard_map.72 = (bf16[128,1792]{1,0:T(8,128)(2,1)S(1)}, bf16[128,1792]{1,0:T(8,128)(2,1)S(1)}) custom-call(bf16[256,896]{1,0:T(8,128)(2,1)S(1)} %get-tuple-element.35.own_ref.refs_0_, bf16[256,896]{1,0:T(8,128)(2,1)S(1)} %collective-permute-done.1.sib_ref.refs_1_, bf16[896,4096]{1,0:T(8,128)(2,1)S(1)} %bitcast.28, ...), custom_call_target="tpu_custom_call" | custom-call | flops 328833440 | tf_op jit(solution)/shard_map/pallas_call | solution.py:39
  67.9 1.0 collective-permute-start.5
  68.9 1.5 %shard_map.73.refs_0_ = bf16[256,896]{1,0:T(8,128)(2,1)S(1)} custom-call(s32[16,128]{1,0:T(8,128)S(1)} %bitcast.31, bf16[2048,896]{1,0:T(8,128)(2,1)S(1)} %get-tuple-element.33.rows_ref.refs_1_, bf16[128,1792]{1,0:T(8,128)(2,1)S(1)} %get-tuple-element.39.refs_2_), custom_call_target="tpu_custom_call" | custom-call | flops 187904816 | tf_op jit(solution)/shard_map/pallas_call | solution.py:39
  70.4 3.1 %shard_map.74 = (bf16[2048,896]{1,0:T(8,128)(2,1)S(1)}, bf16[256,896]{1,0:T(8,128)(2,1)S(1)}) custom-call(s32[16,128]{1,0:T(8,128)S(1)} %bitcast.32, bf16[2048,896]{1,0:T(8,128)(2,1)} %collective-permute-done.2.rows_ref, bf16[256,896]{1,0:T(8,128)(2,1)S(1)} %shard_map.73.refs_0_), custom_call_target="tpu_custom_call" | custom-call | flops 187904816 | tf_op jit(solution)/shard_map/pallas_call | solution.py:129
  73.5 2.1 %shard_map.75.refs_5_ = bf16[256,1792]{1,0:T(8,128)(2,1)S(1)} custom-call(bf16[256,896]{1,0:T(8,128)(2,1)S(1)} %shard_map.73.refs_0_, bf16[256,896]{1,0:T(8,128)(2,1)S(1)} %get-tuple-element.40.refs_1_, bf16[896,4096]{1,0:T(8,128)(2,1)S(1)} %bitcast.28, bf16[512,4096]{1,0:T(8,128)(2,1)S(1)} %get-tuple-element.36.top_w.refs_3_, ...), custom_call_target="tpu_custom_call" | custom-call | flops 328833440 | tf_op jit(solution)/shard_map/pallas_call | solution.py:39
  75.6 1.3 %collective-permute-start.8 = (bf16[256,1792]{1,0:T(8,128)(2,1)S(1)}, bf16[256,1792]{1,0:T(8,128)(2,1)S(1)}, u32[]{:S(2)}, u32[]{:S(2)}) collective-permute-start(bf16[256,1792]{1,0:T(8,128)(2,1)S(1)} %shard_map.75.refs_5_), channel_id=1, source_target_pairs={{0,2},{1,3},{2,0},{3,1},{4,6},{5,7},{6,4},{7,5},{8,10},{9,11},{10,... | collective-permute-start | bytes 2752520 | tf_op jit(solution)/shard_map/ppermute | solution.py:28
  76.9 2.7 %shard_map.76 = (bf16[128,2304]{1,0:T(8,128)(2,1)S(1)}, bf16[128,2304]{1,0:T(8,128)(2,1)S(1)}) custom-call(bf16[256,896]{1,0:T(8,128)(2,1)S(1)} %shard_map.73.refs_0_, bf16[256,896]{1,0:T(8,128)(2,1)S(1)} %get-tuple-element.40.refs_1_, bf16[896,4096]{1,0:T(8,128)(2,1)S(1)} %bitcast.28, bf16[512,4096]{1,0:T(8,128)(2,1)S(1)} %get-tuple-element.36.top_w.refs_3_, ...), custom_call_target="tpu_custom_call" | custom-call | flops 422785856 | tf_op jit(solution)/shard_map/pallas_call | solution.py:39
  81.7 3.3 %collective-permute-start.10 = (bf16[128,3328]{1,0:T(8,128)(2,1)S(1)}, bf16[128,3328]{1,0:T(8,128)(2,1)S(1)}, u32[]{:S(2)}, u32[]{:S(2)}) collective-permute-start(bf16[128,3328]{1,0:T(8,128)(2,1)S(1)} %get-tuple-element.60), channel_id=1, source_target_pairs={{0,4},{1,5},{2,6},{3,7},{4,8},{5,9},{6,10},{7,11},{8,12},{9,13},{1... | collective-permute-start | bytes 2555912 | tf_op jit(solution)/shard_map/ppermute | solution.py:28
  85.1 2.6 %shard_map.79.refs_2_.refs_0_ = bf16[512,896]{1,0:T(8,128)(2,1)S(1)} custom-call(s32[16,128]{1,0:T(8,128)S(1)} %bitcast.33, bf16[2048,896]{1,0:T(8,128)(2,1)S(1)} %get-tuple-element.33.rows_ref.refs_1_, bf16[128,3072]{1,0:T(8,128)(2,1)S(1)} %get-tuple-element.47.refs_2_), custom_call_target="tpu_custom_call" | custom-call | flops 375809632 | tf_op jit(solution)/shard_map/pallas_call | solution.py:39
  87.6 2.6 %shard_map.80.refs_1_ = bf16[512,896]{1,0:T(8,128)(2,1)S(1)} custom-call(s32[16,128]{1,0:T(8,128)S(1)} %bitcast.34, bf16[2048,896]{1,0:T(8,128)(2,1)S(1)} %get-tuple-element.48.refs_1_, bf16[512,896]{1,0:T(8,128)(2,1)S(1)} %shard_map.79.refs_2_.refs_0_), custom_call_target="tpu_custom_call" | custom-call | flops 375809632 | tf_op jit(solution)/shard_map/pallas_call | solution.py:39
  90.2 4.6 %shard_map.81 = (bf16[128,1792]{1,0:T(8,128)(2,1)S(1)}, bf16[128,1792]{1,0:T(8,128)(2,1)S(1)}, bf16[128,2304]{1,0:T(8,128)(2,1)S(1)}, bf16[128,2304]{1,0:T(8,128)(2,1)S(1)}) custom-call(bf16[512,896]{1,0:T(8,128)(2,1)S(1)} %shard_map.79.refs_2_.refs_0_, bf16[512,896]{1,0:T(8,128)(2,1)S(1)} %shard_map.80.refs_1_, bf16[896,4096]{1,0:T(8,128)(2,1)S(1)} %bitcast.28, ...), custom_call_target="tpu_custom_call" | custom-call | flops 751619264 | tf_op jit(solution)/shard_map/pallas_call | solution.py:39
  94.9 4.6 %shard_map.82 = (bf16[128,1792]{1,0:T(8,128)(2,1)S(1)}, bf16[128,1792]{1,0:T(8,128)(2,1)S(1)}, bf16[128,2304]{1,0:T(8,128)(2,1)S(1)}, bf16[128,2304]{1,0:T(8,128)(2,1)S(1)}) custom-call(bf16[512,896]{1,0:T(8,128)(2,1)S(1)} %shard_map.79.refs_2_.refs_0_, bf16[512,896]{1,0:T(8,128)(2,1)S(1)} %shard_map.80.refs_1_, bf16[896,4096]{1,0:T(8,128)(2,1)S(1)} %bitcast.28, ...), custom_call_target="tpu_custom_call" | custom-call | flops 751619264 | tf_op jit(solution)/shard_map/pallas_call | solution.py:39
  99.6 3.3 %collective-permute-start.6 = (bf16[128,2304]{1,0:T(8,128)(2,1)S(1)}, bf16[128,2304]{1,0:T(8,128)(2,1)S(1)}, u32[]{:S(2)}, u32[]{:S(2)}) collective-permute-start(bf16[128,2304]{1,0:T(8,128)(2,1)S(1)} %get-tuple-element.55.refs_3_), channel_id=1, source_target_pairs={{0,4},{1,5},{2,6},{3,7},{4,8},{5,9},{6,10},{7,11},{8,12},{9,13},{1... | collective-permute-start | bytes 1769480 | tf_op jit(solution)/shard_map/ppermute | solution.py:28
  105.0 2.7 %collective-permute-start.12 = (bf16[128,1792]{1,0:T(8,128)(2,1)S(1)}, bf16[128,1792]{1,0:T(8,128)(2,1)S(1)}, u32[]{:S(2)}, u32[]{:S(2)}) collective-permute-start(bf16[128,1792]{1,0:T(8,128)(2,1)S(1)} %shard_map.86.refs_2_), channel_id=1, source_target_pairs={{0,4},{1,5},{2,6},{3,7},{4,8},{5,9},{6,10},{7,11},{8,12},{9,13},{1... | collective-permute-start | bytes 1376264 | tf_op jit(solution)/shard_map/ppermute | solution.py:28
  107.8 8.9 %collective-permute-done.6.refs_2_ = bf16[128,2304]{1,0:T(8,128)(2,1)S(1)} collective-permute-done((bf16[128,2304]{1,0:T(8,128)(2,1)S(1)}, bf16[128,2304]{1,0:T(8,128)(2,1)S(1)}, u32[]{:S(2)}, u32[]{:S(2)}) %collective-permute-start.6) | collective-permute-done | bytes 589856 | tf_op jit(solution)/shard_map/ppermute | solution.py:28
  116.7 3.7 %collective-permute-done.7.refs_3_ = bf16[128,2304]{1,0:T(8,128)(2,1)S(1)} collective-permute-done((bf16[128,2304]{1,0:T(8,128)(2,1)S(1)}, bf16[128,2304]{1,0:T(8,128)(2,1)S(1)}, u32[]{:S(2)}, u32[]{:S(2)}) %collective-permute-start.7) | collective-permute-done | bytes 589856 | tf_op jit(solution)/shard_map/ppermute | solution.py:28
  120.8 5.9 %collective-permute-done.13.refs_3_ = bf16[128,1792]{1,0:T(8,128)(2,1)S(1)} collective-permute-done((bf16[128,1792]{1,0:T(8,128)(2,1)S(1)}, bf16[128,1792]{1,0:T(8,128)(2,1)S(1)}, u32[]{:S(2)}, u32[]{:S(2)}) %collective-permute-start.13) | collective-permute-done | bytes 458784 | tf_op jit(solution)/shard_map/ppermute | solution.py:28
  126.7 1.4 %shard_map.89 = (bf16[128,4096]{1,0:T(8,128)(2,1)}, f32[1,128]{1,0:T(1,128)}) custom-call(f32[128,4096]{1,0:T(8,128)S(1)} %shard_map.88.refs_0_, bf16[128,4096]{1,0:T(8,128)(2,1)S(1)} %collective-permute-done.11.refs_1_, bf16[128,1792]{1,0:T(8,128)(2,1)S(1)} %collective-permute-done.12.refs_2_, bf16[128,1792]{1,0:T(8,128)(2,1)S(1)} %collective-permute-done.13.refs_3_, ...), custom_call_target="tpu_custom_call" | custom-call | flops 814284 | tf_op jit(solution)/shard_map/pallas_call | solution.py:39
  (45 shorter events, 6.4 us)
Async XLA Ops:
  0.6 52.7 %collective-permute-start = (bf16[896,4096]{1,0:T(8,128)(2,1)}, bf16[896,4096]{1,0:T(8,128)(2,1)}, u32[]{:S(2)}, u32[]{:S(2)}) collective-permute-start(bf16[896,4096]{1,0:T(8,128)(2,1)} %refs_2_.9), channel_id=1, source_target_pairs={{0,1},{1,0},{2,3},{3,2},{4,5},{5,4},{6,7},{7,6},{8,9},{9,8},{10,11... | collective-permute-start | bytes 22020104 | tf_op jit(solution)/shard_map/ppermute | solution.py:28
  4.6 48.7 %copy-start.2 = (s32[2048]{0:T(1024)S(1)}, s32[2048]{0:T(1024)}, u32[]{:S(2)}) copy-start(s32[2048]{0:T(1024)} %param.8) | copy-start | bytes 24580
  53.2 17.1 %collective-permute-start.2 = (bf16[2048,896]{1,0:T(8,128)(2,1)}, bf16[2048,896]{1,0:T(8,128)(2,1)}, u32[]{:S(2)}, u32[]{:S(2)}) collective-permute-start(bf16[2048,896]{1,0:T(8,128)(2,1)} %bitcast.18.rows_ref), channel_id=1, source_target_pairs={{0,1},{1,0},{2,3},{3,2},{4,5},{5,4},{6,7},{7,6},{8,9},{9,8},{10,11... | collective-permute-start | bytes 11010056 | tf_op jit(solution)/shard_map/ppermute | solution.py:28
  53.4 6.9 %slice-start = ((s8[7340032]{0:T(1024)(128)(4,1)}), s8[4194304]{0:T(1024)(128)(4,1)S(1)}, s32[]{:S(2)}) async-start(s8[7340032]{0:T(1024)(128)(4,1)} %bitcast.27), calls=%async_computation.1 | async-start | bytes 8388608
  56.6 3.7 %collective-permute-start.1 = (bf16[256,896]{1,0:T(8,128)(2,1)S(1)}, bf16[256,896]{1,0:T(8,128)(2,1)S(1)}, u32[]{:S(2)}, u32[]{:S(2)}) collective-permute-start(bf16[256,896]{1,0:T(8,128)(2,1)S(1)} %get-tuple-element.34.refs_0_), channel_id=1, source_target_pairs={{0,1},{1,0},{2,3},{3,2},{4,5},{5,4},{6,7},{7,6},{8,9},{9,8},{10,11... | collective-permute-start | bytes 1376264 | tf_op jit(solution)/shard_map/ppermute | solution.py:28
  57.2 3.2 %slice-start.1 = ((s8[7340032]{0:T(1024)(128)(4,1)}), s8[3145728]{0:T(1024)(128)(4,1)S(1)}, s32[]{:S(2)}) async-start(s8[7340032]{0:T(1024)(128)(4,1)} %bitcast.27), calls=%async_computation.2 | async-start | bytes 6291456
  63.2 17.3 %collective-permute-start.3 = (bf16[256,1280]{1,0:T(8,128)(2,1)S(1)}, bf16[256,1280]{1,0:T(8,128)(2,1)S(1)}, u32[]{:S(2)}, u32[]{:S(2)}) collective-permute-start(bf16[256,1280]{1,0:T(8,128)(2,1)S(1)} %get-tuple-element.38.refs_5_), channel_id=1, source_target_pairs={{0,4},{1,5},{2,6},{3,7},{4,8},{5,9},{6,10},{7,11},{8,12},{9,13},{1... | collective-permute-start | bytes 1966088 | tf_op jit(solution)/shard_map/ppermute | solution.py:28
  65.7 14.8 %collective-permute-start.4 = (bf16[256,1024]{1,0:T(8,128)(2,1)S(1)}, bf16[256,1024]{1,0:T(8,128)(2,1)S(1)}, u32[]{:S(2)}, u32[]{:S(2)}) collective-permute-start(bf16[256,1024]{1,0:T(8,128)(2,1)S(1)} %get-tuple-element.43), channel_id=1, source_target_pairs={{0,12},{1,13},{2,14},{3,15},{4,0},{5,1},{6,2},{7,3},{8,4},{9,5},{1... | collective-permute-start | bytes 1572872 | tf_op jit(solution)/shard_map/ppermute | solution.py:28
  67.9 13.7 %collective-permute-start.5 = (bf16[128,1792]{1,0:T(8,128)(2,1)S(1)}, bf16[128,1792]{1,0:T(8,128)(2,1)S(1)}, u32[]{:S(2)}, u32[]{:S(2)}) collective-permute-start(bf16[128,1792]{1,0:T(8,128)(2,1)S(1)} %get-tuple-element.39.refs_2_), channel_id=1, source_target_pairs={{0,2},{1,3},{2,0},{3,1},{4,6},{5,7},{6,4},{7,5},{8,10},{9,11},{10,... | collective-permute-start | bytes 1376264 | tf_op jit(solution)/shard_map/ppermute | solution.py:28
  75.6 27.4 %collective-permute-start.8 = (bf16[256,1792]{1,0:T(8,128)(2,1)S(1)}, bf16[256,1792]{1,0:T(8,128)(2,1)S(1)}, u32[]{:S(2)}, u32[]{:S(2)}) collective-permute-start(bf16[256,1792]{1,0:T(8,128)(2,1)S(1)} %shard_map.75.refs_5_), channel_id=1, source_target_pairs={{0,2},{1,3},{2,0},{3,1},{4,6},{5,7},{6,4},{7,5},{8,10},{9,11},{10,... | collective-permute-start | bytes 2752520 | tf_op jit(solution)/shard_map/ppermute | solution.py:28
  81.7 22.0 %collective-permute-start.10 = (bf16[128,3328]{1,0:T(8,128)(2,1)S(1)}, bf16[128,3328]{1,0:T(8,128)(2,1)S(1)}, u32[]{:S(2)}, u32[]{:S(2)}) collective-permute-start(bf16[128,3328]{1,0:T(8,128)(2,1)S(1)} %get-tuple-element.60), channel_id=1, source_target_pairs={{0,4},{1,5},{2,6},{3,7},{4,8},{5,9},{6,10},{7,11},{8,12},{9,13},{1... | collective-permute-start | bytes 2555912 | tf_op jit(solution)/shard_map/ppermute | solution.py:28
  85.1 18.7 %collective-permute-start.9 = (bf16[128,3072]{1,0:T(8,128)(2,1)S(1)}, bf16[128,3072]{1,0:T(8,128)(2,1)S(1)}, u32[]{:S(2)}, u32[]{:S(2)}) collective-permute-start(bf16[128,3072]{1,0:T(8,128)(2,1)S(1)} %get-tuple-element.47.refs_2_), channel_id=1, source_target_pairs={{0,12},{1,13},{2,14},{3,15},{4,0},{5,1},{6,2},{7,3},{8,4},{9,5},{1... | collective-permute-start | bytes 2359304 | tf_op jit(solution)/shard_map/ppermute | solution.py:28
  94.8 8.1 %copy-start.1 = (bf16[4096]{0:T(1024)(128)(2,1)S(1)}, bf16[4096]{0:T(1024)(128)(2,1)}, u32[]{:S(2)}) copy-start(bf16[4096]{0:T(1024)(128)(2,1)} %param.9) | copy-start | bytes 24580
  99.6 17.1 %collective-permute-start.6 = (bf16[128,2304]{1,0:T(8,128)(2,1)S(1)}, bf16[128,2304]{1,0:T(8,128)(2,1)S(1)}, u32[]{:S(2)}, u32[]{:S(2)}) collective-permute-start(bf16[128,2304]{1,0:T(8,128)(2,1)S(1)} %get-tuple-element.55.refs_3_), channel_id=1, source_target_pairs={{0,4},{1,5},{2,6},{3,7},{4,8},{5,9},{6,10},{7,11},{8,12},{9,13},{1... | collective-permute-start | bytes 1769480 | tf_op jit(solution)/shard_map/ppermute | solution.py:28
  102.9 17.5 %collective-permute-start.7 = (bf16[128,2304]{1,0:T(8,128)(2,1)S(1)}, bf16[128,2304]{1,0:T(8,128)(2,1)S(1)}, u32[]{:S(2)}, u32[]{:S(2)}) collective-permute-start(bf16[128,2304]{1,0:T(8,128)(2,1)S(1)} %get-tuple-element.56), channel_id=1, source_target_pairs={{0,12},{1,13},{2,14},{3,15},{4,0},{5,1},{6,2},{7,3},{8,4},{9,5},{1... | collective-permute-start | bytes 1769480 | tf_op jit(solution)/shard_map/ppermute | solution.py:28
  104.0 16.4 %copy-start = (bf16[128,4096]{1,0:T(8,128)(2,1)S(1)}, bf16[128,4096]{1,0:T(8,128)(2,1)}, u32[]{:S(2)}) copy-start(bf16[128,4096]{1,0:T(8,128)(2,1)} %refs_4_.1) | copy-start | bytes 3145732
  104.0 22.7 %collective-permute-start.11 = (bf16[128,4096]{1,0:T(8,128)(2,1)S(1)}, bf16[128,4096]{1,0:T(8,128)(2,1)S(1)}, u32[]{:S(2)}, u32[]{:S(2)}) collective-permute-start(bf16[128,4096]{1,0:T(8,128)(2,1)S(1)} %shard_map.85.refs_2_), channel_id=1, source_target_pairs={{0,2},{1,3},{2,0},{3,1},{4,6},{5,7},{6,4},{7,5},{8,10},{9,11},{10,... | collective-permute-start | bytes 3145736 | tf_op jit(solution)/shard_map/ppermute | solution.py:28
  105.0 21.7 %collective-permute-start.12 = (bf16[128,1792]{1,0:T(8,128)(2,1)S(1)}, bf16[128,1792]{1,0:T(8,128)(2,1)S(1)}, u32[]{:S(2)}, u32[]{:S(2)}) collective-permute-start(bf16[128,1792]{1,0:T(8,128)(2,1)S(1)} %shard_map.86.refs_2_), channel_id=1, source_target_pairs={{0,4},{1,5},{2,6},{3,7},{4,8},{5,9},{6,10},{7,11},{8,12},{9,13},{1... | collective-permute-start | bytes 1376264 | tf_op jit(solution)/shard_map/ppermute | solution.py:28
  107.7 18.9 %collective-permute-start.13 = (bf16[128,1792]{1,0:T(8,128)(2,1)S(1)}, bf16[128,1792]{1,0:T(8,128)(2,1)S(1)}, u32[]{:S(2)}, u32[]{:S(2)}) collective-permute-start(bf16[128,1792]{1,0:T(8,128)(2,1)S(1)} %shard_map.87.refs_5_), channel_id=1, source_target_pairs={{0,12},{1,13},{2,14},{3,15},{4,0},{5,1},{6,2},{7,3},{8,4},{9,5},{1... | collective-permute-start | bytes 1376264 | tf_op jit(solution)/shard_map/ppermute | solution.py:28
